TPU v7x, 512 devices: a whole 4x8x8 slice. The times are simulated.
512 devices in a mesh: clus: 128 (over y, x_hi, z), rows: 4 (over x_lo, core).
Axes of the slice: x: 4 (x_hi: 2, x_lo: 2; x = x_hi * 2 + x_lo), y: 8, z: 8, core: 2. Of those that a mesh axis runs over, the one named last changes fastest.
Arguments:
- right_sides: bfloat16 [256, 1024, 512], P('clus', 'rows'), may hold values from -6 to 6
- leaf_blocks: bfloat16 [256, 1024, 1024], P('clus', 'rows'), may hold values from -0.1875 to 0.1875
- basis_left: bfloat16 [8, 256, 1024, 128], P(None, 'clus', 'rows'), may hold values from -0.1875 to 0.1875
- basis_right: bfloat16 [8, 256, 1024, 128], P(None, 'clus', 'rows')
- block_ranks: int32 [510], replicated, may hold values from 32 to 128, as said below
Outputs:
- product: bfloat16 [256, 1024, 512], P('clus', 'rows')
Inputs may be any that keep to these rules, and one draw needn't show every extreme that they name: `block_ranks`: every block's rank lies between 32 and 128; the top level's first block has rank 128.
All inputs are finite; a program needn't handle non-finite values.
Results may differ from a plain program's by a relative error of at most 0.0036.
Values may be sent and summed in bfloat16 or wider, within the bound.
No kernel may reach another device: no remote copies, remote signals or barrier semaphores. Data moves between devices by JAX's collectives and lax.ppermute only.
A program may use at most 64 MiB of HBM per device.

v0:
```python
import jax
import jax.numpy as jnp
from jax import lax
from jax.sharding import PartitionSpec as P


def partner(block, axis, stride):
    count = lax.axis_size(axis)
    route = []
    for low in range(count):
        high = low | 1 << stride
        if high != low and high < count:
            route += [(low, high), (high, low)]
    return lax.ppermute(block, axis, route)


def rank_keep(heap_index, block_ranks, rank_max):
    table = jnp.arange(block_ranks.shape[0], dtype=jnp.int32)
    onehot = (heap_index[:, None] == table[None, :]).astype(jnp.int32)
    chosen = jnp.sum(onehot * block_ranks[None, :], axis=1)
    columns = jnp.arange(rank_max, dtype=jnp.int32)
    return (columns[None, :] < chosen[:, None]).astype(jnp.bfloat16)


def local(right_sides, leaf_blocks, basis_left, basis_right, block_ranks):
    levels = basis_left.shape[0]
    upper_count = levels - 1
    local_leaves, local_rows, rhs_width = right_sides.shape
    rank_max = basis_left.shape[3]
    dense = jnp.einsum(
        "lrc,lch->lrh",
        leaf_blocks,
        lax.all_gather(right_sides, "rows", axis=1, tiled=True),
        preferred_element_type=jnp.float32,
    )
    upper = jnp.einsum(
        "klrj,lrh->kjh", basis_right[:upper_count], right_sides, preferred_element_type=jnp.float32
    )
    finest = jnp.einsum(
        "lrj,lrh->ljh", basis_right[upper_count], right_sides, preferred_element_type=jnp.float32
    )
    upper, finest = lax.psum((upper, finest), "rows")
    position = lax.axis_index("clus")
    received = []
    for level in range(upper_count):
        distance = upper_count - 1 - level
        partial_value = upper[level]
        for bit_index in range(distance):
            partial_value = partial_value + partner(partial_value, "clus", bit_index)
        received.append(
            partner(partial_value.astype(jnp.bfloat16), "clus", distance).astype(
                partial_value.dtype
            )
        )
    sibling = jnp.stack(received)
    sibling = sibling.astype(jnp.bfloat16)
    finest_sibling = finest[::-1].astype(jnp.bfloat16)
    level_ids = jnp.arange(upper_count, dtype=jnp.int32)
    cluster = jnp.right_shift(position, upper_count - 1 - level_ids)
    heap_upper = jnp.left_shift(1, level_ids + 1) - 2 + cluster
    keep_upper = rank_keep(heap_upper, block_ranks, rank_max)
    heap_leaf = 2**levels - 2 + local_leaves * position + jnp.arange(local_leaves, dtype=jnp.int32)
    keep_leaf = rank_keep(heap_leaf, block_ranks, rank_max)
    coefficient = sibling * keep_upper[:, :, None]
    finest_coef = finest_sibling * keep_leaf[:, :, None]
    accumulated = dense + jnp.einsum(
        "klrj,kjh->lrh", basis_left[:upper_count], coefficient, preferred_element_type=jnp.float32
    )
    accumulated = accumulated + jnp.einsum(
        "lrj,ljh->lrh", basis_left[upper_count], finest_coef, preferred_element_type=jnp.float32
    )
    return accumulated.astype(jnp.bfloat16)


def solution(mesh):
    in_specs = (
        P("clus", "rows", None),
        P("clus", "rows", None),
        P(None, "clus", "rows", None),
        P(None, "clus", "rows", None),
        P(),
    )
    out_specs = P("clus", "rows", None)
    return jax.shard_map(local, mesh=mesh, in_specs=in_specs, out_specs=out_specs, check_vma=False)
```

profile of v0, /device:TPU:1, one launch (start us, length us, event | category | flops | bytes accessed | tf_op | source)
XLA Modules:
  0.0 311.7 jit_solution(16521958805033692381)
XLA Ops:
  6.5 3.3 %convolution_bitcast_fusion = f32[7,128,512]{2,1,0:T(8,128)} fusion(bf16[8,2,256,128]{3,2,1,0:T(8,128)(2,1)} %param.8, bf16[2,256,512]{2,1,0:T(8,128)(2,1)} %param.5), kind=kOutput, calls=%fused_computation | convolution fusion | flops 469762048 | bytes 3407872 | tf_op jit(solution)/shard_map/klrj,lrh->kjh/dot_general | solution.py:36
  10.0 70.1 %all-reduce.3.cloned.1.call-done = f32[7,128,512]{2,1,0:T(8,128)} async-done(((f32[7,128,512]{2,1,0:T(8,128)}), f32[7,128,512]{2,1,0:T(8,128)}) %all-reduce.3.cloned.1.call-update) | async-done | bytes 1835024 | tf_op jit(solution)/shard_map/psum | solution.py:42
  80.0 2.5 slice_bitcast_fusion
  82.5 3.4 %collective-permute-start = (f32[128,512]{1,0:T(8,128)S(1)}, f32[128,512]{1,0:T(8,128)}, u32[]{:S(2)}, u32[]{:S(2)}) collective-permute-start(f32[128,512]{1,0:T(8,128)S(1)} %get-tuple-element.16), channel_id=1, source_target_pairs={{0,4},{4,0},{8,12},{12,8},{16,20},{20,16},{24,28},{28,24},{32,36},... | collective-permute-start | bytes 786440 | tf_op jit(solution)/shard_map/ppermute | solution.py:14
  85.9 2.0 collective-permute-start.13
  87.9 3.3 %collective-permute-start.18 = (f32[128,512]{1,0:T(8,128)}, f32[128,512]{1,0:T(8,128)}, u32[]{:S(2)}, u32[]{:S(2)}) collective-permute-start(f32[128,512]{1,0:T(8,128)} %get-tuple-element.13), channel_id=1, source_target_pairs={{0,4},{4,0},{8,12},{12,8},{16,20},{20,16},{24,28},{28,24},{32,36},... | collective-permute-start | bytes 786440 | tf_op jit(solution)/shard_map/ppermute | solution.py:14
  91.2 2.0 collective-permute-start.22
  93.2 3.3 %collective-permute-start.25 = (f32[128,512]{1,0:T(8,128)}, f32[128,512]{1,0:T(8,128)}, u32[]{:S(2)}, u32[]{:S(2)}) collective-permute-start(f32[128,512]{1,0:T(8,128)} %get-tuple-element.11), channel_id=1, source_target_pairs={{0,4},{4,0},{8,12},{12,8},{16,20},{20,16},{24,28},{28,24},{32,36},... | collective-permute-start | bytes 786440 | tf_op jit(solution)/shard_map/ppermute | solution.py:14
  96.5 2.0 collective-permute-start.7
  98.6 2.1 fusion.12
  100.6 1.1 rev.3
  101.7 1.7 collective-permute-done.18
  103.4 5.6 %collective-permute-done.22 = f32[128,512]{1,0:T(8,128)} collective-permute-done((f32[128,512]{1,0:T(8,128)}, f32[128,512]{1,0:T(8,128)}, u32[]{:S(2)}, u32[]{:S(2)}) %collective-permute-start.22) | collective-permute-done | bytes 262176 | tf_op jit(solution)/shard_map/ppermute | solution.py:14
  109.0 5.6 %collective-permute-done.25 = f32[128,512]{1,0:T(8,128)} collective-permute-done((f32[128,512]{1,0:T(8,128)}, f32[128,512]{1,0:T(8,128)}, u32[]{:S(2)}, u32[]{:S(2)}) %collective-permute-start.25) | collective-permute-done | bytes 262176 | tf_op jit(solution)/shard_map/ppermute | solution.py:14
  114.6 5.6 %collective-permute-done.7 = f32[128,512]{1,0:T(8,128)} collective-permute-done((f32[128,512]{1,0:T(8,128)}, f32[128,512]{1,0:T(8,128)}, u32[]{:S(2)}, u32[]{:S(2)}) %collective-permute-start.7) | collective-permute-done | bytes 262176 | tf_op jit(solution)/shard_map/ppermute | solution.py:14
  120.3 2.5 add_convert_fusion
  122.7 4.3 %collective-permute-start.1 = (f32[128,512]{1,0:T(8,128)}, f32[128,512]{1,0:T(8,128)}, u32[]{:S(2)}, u32[]{:S(2)}) collective-permute-start(f32[128,512]{1,0:T(8,128)} %get-tuple-element.10), channel_id=1, source_target_pairs={{0,8},{8,0},{4,12},{12,4},{16,24},{24,16},{20,28},{28,20},{32,40},... | collective-permute-start | bytes 786440 | tf_op jit(solution)/shard_map/ppermute | solution.py:14
  127.1 19.4 %all-reduce.4 = bf16[2,128,512]{1,2,0:T(8,128)(2,1)} all-reduce(f32[2,128,512]{1,2,0:T(8,128)S(1)} %rev.3), channel_id=1, replica_groups=mesh['clus'=128,'rows'=4] {'rows'}, use_global_device_ids=true, to_apply=%region_2.0 | all-reduce | flops 131072 | bytes 786432 | tf_op jit(solution)/shard_map/psum | solution.py:42
  146.7 3.9 %collective-permute-start.14 = (f32[128,512]{1,0:T(8,128)}, f32[128,512]{1,0:T(8,128)}, u32[]{:S(2)}, u32[]{:S(2)}) collective-permute-start(f32[128,512]{1,0:T(8,128)} %get-tuple-element.8), channel_id=1, source_target_pairs={{0,8},{8,0},{4,12},{12,4},{16,24},{24,16},{20,28},{28,20},{32,40},... | collective-permute-start | bytes 786440 | tf_op jit(solution)/shard_map/ppermute | solution.py:14
  150.6 2.3 collective-permute-start.8
  153.9 7.4 %collective-permute-start.2 = (f32[128,512]{1,0:T(8,128)S(1)}, f32[128,512]{1,0:T(8,128)}, u32[]{:S(2)}, u32[]{:S(2)}) collective-permute-start(f32[128,512]{1,0:T(8,128)S(1)} %add.103), channel_id=1, source_target_pairs={{0,16},{16,0},{4,20},{20,4},{8,24},{24,8},{12,28},{28,12},{32,48},... | collective-permute-start | bytes 786440 | tf_op jit(solution)/shard_map/ppermute | solution.py:14
  161.4 2.5 collective-permute-start.19
  163.9 26.5 %collective-permute-done.8 = f32[128,512]{1,0:T(8,128)} collective-permute-done((f32[128,512]{1,0:T(8,128)}, f32[128,512]{1,0:T(8,128)}, u32[]{:S(2)}, u32[]{:S(2)}) %collective-permute-start.8) | collective-permute-done | bytes 262176 | tf_op jit(solution)/shard_map/ppermute | solution.py:14
  191.4 8.5 %collective-permute-start.9 = (f32[128,512]{1,0:T(8,128)S(1)}, f32[128,512]{1,0:T(8,128)S(1)}, u32[]{:S(2)}, u32[]{:S(2)}) collective-permute-start(f32[128,512]{1,0:T(8,128)S(1)} %add.109), channel_id=1, source_target_pairs={{0,16},{16,0},{4,20},{20,4},{8,24},{24,8},{12,28},{28,12},{32,48},... | collective-permute-start | bytes 786440 | tf_op jit(solution)/shard_map/ppermute | solution.py:14
  200.1 1.9 collective-permute-start.23
  203.1 1.9 collective-permute-start.15
  206.1 5.0 %collective-permute-start.3 = (f32[128,512]{1,0:T(8,128)S(1)}, f32[128,512]{1,0:T(8,128)S(1)}, u32[]{:S(2)}, u32[]{:S(2)}) collective-permute-start(f32[128,512]{1,0:T(8,128)S(1)} %add.104), channel_id=1, source_target_pairs={{0,32},{32,0},{4,36},{36,4},{8,40},{40,8},{12,44},{44,12},{16,48},... | collective-permute-start | bytes 786440 | tf_op jit(solution)/shard_map/ppermute | solution.py:14
  211.2 7.3 %collective-permute-start.20 = (f32[128,512]{1,0:T(8,128)S(1)}, f32[128,512]{1,0:T(8,128)S(1)}, u32[]{:S(2)}, u32[]{:S(2)}) collective-permute-start(f32[128,512]{1,0:T(8,128)S(1)} %add.118), channel_id=1, source_target_pairs={{0,16},{16,0},{4,20},{20,4},{8,24},{24,8},{12,28},{28,12},{32,48},... | collective-permute-start | bytes 786440 | tf_op jit(solution)/shard_map/ppermute | solution.py:14
  218.5 1.9 collective-permute-start.10
  220.5 12.1 %collective-permute-done.15 = f32[128,512]{1,0:T(8,128)S(1)} collective-permute-done((f32[128,512]{1,0:T(8,128)S(1)}, f32[128,512]{1,0:T(8,128)S(1)}, u32[]{:S(2)}, u32[]{:S(2)}) %collective-permute-start.15) | collective-permute-done | bytes 262176 | tf_op jit(solution)/shard_map/ppermute | solution.py:14
  232.6 1.9 collective-permute-start.27
  234.5 4.8 %collective-permute-start.16 = (f32[128,512]{1,0:T(8,128)S(1)}, f32[128,512]{1,0:T(8,128)S(1)}, u32[]{:S(2)}, u32[]{:S(2)}) collective-permute-start(f32[128,512]{1,0:T(8,128)S(1)} %add.115), channel_id=1, source_target_pairs={{0,32},{32,0},{4,36},{36,4},{8,40},{40,8},{12,44},{44,12},{16,48},... | collective-permute-start | bytes 786440 | tf_op jit(solution)/shard_map/ppermute | solution.py:14
  239.4 6.8 %collective-permute-done.23 = f32[128,512]{1,0:T(8,128)S(1)} collective-permute-done((f32[128,512]{1,0:T(8,128)}, f32[128,512]{1,0:T(8,128)S(1)}, u32[]{:S(2)}, u32[]{:S(2)}) %collective-permute-start.23) | collective-permute-done | bytes 262176 | tf_op jit(solution)/shard_map/ppermute | solution.py:14
  246.3 3.1 collective-permute-start.4
  249.4 1.9 collective-permute-start.26
  251.4 2.2 collective-permute-start.11
  253.6 1.8 collective-permute-done.4
  255.5 4.2 %collective-permute-start.24 = (bf16[128,512]{1,0:T(8,128)(2,1)S(1)}, bf16[128,512]{1,0:T(8,128)(2,1)S(1)}, u32[]{:S(2)}, u32[]{:S(2)}) collective-permute-start(bf16[128,512]{1,0:T(8,128)(2,1)S(1)} %add_convert_fusion.1), channel_id=1, source_target_pairs={{0,16},{16,0},{4,20},{20,4},{8,24},{24,8},{12,28},{28,12},{32,48},... | collective-permute-start | bytes 393224 | tf_op jit(solution)/shard_map/ppermute | solution.py:14
  259.8 4.0 %collective-permute-start.5 = (f32[128,512]{1,0:T(8,128)S(1)}, f32[128,512]{1,0:T(8,128)S(1)}, u32[]{:S(2)}, u32[]{:S(2)}) collective-permute-start(f32[128,512]{1,0:T(8,128)S(1)} %add.106), channel_id=1, source_target_pairs={{0,128},{128,0},{4,132},{132,4},{8,136},{136,8},{12,140},{140,12},... | collective-permute-start | bytes 786440 | tf_op jit(solution)/shard_map/ppermute | solution.py:14
  263.9 4.9 %collective-permute-start.21 = (bf16[128,512]{1,0:T(8,128)(2,1)S(1)}, bf16[128,512]{1,0:T(8,128)(2,1)S(1)}, u32[]{:S(2)}, u32[]{:S(2)}) collective-permute-start(bf16[128,512]{1,0:T(8,128)(2,1)S(1)} %add_convert_fusion.2), channel_id=1, source_target_pairs={{0,32},{32,0},{4,36},{36,4},{8,40},{40,8},{12,44},{44,12},{16,48},... | collective-permute-start | bytes 393224 | tf_op jit(solution)/shard_map/ppermute | solution.py:14
  268.8 6.6 %collective-permute-done.5 = f32[128,512]{1,0:T(8,128)S(1)} collective-permute-done((f32[128,512]{1,0:T(8,128)S(1)}, f32[128,512]{1,0:T(8,128)S(1)}, u32[]{:S(2)}, u32[]{:S(2)}) %collective-permute-start.5) | collective-permute-done | bytes 262176 | tf_op jit(solution)/shard_map/ppermute | solution.py:14
  275.4 8.1 %collective-permute-start.6 = (bf16[128,512]{1,0:T(8,128)(2,1)S(1)}, bf16[128,512]{1,0:T(8,128)(2,1)S(1)}, u32[]{:S(2)}, u32[]{:S(2)}) collective-permute-start(bf16[128,512]{1,0:T(8,128)(2,1)S(1)} %add_convert_fusion.5), channel_id=1, source_target_pairs={{0,256},{256,0},{4,260},{260,4},{8,264},{264,8},{12,268},{268,12},... | collective-permute-start | bytes 393224 | tf_op jit(solution)/shard_map/ppermute | solution.py:14
  283.5 2.3 fusion.24
  286.4 1.9 collective-permute-start.12
  288.3 4.7 %collective-permute-done.12 = bf16[128,512]{1,0:T(8,128)(2,1)S(1)} collective-permute-done((bf16[128,512]{1,0:T(8,128)(2,1)S(1)}, bf16[128,512]{1,0:T(8,128)(2,1)S(1)}, u32[]{:S(2)}, u32[]{:S(2)}) %collective-permute-start.12) | collective-permute-done | bytes 131104 | tf_op jit(solution)/shard_map/ppermute | solution.py:14
  293.0 7.3 %collective-permute-start.17 = (bf16[128,512]{1,0:T(8,128)(2,1)S(1)}, bf16[128,512]{1,0:T(8,128)(2,1)S(1)}, u32[]{:S(2)}, u32[]{:S(2)}) collective-permute-start(bf16[128,512]{1,0:T(8,128)(2,1)S(1)} %add_convert_fusion.3), channel_id=1, source_target_pairs={{0,64},{64,0},{4,68},{68,4},{8,72},{72,8},{12,76},{76,12},{16,80},... | collective-permute-start | bytes 393224 | tf_op jit(solution)/shard_map/ppermute | solution.py:14
  300.3 2.3 collective-permute-done.17
  303.8 1.1 fusion.2
  (68 shorter events, 6.8 us)
Async XLA Ops:
  6.5 277.0 %copy-start = (bf16[2,256,1024]{2,1,0:T(8,128)(2,1)S(1)}, bf16[2,256,1024]{2,1,0:T(8,128)(2,1)}, u32[]{:S(2)}) copy-start(bf16[2,256,1024]{2,1,0:T(8,128)(2,1)} %param.6) | copy-start | bytes 3145732
  6.5 73.5 %all-reduce.3.cloned.1.call-start = ((), (), s32[]{:S(2)}) async-start(), calls=%async_computation.1 | async-start | bytes 3670016 | tf_op jit(solution)/shard_map/psum | solution.py:42
  9.9 88.7 %copy-start.2 = (bf16[2,256,512]{2,1,0:T(8,128)(2,1)S(1)}, bf16[2,256,512]{2,1,0:T(8,128)(2,1)}, u32[]{:S(2)}) copy-start(bf16[2,256,512]{2,1,0:T(8,128)(2,1)} %param.5) | copy-start | bytes 1572868
  9.9 273.6 %all-gather.2.cloned.1.call-start = ((), (), s32[]{:S(2)}) async-start(), calls=%async_computation | async-start | bytes 2621440 | tf_op jit(solution)/shard_map/all_gather | solution.py:33
  82.5 37.8 %copy-start.1 = (f32[7,128,512]{2,1,0:T(8,128)S(1)}, f32[7,128,512]{2,1,0:T(8,128)}, u32[]{:S(2)}) copy-start(f32[7,128,512]{2,1,0:T(8,128)} %all-reduce.3.cloned.1.call-done) | copy-start | bytes 5505028
  82.5 14.0 %collective-permute-start = (f32[128,512]{1,0:T(8,128)S(1)}, f32[128,512]{1,0:T(8,128)}, u32[]{:S(2)}, u32[]{:S(2)}) collective-permute-start(f32[128,512]{1,0:T(8,128)S(1)} %get-tuple-element.16), channel_id=1, source_target_pairs={{0,4},{4,0},{8,12},{12,8},{16,20},{20,16},{24,28},{28,24},{32,36},... | collective-permute-start | bytes 786440 | tf_op jit(solution)/shard_map/ppermute | solution.py:14
  85.9 15.8 %collective-permute-start.13 = (f32[128,512]{1,0:T(8,128)}, f32[128,512]{1,0:T(8,128)}, u32[]{:S(2)}, u32[]{:S(2)}) collective-permute-start(f32[128,512]{1,0:T(8,128)} %get-tuple-element.14), channel_id=1, source_target_pairs={{0,4},{4,0},{8,12},{12,8},{16,20},{20,16},{24,28},{28,24},{32,36},... | collective-permute-start | bytes 786440 | tf_op jit(solution)/shard_map/ppermute | solution.py:14
  87.9 15.5 %collective-permute-start.18 = (f32[128,512]{1,0:T(8,128)}, f32[128,512]{1,0:T(8,128)}, u32[]{:S(2)}, u32[]{:S(2)}) collective-permute-start(f32[128,512]{1,0:T(8,128)} %get-tuple-element.13), channel_id=1, source_target_pairs={{0,4},{4,0},{8,12},{12,8},{16,20},{20,16},{24,28},{28,24},{32,36},... | collective-permute-start | bytes 786440 | tf_op jit(solution)/shard_map/ppermute | solution.py:14
  91.2 17.8 %collective-permute-start.22 = (f32[128,512]{1,0:T(8,128)}, f32[128,512]{1,0:T(8,128)}, u32[]{:S(2)}, u32[]{:S(2)}) collective-permute-start(f32[128,512]{1,0:T(8,128)} %get-tuple-element.12), channel_id=1, source_target_pairs={{0,4},{4,0},{8,12},{12,8},{16,20},{20,16},{24,28},{28,24},{32,36},... | collective-permute-start | bytes 786440 | tf_op jit(solution)/shard_map/ppermute | solution.py:14
  93.2 21.4 %collective-permute-start.25 = (f32[128,512]{1,0:T(8,128)}, f32[128,512]{1,0:T(8,128)}, u32[]{:S(2)}, u32[]{:S(2)}) collective-permute-start(f32[128,512]{1,0:T(8,128)} %get-tuple-element.11), channel_id=1, source_target_pairs={{0,4},{4,0},{8,12},{12,8},{16,20},{20,16},{24,28},{28,24},{32,36},... | collective-permute-start | bytes 786440 | tf_op jit(solution)/shard_map/ppermute | solution.py:14
  96.5 23.7 %collective-permute-start.7 = (f32[128,512]{1,0:T(8,128)}, f32[128,512]{1,0:T(8,128)}, u32[]{:S(2)}, u32[]{:S(2)}) collective-permute-start(f32[128,512]{1,0:T(8,128)} %get-tuple-element.15), channel_id=1, source_target_pairs={{0,4},{4,0},{8,12},{12,8},{16,20},{20,16},{24,28},{28,24},{32,36},... | collective-permute-start | bytes 786440 | tf_op jit(solution)/shard_map/ppermute | solution.py:14
  101.7 44.8 %copy-start.7 = (s32[510]{0:T(512)S(1)}, s32[510]{0:T(512)}, u32[]{:S(2)}) copy-start(s32[510]{0:T(512)} %param.9) | copy-start | bytes 6124
  122.7 30.2 %collective-permute-start.1 = (f32[128,512]{1,0:T(8,128)}, f32[128,512]{1,0:T(8,128)}, u32[]{:S(2)}, u32[]{:S(2)}) collective-permute-start(f32[128,512]{1,0:T(8,128)} %get-tuple-element.10), channel_id=1, source_target_pairs={{0,8},{8,0},{4,12},{12,4},{16,24},{24,16},{20,28},{28,20},{32,40},... | collective-permute-start | bytes 786440 | tf_op jit(solution)/shard_map/ppermute | solution.py:14
  146.5 64.7 %copy-start.4 = (f32[128,512]{1,0:T(8,128)S(1)}, f32[128,512]{1,0:T(8,128)}, u32[]{:S(2)}) copy-start(f32[128,512]{1,0:T(8,128)} %get-tuple-element.7) | copy-start | bytes 786436
  146.7 55.4 %collective-permute-start.14 = (f32[128,512]{1,0:T(8,128)}, f32[128,512]{1,0:T(8,128)}, u32[]{:S(2)}, u32[]{:S(2)}) collective-permute-start(f32[128,512]{1,0:T(8,128)} %get-tuple-element.8), channel_id=1, source_target_pairs={{0,8},{8,0},{4,12},{12,4},{16,24},{24,16},{20,28},{28,20},{32,40},... | collective-permute-start | bytes 786440 | tf_op jit(solution)/shard_map/ppermute | solution.py:14
  150.6 39.8 %collective-permute-start.8 = (f32[128,512]{1,0:T(8,128)}, f32[128,512]{1,0:T(8,128)}, u32[]{:S(2)}, u32[]{:S(2)}) collective-permute-start(f32[128,512]{1,0:T(8,128)} %get-tuple-element.9), channel_id=1, source_target_pairs={{0,8},{8,0},{4,12},{12,4},{16,24},{24,16},{20,28},{28,20},{32,40},... | collective-permute-start | bytes 786440 | tf_op jit(solution)/shard_map/ppermute | solution.py:14
  153.9 51.1 %collective-permute-start.2 = (f32[128,512]{1,0:T(8,128)S(1)}, f32[128,512]{1,0:T(8,128)}, u32[]{:S(2)}, u32[]{:S(2)}) collective-permute-start(f32[128,512]{1,0:T(8,128)S(1)} %add.103), channel_id=1, source_target_pairs={{0,16},{16,0},{4,20},{20,4},{8,24},{24,8},{12,28},{28,12},{32,48},... | collective-permute-start | bytes 786440 | tf_op jit(solution)/shard_map/ppermute | solution.py:14
  161.4 49.8 %collective-permute-start.19 = (f32[128,512]{1,0:T(8,128)}, f32[128,512]{1,0:T(8,128)S(1)}, u32[]{:S(2)}, u32[]{:S(2)}) collective-permute-start(f32[128,512]{1,0:T(8,128)} %get-tuple-element.7), channel_id=1, source_target_pairs={{0,8},{8,0},{4,12},{12,4},{16,24},{24,16},{20,28},{28,20},{32,40},... | collective-permute-start | bytes 786440 | tf_op jit(solution)/shard_map/ppermute | solution.py:14
  191.4 27.1 %collective-permute-start.9 = (f32[128,512]{1,0:T(8,128)S(1)}, f32[128,512]{1,0:T(8,128)S(1)}, u32[]{:S(2)}, u32[]{:S(2)}) collective-permute-start(f32[128,512]{1,0:T(8,128)S(1)} %add.109), channel_id=1, source_target_pairs={{0,16},{16,0},{4,20},{20,4},{8,24},{24,8},{12,28},{28,12},{32,48},... | collective-permute-start | bytes 786440 | tf_op jit(solution)/shard_map/ppermute | solution.py:14
  200.1 46.1 %collective-permute-start.23 = (f32[128,512]{1,0:T(8,128)}, f32[128,512]{1,0:T(8,128)S(1)}, u32[]{:S(2)}, u32[]{:S(2)}) collective-permute-start(f32[128,512]{1,0:T(8,128)} %get-tuple-element.6), channel_id=1, source_target_pairs={{0,8},{8,0},{4,12},{12,4},{16,24},{24,16},{20,28},{28,20},{32,40},... | collective-permute-start | bytes 786440 | tf_op jit(solution)/shard_map/ppermute | solution.py:14
  203.1 29.4 %collective-permute-start.15 = (f32[128,512]{1,0:T(8,128)S(1)}, f32[128,512]{1,0:T(8,128)S(1)}, u32[]{:S(2)}, u32[]{:S(2)}) collective-permute-start(f32[128,512]{1,0:T(8,128)S(1)} %add.114), channel_id=1, source_target_pairs={{0,16},{16,0},{4,20},{20,4},{8,24},{24,8},{12,28},{28,12},{32,48},... | collective-permute-start | bytes 786440 | tf_op jit(solution)/shard_map/ppermute | solution.py:14
  206.1 43.3 %copy-start.5 = (f32[128,512]{1,0:T(8,128)S(1)}, f32[128,512]{1,0:T(8,128)}, u32[]{:S(2)}) copy-start(f32[128,512]{1,0:T(8,128)} %get-tuple-element.6) | copy-start | bytes 786436
  206.1 28.4 %collective-permute-start.3 = (f32[128,512]{1,0:T(8,128)S(1)}, f32[128,512]{1,0:T(8,128)S(1)}, u32[]{:S(2)}, u32[]{:S(2)}) collective-permute-start(f32[128,512]{1,0:T(8,128)S(1)} %add.104), channel_id=1, source_target_pairs={{0,32},{32,0},{4,36},{36,4},{8,40},{40,8},{12,44},{44,12},{16,48},... | collective-permute-start | bytes 786440 | tf_op jit(solution)/shard_map/ppermute | solution.py:14
  211.2 40.2 %collective-permute-start.20 = (f32[128,512]{1,0:T(8,128)S(1)}, f32[128,512]{1,0:T(8,128)S(1)}, u32[]{:S(2)}, u32[]{:S(2)}) collective-permute-start(f32[128,512]{1,0:T(8,128)S(1)} %add.118), channel_id=1, source_target_pairs={{0,16},{16,0},{4,20},{20,4},{8,24},{24,8},{12,28},{28,12},{32,48},... | collective-permute-start | bytes 786440 | tf_op jit(solution)/shard_map/ppermute | solution.py:14
  218.5 30.9 %collective-permute-start.10 = (f32[128,512]{1,0:T(8,128)S(1)}, f32[128,512]{1,0:T(8,128)S(1)}, u32[]{:S(2)}, u32[]{:S(2)}) collective-permute-start(f32[128,512]{1,0:T(8,128)S(1)} %add.110), channel_id=1, source_target_pairs={{0,32},{32,0},{4,36},{36,4},{8,40},{40,8},{12,44},{44,12},{16,48},... | collective-permute-start | bytes 786440 | tf_op jit(solution)/shard_map/ppermute | solution.py:14
  232.6 70.2 %collective-permute-start.27 = (bf16[128,512]{1,0:T(8,128)(2,1)S(1)}, bf16[128,512]{1,0:T(8,128)(2,1)S(1)}, u32[]{:S(2)}, u32[]{:S(2)}) collective-permute-start(bf16[128,512]{1,0:T(8,128)(2,1)S(1)} %fusion.10), channel_id=1, source_target_pairs={{0,4},{4,0},{8,12},{12,8},{16,20},{20,16},{24,28},{28,24},{32,36},... | collective-permute-start | bytes 393224 | tf_op jit(solution)/shard_map/ppermute | solution.py:14
  234.5 25.2 %collective-permute-start.16 = (f32[128,512]{1,0:T(8,128)S(1)}, f32[128,512]{1,0:T(8,128)S(1)}, u32[]{:S(2)}, u32[]{:S(2)}) collective-permute-start(f32[128,512]{1,0:T(8,128)S(1)} %add.115), channel_id=1, source_target_pairs={{0,32},{32,0},{4,36},{36,4},{8,40},{40,8},{12,44},{44,12},{16,48},... | collective-permute-start | bytes 786440 | tf_op jit(solution)/shard_map/ppermute | solution.py:14
  246.3 9.2 %collective-permute-start.4 = (f32[128,512]{1,0:T(8,128)S(1)}, f32[128,512]{1,0:T(8,128)S(1)}, u32[]{:S(2)}, u32[]{:S(2)}) collective-permute-start(f32[128,512]{1,0:T(8,128)S(1)} %add.105), channel_id=1, source_target_pairs={{0,64},{64,0},{4,68},{68,4},{8,72},{72,8},{12,76},{76,12},{16,80},... | collective-permute-start | bytes 786440 | tf_op jit(solution)/shard_map/ppermute | solution.py:14
  249.4 53.3 %collective-permute-start.26 = (bf16[128,512]{1,0:T(8,128)(2,1)S(1)}, bf16[128,512]{1,0:T(8,128)(2,1)S(1)}, u32[]{:S(2)}, u32[]{:S(2)}) collective-permute-start(bf16[128,512]{1,0:T(8,128)(2,1)S(1)} %get-tuple-element.5), channel_id=1, source_target_pairs={{0,8},{8,0},{4,12},{12,4},{16,24},{24,16},{20,28},{28,20},{32,40},... | collective-permute-start | bytes 393224 | tf_op jit(solution)/shard_map/ppermute | solution.py:14
  251.4 12.4 %collective-permute-start.11 = (f32[128,512]{1,0:T(8,128)S(1)}, f32[128,512]{1,0:T(8,128)S(1)}, u32[]{:S(2)}, u32[]{:S(2)}) collective-permute-start(f32[128,512]{1,0:T(8,128)S(1)} %add.111), channel_id=1, source_target_pairs={{0,64},{64,0},{4,68},{68,4},{8,72},{72,8},{12,76},{76,12},{16,80},... | collective-permute-start | bytes 786440 | tf_op jit(solution)/shard_map/ppermute | solution.py:14
  255.5 47.2 %collective-permute-start.24 = (bf16[128,512]{1,0:T(8,128)(2,1)S(1)}, bf16[128,512]{1,0:T(8,128)(2,1)S(1)}, u32[]{:S(2)}, u32[]{:S(2)}) collective-permute-start(bf16[128,512]{1,0:T(8,128)(2,1)S(1)} %add_convert_fusion.1), channel_id=1, source_target_pairs={{0,16},{16,0},{4,20},{20,4},{8,24},{24,8},{12,28},{28,12},{32,48},... | collective-permute-start | bytes 393224 | tf_op jit(solution)/shard_map/ppermute | solution.py:14
  259.8 15.6 %collective-permute-start.5 = (f32[128,512]{1,0:T(8,128)S(1)}, f32[128,512]{1,0:T(8,128)S(1)}, u32[]{:S(2)}, u32[]{:S(2)}) collective-permute-start(f32[128,512]{1,0:T(8,128)S(1)} %add.106), channel_id=1, source_target_pairs={{0,128},{128,0},{4,132},{132,4},{8,136},{136,8},{12,140},{140,12},... | collective-permute-start | bytes 786440 | tf_op jit(solution)/shard_map/ppermute | solution.py:14
  263.9 38.8 %collective-permute-start.21 = (bf16[128,512]{1,0:T(8,128)(2,1)S(1)}, bf16[128,512]{1,0:T(8,128)(2,1)S(1)}, u32[]{:S(2)}, u32[]{:S(2)}) collective-permute-start(bf16[128,512]{1,0:T(8,128)(2,1)S(1)} %add_convert_fusion.2), channel_id=1, source_target_pairs={{0,32},{32,0},{4,36},{36,4},{8,40},{40,8},{12,44},{44,12},{16,48},... | collective-permute-start | bytes 393224 | tf_op jit(solution)/shard_map/ppermute | solution.py:14
  275.4 10.9 %collective-permute-start.6 = (bf16[128,512]{1,0:T(8,128)(2,1)S(1)}, bf16[128,512]{1,0:T(8,128)(2,1)S(1)}, u32[]{:S(2)}, u32[]{:S(2)}) collective-permute-start(bf16[128,512]{1,0:T(8,128)(2,1)S(1)} %add_convert_fusion.5), channel_id=1, source_target_pairs={{0,256},{256,0},{4,260},{260,4},{8,264},{264,8},{12,268},{268,12},... | collective-permute-start | bytes 393224 | tf_op jit(solution)/shard_map/ppermute | solution.py:14
  285.8 17.0 %copy-start.6 = (bf16[8,2,256,128]{3,2,1,0:T(8,128)(2,1)S(1)}, bf16[8,2,256,128]{3,2,1,0:T(8,128)(2,1)}, u32[]{:S(2)}) copy-start(bf16[8,2,256,128]{3,2,1,0:T(8,128)(2,1)} %param.7) | copy-start | bytes 3145732
  286.4 6.6 %collective-permute-start.12 = (bf16[128,512]{1,0:T(8,128)(2,1)S(1)}, bf16[128,512]{1,0:T(8,128)(2,1)S(1)}, u32[]{:S(2)}, u32[]{:S(2)}) collective-permute-start(bf16[128,512]{1,0:T(8,128)(2,1)S(1)} %add_convert_fusion.4), channel_id=1, source_target_pairs={{0,128},{128,0},{4,132},{132,4},{8,136},{136,8},{12,140},{140,12},... | collective-permute-start | bytes 393224 | tf_op jit(solution)/shard_map/ppermute | solution.py:14
  293.0 9.7 %collective-permute-start.17 = (bf16[128,512]{1,0:T(8,128)(2,1)S(1)}, bf16[128,512]{1,0:T(8,128)(2,1)S(1)}, u32[]{:S(2)}, u32[]{:S(2)}) collective-permute-start(bf16[128,512]{1,0:T(8,128)(2,1)S(1)} %add_convert_fusion.3), channel_id=1, source_target_pairs={{0,64},{64,0},{4,68},{68,4},{8,72},{72,8},{12,76},{76,12},{16,80},... | collective-permute-start | bytes 393224 | tf_op jit(solution)/shard_map/ppermute | solution.py:14
  302.8 1.0 copy-start.3
Sparse Core Ops, SparseCore 0:
  10.3 69.6 all-reduce.2
  98.7 40.8 all-gather.1
where the time goes:
time: 315 us; the launch traced here: 312 us
  waiting for transfers between devices  150 us (48%)
  starting transfers between devices  107 us (34%)
  blocking collectives  19.4 us (6%)
  between operations  14 us (4%)
  matrix products  9.57 us (3%)
  other arithmetic  7.59 us (2%)
  local copies, waits for them, and re-layouts  3.83 us (1%)
    ppermute x28, starting transfers between devices, partner(): return lax.ppermute(block, axis, route)  107 us
    ppermute x28, waiting for transfers between devices, partner(): return lax.ppermute(block, axis, route)  79.8 us
    psum x1, waiting for transfers between devices, local(): upper, finest = lax.psum((upper, finest), 'rows')  70.1 us
    psum x1, blocking collectives, local(): upper, finest = lax.psum((upper, finest), 'rows')  19.4 us
  transfers between devices with their start and end apart: 30, of which 13 were waited for; matrix products, arithmetic and copies ran while one was open for 4% of the time, Pallas kernels for 0%

commit v1 on v0

v1 whole, which is shorter than its diff:
```python
import functools

import jax
import jax.numpy as jnp
from jax import lax
from jax.experimental import pallas as pl
from jax.experimental.pallas import tpu as pltpu
from jax.sharding import Mesh, PartitionSpec as P

VMEM_BYTES = 48 * 1024 * 1024
F32 = jnp.float32
BF16 = jnp.bfloat16


def call(kernel, out_shape, in_specs, scratch=(), flops=0, moved=0):
    many = isinstance(out_shape, (list, tuple))
    whole = pl.BlockSpec(memory_space=pltpu.VMEM)
    return pl.pallas_call(
        kernel,
        out_shape=out_shape,
        in_specs=in_specs,
        out_specs=[whole] * len(out_shape) if many else whole,
        scratch_shapes=list(scratch),
        compiler_params=pltpu.CompilerParams(vmem_limit_bytes=VMEM_BYTES),
        cost_estimate=pl.CostEstimate(flops=flops, bytes_accessed=moved, transcendentals=0),
    )


SMEM = pl.BlockSpec(memory_space=pltpu.SMEM)
VMEM = pl.BlockSpec(memory_space=pltpu.VMEM)


def project_kernel(other, place, basis, sides, out):
    levels, leaves, rows, rank = basis.shape
    half = sides.shape[2] // 2
    core = place[1]
    column = pl.multiple_of((1 - core if other else core) * half, half)
    both = sides[:, :, pl.ds(column, half)]
    contract = (((0,), (0,)), ((), ()))
    for level in range(levels - 1):
        out[level] = lax.dot_general(
            basis[level].reshape(leaves * rows, rank),
            both.reshape(leaves * rows, half),
            contract,
            preferred_element_type=F32,
        )
    for leaf in range(leaves):
        out[levels - 1 + leaf] = lax.dot_general(
            basis[levels - 1, leaf], both[leaf], contract, preferred_element_type=F32
        )


def combine_kernel(mine, theirs, tiles, finest):
    upper = mine.shape[0] - finest.shape[0]
    slots, down, across = tiles.shape[:3]
    for level in range(upper):
        total = mine[level] + theirs[level]
        for col in range(across):
            part = total[:, col * 128 : (col + 1) * 128]
            tiles[level, :, col] = part.reshape(down, 8, 128).astype(BF16)
    for level in range(upper, slots):
        tiles[level] = jnp.zeros(tiles.shape[1:], BF16)
    finest[...] = mine[upper:] + theirs[upper:]


def tree_kernel(place, parts, out, total):
    count = total.shape[0]
    bits = count.bit_length() - 1
    depth = bits - 1 - place[3] // 32
    whole = parts[...].astype(F32)
    total[...] = whole[:, 0] + whole[:, 1]

    def swapped(bit):
        view = total[...].reshape(count >> (bit + 1), 2, 1 << bit, 8, 128)
        flipped = jnp.concatenate([view[:, 1:], view[:, :1]], axis=1)
        return flipped.reshape(count, 8, 128)

    for bit in range(bits):

        @pl.when(bit < depth)
        def _():
            total[...] = total[...] + swapped(bit)

        @pl.when(bit == depth)
        def _():
            total[...] = swapped(bit)

    rounded = total[...].astype(BF16)
    out[:, 0] = rounded
    out[:, 1] = rounded


def dense_kernel(place, blocks, own, by_core, by_chip, by_both, out):
    leaves, rows, _ = blocks.shape
    row = place[2]
    for leaf in range(leaves):
        total = None
        for step, sides in enumerate((own, by_core, by_chip, by_both)):
            column = pl.multiple_of(jnp.bitwise_xor(row, step) * rows, rows)
            term = jnp.dot(
                blocks[leaf, :, pl.ds(column, rows)], sides[leaf], preferred_element_type=F32
            )
            total = term if total is None else total + term
        out[leaf] = total


def update(place, ranks, tiles, finest, basis, dense, column, coef, store):
    levels, leaves, rows, rank = basis.shape
    upper = levels - 1
    half = finest.shape[2]
    across = half // 128
    position = place[0]

    def keep(shape, heap):
        return lax.broadcasted_iota(jnp.int32, shape, 0) < ranks[heap]

    for level in range(upper):
        heap = 2 ** (level + 1) - 2 + lax.shift_right_logical(position, upper - 1 - level)
        for col in range(across):
            part = tiles[level, :, col].astype(F32).reshape(rank, 128)
            part = jnp.where(keep(part.shape, heap), part, 0.0)
            coef[level * rank : (level + 1) * rank, col * 128 : (col + 1) * 128] = part.astype(BF16)
    for leaf in range(leaves):
        heap = 2**levels - 2 + leaves * position + leaf
        part = finest[leaves - 1 - leaf].astype(F32)
        part = jnp.where(keep(part.shape, heap), part, 0.0)
        coef[upper * rank : levels * rank, :] = part.astype(BF16)
        left = jnp.concatenate([basis[level, leaf] for level in range(levels)], axis=1)
        term = jnp.dot(left, coef[...], preferred_element_type=F32)
        store(leaf, (dense[leaf, :, pl.ds(column, half)] + term).astype(BF16))


def own_kernel(place, ranks, tiles, finest, basis, dense, out, coef):
    half = out.shape[2]
    column = pl.multiple_of(place[1] * half, half)

    def store(leaf, value):
        out[leaf] = value

    update(place, ranks, tiles, finest, basis, dense, column, coef, store)


def last_kernel(place, ranks, tiles, finest, basis, dense, ready, out, coef):
    half = ready.shape[2]
    mine = pl.multiple_of(place[1] * half, half)
    column = pl.multiple_of((1 - place[1]) * half, half)
    out[:, :, pl.ds(mine, half)] = ready[...]

    def store(leaf, value):
        out[leaf, :, pl.ds(column, half)] = value

    update(place, ranks, tiles, finest, basis, dense, column, coef, store)


def swap(block, axis):
    return lax.ppermute(block, axis, [(0, 1), (1, 0)])


def local(right_sides, leaf_blocks, basis_left, basis_right, block_ranks):
    leaves, rows, width = right_sides.shape
    levels, _, _, rank = basis_left.shape
    half = width // 2
    clusters = lax.axis_size("clus")
    owners = 2 * clusters
    position = lax.axis_index("clus")
    chip = lax.axis_index("chip")
    core = lax.axis_index("core")
    place = jnp.stack([position, core, 2 * chip + core, 2 * position + chip]).astype(jnp.int32)
    shape = jax.ShapeDtypeStruct
    slots = levels - 1 + leaves
    flops = 2 * levels * leaves * rows * rank * half

    def project(other):
        return call(
            functools.partial(project_kernel, other),
            shape((slots, rank, half), F32),
            [SMEM, VMEM, VMEM],
            flops=flops,
            moved=2 * (basis_right.size + right_sides.size) + 4 * slots * rank * half,
        )(place, basis_right, right_sides)

    sent = project(True)
    theirs = swap(sent, "core")
    mine = project(False)
    tiles, finest = call(
        combine_kernel,
        [shape((levels, rank // 8, half // 128, 8, 128), BF16), shape((leaves, rank, half), F32)],
        [VMEM, VMEM],
        moved=10 * slots * rank * half,
    )(mine, theirs)
    parts = lax.all_to_all(
        tiles.reshape(owners, 8, 128), ("clus", "chip"), split_axis=0, concat_axis=0, tiled=True
    )
    by_chip = swap(right_sides, "chip")
    by_core = swap(right_sides, "core")
    by_both = swap(by_chip, "core")
    finest = (finest + swap(finest, "chip")).astype(BF16)
    finest_other = swap(finest, "core")
    dense = call(
        dense_kernel,
        shape((leaves, rows, width), F32),
        [SMEM] + [VMEM] * 5,
        flops=2 * leaves * rows * leaf_blocks.shape[2] * width,
        moved=2 * leaf_blocks.size + 8 * right_sides.size + 4 * right_sides.size,
    )(place, leaf_blocks, right_sides, by_core, by_chip, by_both)
    coefs = call(
        tree_kernel,
        shape((clusters, 2, 8, 128), BF16),
        [SMEM, VMEM],
        scratch=[pltpu.VMEM((clusters, 8, 128), F32)],
        moved=4 * owners * 1024,
    )(place, parts.reshape(clusters, 2, 8, 128))
    coefs = lax.all_to_all(
        coefs.reshape(owners, 8, 128), ("clus", "chip"), split_axis=0, concat_axis=0, tiled=True
    ).reshape(tiles.shape)
    coefs_other = swap(coefs, "core")
    scratch = [pltpu.VMEM((levels * rank, half), BF16)]
    moved = 2 * (basis_left.size + coefs.size) + 4 * right_sides.size
    ready = call(
        own_kernel,
        shape((leaves, rows, half), BF16),
        [SMEM, SMEM] + [VMEM] * 4,
        scratch=scratch,
        flops=flops,
        moved=moved,
    )(place, block_ranks, coefs, finest, basis_left, dense)
    return call(
        last_kernel,
        shape((leaves, rows, width), BF16),
        [SMEM, SMEM] + [VMEM] * 5,
        scratch=scratch,
        flops=flops,
        moved=moved,
    )(place, block_ranks, coefs_other, finest_other, basis_left, dense, ready)


def solution(mesh):
    clusters = mesh.shape["clus"]
    fine = Mesh(mesh.devices.reshape(clusters, 2, 2), ("clus", "chip", "core"))
    rows = ("chip", "core")
    in_specs = (
        P("clus", rows, None),
        P("clus", rows, None),
        P(None, "clus", rows, None),
        P(None, "clus", rows, None),
        P(),
    )
    return jax.shard_map(
        local, mesh=fine, in_specs=in_specs, out_specs=P("clus", rows, None), check_vma=False
    )
```

time: 315 us -> 97 us (0.31)
  waiting for transfers between devices: 150 us -> 10.8 us
  starting transfers between devices: 107 us -> 37.5 us
  blocking collectives: 19.4 us -> 35.9 us
  between operations: 14 us -> 0.2 us
  matrix products: 9.57 us -> 0 us
  Pallas kernels: 0 us -> 8.59 us
  other arithmetic: 7.59 us -> 1.06 us
    ppermute x28 -> x7, starting transfers between devices: 107 us -> 28.3 us  [swap(): return lax.ppermute(block, axis, [(0, 1), (1, 0)])]
    psum x1 -> x0, waiting for transfers between devices: 70.1 us -> none  [local(): upper, finest = lax.psum((upper, finest), 'rows')]
    ppermute x28 -> x7, waiting for transfers between devices: 79.8 us -> 10.8 us  [swap(): return lax.ppermute(block, axis, [(0, 1), (1, 0)])]
    all_to_all x0 -> x1, blocking collectives: none -> 35.9 us  [local(): lax.all_to_all(tiles.reshape(owners, 8, 128), ('clus', 'chip'), split_axi...]
    psum x1 -> x0, blocking collectives: 19.4 us -> none  [local(): upper, finest = lax.psum((upper, finest), 'rows')]
    dot_general x5 -> x0, matrix products: 9.57 us -> none  [the longest x1 3.34 us: local(): jnp.einsum('klrj,lrh->kjh', basis_right[:upper_count], right_sides, prefe...]
    all_to_all x0 -> x1, starting transfers between devices: none -> 9.27 us  [local(): lax.all_to_all(coefs.reshape(owners, 8, 128), ('clus', 'chip'), split_axi...]
    pallas_call x0 -> x7, Pallas kernels: none -> 8.59 us  [the longest x2 2.05 us: project(): call(functools.partial(project_kernel, other), shape((slots, rank, half),...]
  transfers between devices with their start and end apart: 30 -> 8, of which waited for: 13 -> 2; matrix products, arithmetic and copies ran while one was open for 4% -> 1% of each run, Pallas kernels for 0% -> 4%
where the time goes in v1:
time: 97 us; the launch traced here: 96.4 us
  starting transfers between devices  37.5 us (39%)
  blocking collectives  35.9 us (37%)
  waiting for transfers between devices  10.8 us (11%)
  Pallas kernels  8.59 us (9%)
  local copies, waits for them, and re-layouts  2.29 us (2%)
  other arithmetic  1.06 us (1%)
    all_to_all x1, blocking collectives, local(): lax.all_to_all(tiles.reshape(owners, 8, 128), ('clus', 'chip'), split_axi...  35.9 us
    ppermute x7, starting transfers between devices, swap(): return lax.ppermute(block, axis, [(0, 1), (1, 0)])  28.3 us
    ppermute x7, waiting for transfers between devices, swap(): return lax.ppermute(block, axis, [(0, 1), (1, 0)])  10.8 us
    all_to_all x1, starting transfers between devices, local(): lax.all_to_all(coefs.reshape(owners, 8, 128), ('clus', 'chip'), split_axi...  9.27 us
    unnamed x12, local copies, waits for them, and re-layouts  2.29 us
    pallas_call x2, Pallas kernels, project(): call(functools.partial(project_kernel, other), shape((slots, rank, half),...  2.05 us
  transfers between devices with their start and end apart: 8, of which 2 were waited for; matrix products, arithmetic and copies ran while one was open for 1% of the time, Pallas kernels for 4%

profile of v1, /device:TPU:1, one launch (start us, length us, event | category | flops | bytes accessed | tf_op | source)
XLA Modules:
  0.0 96.4 jit_solution(17593002500358780196)
XLA Ops:
  0.0 0.1 pad_add_fusion.place
  0.1 0.0 copy-start
  0.1 1.0 %copy-done = bf16[2,256,512]{2,1,0:T(8,128)(2,1)S(1)} copy-done((bf16[2,256,512]{2,1,0:T(8,128)(2,1)S(1)}, bf16[2,256,512]{2,1,0:T(8,128)(2,1)}, u32[]{:S(2)}) %copy-start) | copy-done | bytes 524312
  1.1 0.0 copy-start.2
  1.1 1.2 %copy-done.2 = bf16[8,2,256,128]{3,2,1,0:T(8,128)(2,1)S(1)} copy-done((bf16[8,2,256,128]{3,2,1,0:T(8,128)(2,1)S(1)}, bf16[8,2,256,128]{3,2,1,0:T(8,128)(2,1)}, u32[]{:S(2)}) %copy-start.2) | copy-done | bytes 1048600
  2.3 1.0 %shard_map.56 = f32[9,128,256]{2,1,0:T(8,128)S(1)} custom-call(s32[4]{0:T(128)S(1)} %pad_add_fusion.place, bf16[8,2,256,128]{3,2,1,0:T(8,128)(2,1)S(1)} %copy-done.2, bf16[2,256,512]{2,1,0:T(8,128)(2,1)S(1)} %copy-done), custom_call_target="tpu_custom_call" | custom-call | flops 268435456 | bytes 2752512 | tf_op jit(solution)/shard_map/pallas_call | solution.py:174
  3.4 8.8 %collective-permute-start = (f32[9,128,256]{2,1,0:T(8,128)S(1)}, f32[9,128,256]{2,1,0:T(8,128)S(1)}, u32[]{:S(2)}, u32[]{:S(2)}) collective-permute-start(f32[9,128,256]{2,1,0:T(8,128)S(1)} %shard_map.56), channel_id=1, source_target_pairs={{0,1},{1,0},{2,3},{3,2},{4,5},{5,4},{6,7},{7,6},{8,9},{9,8},{10,11... | collective-permute-start | bytes 3538952 | tf_op jit(solution)/shard_map/ppermute | solution.py:156
  12.2 1.0 %shard_map.55.mine = f32[9,128,256]{2,1,0:T(8,128)S(1)} custom-call(s32[4]{0:T(128)S(1)} %pad_add_fusion.place, bf16[8,2,256,128]{3,2,1,0:T(8,128)(2,1)S(1)} %copy-done.2, bf16[2,256,512]{2,1,0:T(8,128)(2,1)S(1)} %copy-done), custom_call_target="tpu_custom_call" | custom-call | flops 268435456 | bytes 2752512 | tf_op jit(solution)/shard_map/pallas_call | solution.py:174
  13.2 1.4 %collective-permute-done.theirs = f32[9,128,256]{2,1,0:T(8,128)S(1)} collective-permute-done((f32[9,128,256]{2,1,0:T(8,128)S(1)}, f32[9,128,256]{2,1,0:T(8,128)S(1)}, u32[]{:S(2)}, u32[]{:S(2)}) %collective-permute-start) | collective-permute-done | bytes 1179680 | tf_op jit(solution)/shard_map/ppermute | solution.py:156
  14.6 0.1 shard_map.57
  14.8 35.9 %all_to_all.10 = bf16[256,8,128]{2,1,0:T(8,128)(2,1)S(1)} all-to-all(bf16[256,8,128]{2,1,0:T(8,128)(2,1)S(1)} %bitcast.11), channel_id=1, replica_groups=mesh['clus'=128,'chip'=2,'core'=2] {'clus','chip'}, dimensions={0} | all-to-all | bytes 1048576 | tf_op jit(solution)/shard_map/all_to_all | solution.py:191
  50.6 0.0 copy-start.1
  50.6 0.0 copy-start.4
  50.7 1.7 %shard_map.58 = bf16[128,2,8,128]{3,2,1,0:T(8,128)(2,1)} custom-call(s32[4]{0:T(128)S(1)} %pad_add_fusion.place, bf16[128,2,8,128]{3,2,1,0:T(8,128)(2,1)S(1)} %bitcast.8), custom_call_target="tpu_custom_call" | custom-call | bytes 1048576 | tf_op jit(solution)/shard_map/pallas_call | solution.py:206
  52.4 9.3 %all-to-all-start.1 = ((bf16[256,8,128]{2,1,0:T(8,128)(2,1)}), bf16[256,8,128]{2,1,0:T(8,128)(2,1)S(1)}, u32[]{:S(2)}, u32[]{:S(2)}) async-start(bf16[256,8,128]{2,1,0:T(8,128)(2,1)} %bitcast.6), calls=%async_computation.1 | async-start | bytes 1048576 | tf_op jit(solution)/shard_map/all_to_all | solution.py:213
  61.7 0.0 copy-done.1
  61.7 1.9 %collective-permute-start.5 = (bf16[2,256,512]{2,1,0:T(8,128)(2,1)S(1)}, bf16[2,256,512]{2,1,0:T(8,128)(2,1)S(1)}, u32[]{:S(2)}, u32[]{:S(2)}) collective-permute-start(bf16[2,256,512]{2,1,0:T(8,128)(2,1)S(1)} %copy-done.1), channel_id=1, source_target_pairs={{0,2},{2,0},{1,3},{3,1},{4,6},{6,4},{5,7},{7,5},{8,10},{10,8},{9,1... | collective-permute-start | bytes 1572872 | tf_op jit(solution)/shard_map/ppermute | solution.py:156
  63.6 3.4 %collective-permute-start.2 = (f32[2,128,256]{2,1,0:T(8,128)S(1)}, f32[2,128,256]{2,1,0:T(8,128)}, u32[]{:S(2)}, u32[]{:S(2)}) collective-permute-start(f32[2,128,256]{2,1,0:T(8,128)S(1)} %get-tuple-element.8), channel_id=1, source_target_pairs={{0,2},{2,0},{1,3},{3,1},{4,6},{6,4},{5,7},{7,5},{8,10},{10,8},{9,1... | collective-permute-start | bytes 786440 | tf_op jit(solution)/shard_map/ppermute | solution.py:156
  67.0 4.4 %collective-permute-start.4 = (bf16[2,256,512]{2,1,0:T(8,128)(2,1)S(1)}, bf16[2,256,512]{2,1,0:T(8,128)(2,1)S(1)}, u32[]{:S(2)}, u32[]{:S(2)}) collective-permute-start(bf16[2,256,512]{2,1,0:T(8,128)(2,1)S(1)} %copy-done.1), channel_id=1, source_target_pairs={{0,1},{1,0},{2,3},{3,2},{4,5},{5,4},{6,7},{7,6},{8,9},{9,8},{10,11... | collective-permute-start | bytes 1572872 | tf_op jit(solution)/shard_map/ppermute | solution.py:156
  71.4 9.4 %collective-permute-done.5.by_chip = bf16[2,256,512]{2,1,0:T(8,128)(2,1)S(1)} collective-permute-done((bf16[2,256,512]{2,1,0:T(8,128)(2,1)S(1)}, bf16[2,256,512]{2,1,0:T(8,128)(2,1)S(1)}, u32[]{:S(2)}, u32[]{:S(2)}) %collective-permute-start.5) | collective-permute-done | bytes 524320 | tf_op jit(solution)/shard_map/ppermute | solution.py:156
  80.8 5.3 %collective-permute-start.6 = (bf16[2,256,512]{2,1,0:T(8,128)(2,1)S(1)}, bf16[2,256,512]{2,1,0:T(8,128)(2,1)}, u32[]{:S(2)}, u32[]{:S(2)}) collective-permute-start(bf16[2,256,512]{2,1,0:T(8,128)(2,1)S(1)} %collective-permute-done.5.by_chip), channel_id=1, source_target_pairs={{0,1},{1,0},{2,3},{3,2},{4,5},{5,4},{6,7},{7,6},{8,9},{9,8},{10,11... | collective-permute-start | bytes 1572872 | tf_op jit(solution)/shard_map/ppermute | solution.py:156
  86.1 0.0 all-to-all-done.1
  86.2 1.9 %collective-permute-start.1 = (bf16[8,16,2,8,128]{4,3,2,1,0:T(8,128)(2,1)S(1)}, bf16[8,16,2,8,128]{4,3,2,1,0:T(8,128)(2,1)S(1)}, u32[]{:S(2)}, u32[]{:S(2)}) collective-permute-start(bf16[8,16,2,8,128]{4,3,2,1,0:T(8,128)(2,1)S(1)} %bitcast.9), channel_id=1, source_target_pairs={{0,1},{1,0},{2,3},{3,2},{4,5},{5,4},{6,7},{7,6},{8,9},{9,8},{10,11... | collective-permute-start | bytes 1572872 | tf_op jit(solution)/shard_map/ppermute | solution.py:156
  88.1 0.0 collective-permute-done.2
  88.1 1.0 %add_convert_fusion.finest = bf16[2,128,256]{2,1,0:T(8,128)(2,1)S(1)} fusion(f32[2,128,256]{2,1,0:T(8,128)S(1)} %get-tuple-element.8, f32[2,128,256]{2,1,0:T(8,128)} %collective-permute-done.2), kind=kLoop, calls=%fused_computation | loop fusion | flops 131072 | bytes 655360 | tf_op jit(solution)/shard_map/convert_element_type | solution.py:197
  89.1 0.0 copy-start.3
  89.1 0.0 copy-start.5
  89.1 2.5 %collective-permute-start.3 = (bf16[2,128,256]{2,1,0:T(8,128)(2,1)S(1)}, bf16[2,128,256]{2,1,0:T(8,128)(2,1)S(1)}, u32[]{:S(2)}, u32[]{:S(2)}) collective-permute-start(bf16[2,128,256]{2,1,0:T(8,128)(2,1)S(1)} %add_convert_fusion.finest), channel_id=1, source_target_pairs={{0,1},{1,0},{2,3},{3,2},{4,5},{5,4},{6,7},{7,6},{8,9},{9,8},{10,11... | collective-permute-start | bytes 393224 | tf_op jit(solution)/shard_map/ppermute | solution.py:156
  91.6 0.0 collective-permute-done.4.by_core
  91.7 0.0 collective-permute-done.6.by_both
  91.7 0.0 copy-done.4
  91.7 1.8 %shard_map.59.dense = f32[2,256,512]{2,1,0:T(8,128)S(1)} custom-call(s32[4]{0:T(128)S(1)} %pad_add_fusion.place, bf16[2,256,1024]{2,1,0:T(8,128)(2,1)S(1)} %copy-done.4, bf16[2,256,512]{2,1,0:T(8,128)(2,1)S(1)} %copy-done.1, bf16[2,256,512]{2,1,0:T(8,128)(2,1)S(1)} %collective-permute-done.4.by_core, ...), custom_call_target="tpu_custom_call" | custom-call | flops 536870912 | bytes 4194304 | tf_op jit(solution)/shard_map/pallas_call | solution.py:199
  93.4 0.0 copy-done.3
  93.5 0.0 copy-done.5
  93.5 1.1 %shard_map.60.ready = bf16[2,256,256]{2,1,0:T(8,128)(2,1)S(1)} custom-call(s32[4]{0:T(128)S(1)} %pad_add_fusion.place, s32[510]{0:T(512)S(1)} %copy-done.5, bf16[8,16,2,8,128]{4,3,2,1,0:T(8,128)(2,1)S(1)} %bitcast.10, bf16[2,128,256]{2,1,0:T(8,128)(2,1)S(1)} %add_convert_fusion.finest, bf16[8,2,256,128]{3,2,1,0:T(8,128)(2,1)S(1)} %copy-done.3, ...), custom_call_target="tpu_custom_call" | custom-call | flops 268435456 | bytes 2621440 | tf_op jit(solution)/shard_map/pallas_call | solution.py:219
  94.5 0.0 collective-permute-done.3.finest
  94.5 0.0 collective-permute-done.1.tiles
  94.6 1.9 %shard_map.61 = bf16[2,256,512]{2,1,0:T(8,128)(2,1)} custom-call(s32[4]{0:T(128)S(1)} %pad_add_fusion.place, s32[510]{0:T(512)S(1)} %copy-done.5, bf16[8,16,2,8,128]{4,3,2,1,0:T(8,128)(2,1)S(1)} %collective-permute-done.1.tiles, bf16[2,128,256]{2,1,0:T(8,128)(2,1)S(1)} %collective-permute-done.3.finest, bf16[8,2,256,128]{3,2,1,0:T(8,128)(2,1)S(1)} %copy-done.3, ...), custom_call_target="tpu_custom_call" | custom-call | flops 268435456 | bytes 2621440 | tf_op jit(solution)/shard_map/pallas_call | solution.py:227
Async XLA Ops:
  0.1 1.0 %copy-start = (bf16[2,256,512]{2,1,0:T(8,128)(2,1)S(1)}, bf16[2,256,512]{2,1,0:T(8,128)(2,1)}, u32[]{:S(2)}) copy-start(bf16[2,256,512]{2,1,0:T(8,128)(2,1)} %own.1) | copy-start | bytes 1572868
  1.1 1.2 %copy-start.2 = (bf16[8,2,256,128]{3,2,1,0:T(8,128)(2,1)S(1)}, bf16[8,2,256,128]{3,2,1,0:T(8,128)(2,1)}, u32[]{:S(2)}) copy-start(bf16[8,2,256,128]{3,2,1,0:T(8,128)(2,1)} %basis.5) | copy-start | bytes 3145732
  3.4 11.3 %collective-permute-start = (f32[9,128,256]{2,1,0:T(8,128)S(1)}, f32[9,128,256]{2,1,0:T(8,128)S(1)}, u32[]{:S(2)}, u32[]{:S(2)}) collective-permute-start(f32[9,128,256]{2,1,0:T(8,128)S(1)} %shard_map.56), channel_id=1, source_target_pairs={{0,1},{1,0},{2,3},{3,2},{4,5},{5,4},{6,7},{7,6},{8,9},{9,8},{10,11... | collective-permute-start | bytes 3538952 | tf_op jit(solution)/shard_map/ppermute | solution.py:156
  50.6 11.0 %copy-start.1 = (bf16[2,256,512]{2,1,0:T(8,128)(2,1)S(1)}, bf16[2,256,512]{2,1,0:T(8,128)(2,1)}, u32[]{:S(2)}) copy-start(bf16[2,256,512]{2,1,0:T(8,128)(2,1)} %own.1) | copy-start | bytes 1572868
  50.6 41.0 %copy-start.4 = (bf16[2,256,1024]{2,1,0:T(8,128)(2,1)S(1)}, bf16[2,256,1024]{2,1,0:T(8,128)(2,1)}, u32[]{:S(2)}) copy-start(bf16[2,256,1024]{2,1,0:T(8,128)(2,1)} %blocks.1) | copy-start | bytes 3145732
  52.4 33.8 %all-to-all-start.1 = ((bf16[256,8,128]{2,1,0:T(8,128)(2,1)}), bf16[256,8,128]{2,1,0:T(8,128)(2,1)S(1)}, u32[]{:S(2)}, u32[]{:S(2)}) async-start(bf16[256,8,128]{2,1,0:T(8,128)(2,1)} %bitcast.6), calls=%async_computation.1 | async-start | bytes 1048576 | tf_op jit(solution)/shard_map/all_to_all | solution.py:213
  61.7 19.1 %collective-permute-start.5 = (bf16[2,256,512]{2,1,0:T(8,128)(2,1)S(1)}, bf16[2,256,512]{2,1,0:T(8,128)(2,1)S(1)}, u32[]{:S(2)}, u32[]{:S(2)}) collective-permute-start(bf16[2,256,512]{2,1,0:T(8,128)(2,1)S(1)} %copy-done.1), channel_id=1, source_target_pairs={{0,2},{2,0},{1,3},{3,1},{4,6},{6,4},{5,7},{7,5},{8,10},{10,8},{9,1... | collective-permute-start | bytes 1572872 | tf_op jit(solution)/shard_map/ppermute | solution.py:156
  63.6 24.5 %collective-permute-start.2 = (f32[2,128,256]{2,1,0:T(8,128)S(1)}, f32[2,128,256]{2,1,0:T(8,128)}, u32[]{:S(2)}, u32[]{:S(2)}) collective-permute-start(f32[2,128,256]{2,1,0:T(8,128)S(1)} %get-tuple-element.8), channel_id=1, source_target_pairs={{0,2},{2,0},{1,3},{3,1},{4,6},{6,4},{5,7},{7,5},{8,10},{10,8},{9,1... | collective-permute-start | bytes 786440 | tf_op jit(solution)/shard_map/ppermute | solution.py:156
  67.0 24.7 %collective-permute-start.4 = (bf16[2,256,512]{2,1,0:T(8,128)(2,1)S(1)}, bf16[2,256,512]{2,1,0:T(8,128)(2,1)S(1)}, u32[]{:S(2)}, u32[]{:S(2)}) collective-permute-start(bf16[2,256,512]{2,1,0:T(8,128)(2,1)S(1)} %copy-done.1), channel_id=1, source_target_pairs={{0,1},{1,0},{2,3},{3,2},{4,5},{5,4},{6,7},{7,6},{8,9},{9,8},{10,11... | collective-permute-start | bytes 1572872 | tf_op jit(solution)/shard_map/ppermute | solution.py:156
  80.8 10.8 %collective-permute-start.6 = (bf16[2,256,512]{2,1,0:T(8,128)(2,1)S(1)}, bf16[2,256,512]{2,1,0:T(8,128)(2,1)}, u32[]{:S(2)}, u32[]{:S(2)}) collective-permute-start(bf16[2,256,512]{2,1,0:T(8,128)(2,1)S(1)} %collective-permute-done.5.by_chip), channel_id=1, source_target_pairs={{0,1},{1,0},{2,3},{3,2},{4,5},{5,4},{6,7},{7,6},{8,9},{9,8},{10,11... | collective-permute-start | bytes 1572872 | tf_op jit(solution)/shard_map/ppermute | solution.py:156
  86.2 8.4 %collective-permute-start.1 = (bf16[8,16,2,8,128]{4,3,2,1,0:T(8,128)(2,1)S(1)}, bf16[8,16,2,8,128]{4,3,2,1,0:T(8,128)(2,1)S(1)}, u32[]{:S(2)}, u32[]{:S(2)}) collective-permute-start(bf16[8,16,2,8,128]{4,3,2,1,0:T(8,128)(2,1)S(1)} %bitcast.9), channel_id=1, source_target_pairs={{0,1},{1,0},{2,3},{3,2},{4,5},{5,4},{6,7},{7,6},{8,9},{9,8},{10,11... | collective-permute-start | bytes 1572872 | tf_op jit(solution)/shard_map/ppermute | solution.py:156
  89.1 4.4 %copy-start.3 = (bf16[8,2,256,128]{3,2,1,0:T(8,128)(2,1)S(1)}, bf16[8,2,256,128]{3,2,1,0:T(8,128)(2,1)}, u32[]{:S(2)}) copy-start(bf16[8,2,256,128]{3,2,1,0:T(8,128)(2,1)} %basis.7) | copy-start | bytes 3145732
  89.1 4.4 %copy-start.5 = (s32[510]{0:T(512)S(1)}, s32[510]{0:T(512)}, u32[]{:S(2)}) copy-start(s32[510]{0:T(512)} %ranks.3) | copy-start | bytes 6124
  89.1 5.4 %collective-permute-start.3 = (bf16[2,128,256]{2,1,0:T(8,128)(2,1)S(1)}, bf16[2,128,256]{2,1,0:T(8,128)(2,1)S(1)}, u32[]{:S(2)}, u32[]{:S(2)}) collective-permute-start(bf16[2,128,256]{2,1,0:T(8,128)(2,1)S(1)} %add_convert_fusion.finest), channel_id=1, source_target_pairs={{0,1},{1,0},{2,3},{3,2},{4,5},{5,4},{6,7},{7,6},{8,9},{9,8},{10,11... | collective-permute-start | bytes 393224 | tf_op jit(solution)/shard_map/ppermute | solution.py:156

commit v2 on v1

v2 whole, which is shorter than its diff:
```python
import functools

import jax
import jax.numpy as jnp
from jax import lax
from jax.experimental import pallas as pl
from jax.experimental.pallas import tpu as pltpu
from jax.sharding import Mesh, PartitionSpec as P

VMEM_BYTES = 48 * 1024 * 1024
F32 = jnp.float32
BF16 = jnp.bfloat16


def call(kernel, out_shape, in_specs, scratch=(), flops=0, moved=0):
    many = isinstance(out_shape, (list, tuple))
    whole = pl.BlockSpec(memory_space=pltpu.VMEM)
    return pl.pallas_call(
        kernel,
        out_shape=out_shape,
        in_specs=in_specs,
        out_specs=[whole] * len(out_shape) if many else whole,
        scratch_shapes=list(scratch),
        compiler_params=pltpu.CompilerParams(vmem_limit_bytes=VMEM_BYTES),
        cost_estimate=pl.CostEstimate(flops=flops, bytes_accessed=moved, transcendentals=0),
    )


SMEM = pl.BlockSpec(memory_space=pltpu.SMEM)
VMEM = pl.BlockSpec(memory_space=pltpu.VMEM)
ANY = pl.BlockSpec(memory_space=pl.ANY)


def project_kernel(other, place, basis, sides, out):
    levels, leaves, rows, rank = basis.shape
    half = sides.shape[2] // 2
    core = place[1]
    column = pl.multiple_of((1 - core if other else core) * half, half)
    both = sides[:, :, pl.ds(column, half)]
    contract = (((0,), (0,)), ((), ()))
    for level in range(levels - 1):
        out[level] = lax.dot_general(
            basis[level].reshape(leaves * rows, rank),
            both.reshape(leaves * rows, half),
            contract,
            preferred_element_type=F32,
        )
    for leaf in range(leaves):
        out[levels - 1 + leaf] = lax.dot_general(
            basis[levels - 1, leaf], both[leaf], contract, preferred_element_type=F32
        )


def combine_kernel(mine, theirs, tiles, finest):
    down, upper, across = tiles.shape[:3]
    for level in range(upper):
        total = mine[level] + theirs[level]
        for col in range(across):
            part = total[:, col * 128 : (col + 1) * 128]
            tiles[:, level, col] = part.reshape(down, 8, 128).astype(BF16)
    finest[...] = (mine[upper:] + theirs[upper:]).astype(BF16)


def ring_kernel(place, parts, *rest):
    out = rest[-1]
    high = place[3]
    bits = out.shape[0].bit_length() - 1
    total = [None] * bits
    for level in range(bits):
        for member in range(parts.shape[0]):
            part = parts[member, level].astype(F32)
            total[level] = part if total[level] is None else total[level] + part
    out[high] = jnp.zeros(out.shape[1:], F32)
    for step in range(1, out.shape[0]):
        out[jnp.bitwise_xor(high, step)] = total[bits - step.bit_length()]


def low_kernel(parts, sides, out, sides_out):
    sides_out[...] = sides[...]
    count, low = out.shape[:2]
    first = parts.shape[1] - low
    for level in range(low):
        part = [
            parts[2 * z, first + level].astype(F32) + parts[2 * z + 1, first + level].astype(F32)
            for z in range(count)
        ]
        distance = low - 1 - level
        size = 1 << distance
        sums = [sum(part[g * size + 1 : (g + 1) * size], part[g * size]) for g in range(count // size)]
        for z in range(count):
            out[z, level] = sums[(z >> distance) ^ 1].astype(BF16)


def back_kernel(place, high_parts, low, out):
    high = place[3]
    steps = high_parts.shape[0]
    bits = steps.bit_length() - 1
    for level in range(bits):
        first = 1 << (bits - 1 - level)
        total = high_parts[jnp.bitwise_xor(high, first)]
        for step in range(first + 1, 2 * first):
            total = total + high_parts[jnp.bitwise_xor(high, step)]
        rounded = total.astype(BF16)
        for member in range(out.shape[0]):
            out[member, level] = rounded
    for member in range(out.shape[0]):
        out[member, bits:] = low[member // 2]


def dense_kernel(place, blocks, own, by_core, by_chip, by_both, out):
    leaves, rows, _ = blocks.shape
    row = place[2]
    for leaf in range(leaves):
        total = None
        for step, sides in enumerate((own, by_core, by_chip, by_both)):
            column = pl.multiple_of(jnp.bitwise_xor(row, step) * rows, rows)
            term = jnp.dot(
                blocks[leaf, :, pl.ds(column, rows)], sides[leaf], preferred_element_type=F32
            )
            total = term if total is None else total + term
        out[leaf] = total


def gather_kernel(place, ranks, tiles, finest, finest_chip, dense, out):
    rank = tiles.shape[0] * 8
    upper, across = tiles.shape[1:3]
    position = place[0]

    def keep(shape, heap):
        return lax.broadcasted_iota(jnp.int32, shape, 0) < ranks[heap]

    for level in range(upper):
        heap = 2 ** (level + 1) - 2 + lax.shift_right_logical(position, upper - 1 - level)
        for col in range(across):
            part = tiles[:, level, col].astype(F32).reshape(rank, 128)
            part = jnp.where(keep(part.shape, heap), part, 0.0)
            row = (1 + level) * rank
            out[row : row + rank, col * 128 : (col + 1) * 128] = part.astype(BF16)
    for leaf in range(2):
        heap = 2 ** (upper + 1) - 2 + 2 * position + leaf
        part = finest[1 - leaf].astype(F32) + finest_chip[1 - leaf].astype(F32)
        part = jnp.where(keep(part.shape, heap), part, 0.0)
        row = leaf * (1 + upper) * rank
        out[row : row + rank, :] = part.astype(BF16)


def update(coef, basis, dense, column, store):
    levels, leaves, _, rank = basis.shape
    half = coef.shape[1]
    for leaf in range(leaves):
        order = list(range(levels - 1))
        order = order + [levels - 1] if leaf else [levels - 1] + order
        left = jnp.concatenate([basis[level, leaf] for level in order], axis=1)
        right = coef[leaf * rank : (leaf + levels) * rank, :]
        term = jnp.dot(left, right, preferred_element_type=F32)
        store(leaf, (dense[leaf, :, pl.ds(column, half)] + term).astype(BF16))


def own_kernel(place, coef, basis, dense, out):
    half = out.shape[2]
    column = pl.multiple_of(place[1] * half, half)

    def store(leaf, value):
        out[leaf] = value

    update(coef, basis, dense, column, store)


def last_kernel(place, coef, basis, dense, ready, out):
    half = ready.shape[2]
    mine = pl.multiple_of(place[1] * half, half)
    column = pl.multiple_of((1 - place[1]) * half, half)
    out[:, :, pl.ds(mine, half)] = ready[...]

    def store(leaf, value):
        out[leaf, :, pl.ds(column, half)] = value

    update(coef, basis, dense, column, store)


def swap(block, axis):
    return lax.ppermute(block, axis, [(0, 1), (1, 0)])


def local(right_sides, leaf_blocks, basis_left, basis_right, block_ranks):
    leaves, rows, width = right_sides.shape
    levels, _, _, rank = basis_left.shape
    half = width // 2
    upper = levels - 1
    ring = lax.axis_size("z")
    highs = lax.axis_size("high")
    low_levels = ring.bit_length() - 1
    owners = 2 * ring
    high = lax.axis_index("high")
    position = ring * high + lax.axis_index("z")
    chip = lax.axis_index("chip")
    core = lax.axis_index("core")
    place = jnp.stack([position, core, 2 * chip + core, high]).astype(jnp.int32)
    shape = jax.ShapeDtypeStruct
    slots = upper + leaves
    tile = (half // 128, 8, 128)
    flops = 2 * levels * leaves * rows * rank * half

    def project(other):
        return call(
            functools.partial(project_kernel, other),
            shape((slots, rank, half), F32),
            [SMEM, VMEM, VMEM],
            flops=flops,
            moved=2 * (basis_right.size + right_sides.size) + 4 * slots * rank * half,
        )(place, basis_right, right_sides)

    def exchange(block, axes):
        flat = block.reshape((block.shape[0], -1, 128))
        moved = lax.all_to_all(flat, axes, split_axis=0, concat_axis=0, tiled=True)
        return moved.reshape(block.shape)

    sent = project(True)
    theirs = swap(sent, "core")
    mine = project(False)
    tiles, finest = call(
        combine_kernel,
        [shape((owners, upper) + tile, BF16), shape((leaves, rank, half), BF16)],
        [VMEM, VMEM],
        moved=10 * slots * rank * half,
    )(mine, theirs)
    parts = exchange(tiles, ("z", "chip"))
    by_core = swap(right_sides, "core")
    finest_chip = swap(finest, "chip")
    to_high = call(
        ring_kernel,
        shape((highs,) + tile, F32),
        [SMEM, VMEM, ANY, ANY],
        moved=2 * parts.size,
    )(place, parts, finest_chip, by_core)
    low, sides_late = call(
        low_kernel,
        [shape((ring, low_levels) + tile, BF16), shape(right_sides.shape, BF16)],
        [VMEM, VMEM],
        moved=2 * parts.size + 4 * right_sides.size,
    )(parts, right_sides)
    from_high = exchange(to_high, ("high",))
    by_chip = swap(sides_late, "chip")
    by_both = swap(by_chip, "core")
    dense = call(
        dense_kernel,
        shape((leaves, rows, width), F32),
        [SMEM] + [VMEM] * 5,
        flops=2 * leaves * rows * leaf_blocks.shape[2] * width,
        moved=2 * leaf_blocks.size + 8 * right_sides.size + 4 * right_sides.size,
    )(place, leaf_blocks, right_sides, by_core, by_chip, by_both)
    coefs = call(
        back_kernel,
        shape(tiles.shape, BF16),
        [SMEM, VMEM, VMEM],
        moved=4 * parts.size,
    )(place, from_high, low)
    coefs = exchange(coefs, ("z", "chip"))
    coef = call(
        gather_kernel,
        shape((slots * rank, half), BF16),
        [SMEM, SMEM, VMEM, VMEM, VMEM, ANY],
        moved=4 * slots * rank * half,
    )(place, block_ranks, coefs, finest, finest_chip, dense)
    coef_other = swap(coef, "core")
    moved = 2 * (basis_left.size + coef.size) + 4 * right_sides.size
    ready = call(
        own_kernel,
        shape((leaves, rows, half), BF16),
        [SMEM] + [VMEM] * 3,
        flops=flops,
        moved=moved,
    )(place, coef, basis_left, dense)
    return call(
        last_kernel,
        shape((leaves, rows, width), BF16),
        [SMEM] + [VMEM] * 4,
        flops=flops,
        moved=moved,
    )(place, coef_other, basis_left, dense, ready)


def solution(mesh):
    clusters = mesh.shape["clus"]
    ring = 8
    fine = Mesh(
        mesh.devices.reshape(clusters // ring, ring, 2, 2), ("high", "z", "chip", "core")
    )
    places, rows = ("high", "z"), ("chip", "core")
    in_specs = (
        P(places, rows, None),
        P(places, rows, None),
        P(None, places, rows, None),
        P(None, places, rows, None),
        P(),
    )
    return jax.shard_map(
        local, mesh=fine, in_specs=in_specs, out_specs=P(places, rows, None), check_vma=False
    )
```

time: 97 us -> 87.1 us (0.90)
  blocking collectives: 35.9 us -> 0 us
  waiting for transfers between devices: 10.8 us -> 24.5 us
  starting transfers between devices: 37.5 us -> 47.9 us
  Pallas kernels: 8.59 us -> 10.3 us
  local copies, waits for them, and re-layouts: 2.29 us -> 3.5 us
  other arithmetic: 1.06 us -> 0.08 us
    all_to_all x1 -> x0, blocking collectives: 35.9 us -> none  [local(): lax.all_to_all(tiles.reshape(owners, 8, 128), ('clus', 'chip'), split_axi...]
    all_to_all x1 -> x3, waiting for transfers between devices: 0.01 us -> 15.3 us  [exchange(): moved = lax.all_to_all(flat, axes, split_axis=0, concat_axis=0, tiled=True)]
    all_to_all x1 -> x3, starting transfers between devices: 9.27 us -> 20.7 us  [exchange(): moved = lax.all_to_all(flat, axes, split_axis=0, concat_axis=0, tiled=True)]
    pallas_call x4 -> x7, Pallas kernels: 4.78 us -> 7.02 us  [the longest x1 1.77 us: local(): call(last_kernel, shape((leaves, rows, width), BF16), [SMEM] + [VMEM] * 4...]
    ppermute x7 -> x6, waiting for transfers between devices: 10.8 us -> 9.21 us  [swap(): return lax.ppermute(block, axis, [(0, 1), (1, 0)])]
    unnamed x12, local copies, waits for them, and re-layouts: 2.29 us -> 3.5 us
    ppermute x7 -> x6, starting transfers between devices: 28.3 us -> 27.3 us  [swap(): return lax.ppermute(block, axis, [(0, 1), (1, 0)])]
    convert_element_type x1 -> x0, other arithmetic: 0.98 us -> none  [local(): finest = (finest + swap(finest, 'chip')).astype(BF16)]
  transfers between devices with their start and end apart: 8 -> 9, of which waited for: 2 -> 7; matrix products, arithmetic and copies ran while one was open for 1% -> 0% of each run, Pallas kernels for 4% -> 5%
where the time goes in v2:
time: 87.1 us; the launch traced here: 86.5 us
  starting transfers between devices  47.9 us (55%)
  waiting for transfers between devices  24.5 us (28%)
  Pallas kernels  10.3 us (12%)
  local copies, waits for them, and re-layouts  3.5 us (4%)
    ppermute x6, starting transfers between devices, swap(): return lax.ppermute(block, axis, [(0, 1), (1, 0)])  27.3 us
    all_to_all x3, starting transfers between devices, exchange(): moved = lax.all_to_all(flat, axes, split_axis=0, concat_axis=0, tiled=True)  20.7 us
    all_to_all x3, waiting for transfers between devices, exchange(): moved = lax.all_to_all(flat, axes, split_axis=0, concat_axis=0, tiled=True)  15.3 us
    ppermute x6, waiting for transfers between devices, swap(): return lax.ppermute(block, axis, [(0, 1), (1, 0)])  9.21 us
    unnamed x12, local copies, waits for them, and re-layouts  3.5 us
    pallas_call x2, Pallas kernels, project(): call(functools.partial(project_kernel, other), shape((slots, rank, half),...  2.05 us
    pallas_call x1, Pallas kernels, local(): call(last_kernel, shape((leaves, rows, width), BF16), [SMEM] + [VMEM] * 4...  1.77 us
  transfers between devices with their start and end apart: 9, of which 7 were waited for; matrix products, arithmetic and copies ran while one was open for 0% of the time, Pallas kernels for 5%

profile of v2, /device:TPU:1, one launch (start us, length us, event | category | flops | bytes accessed | tf_op | source)
XLA Modules:
  0.0 86.5 jit_solution(7985097959111543712)
XLA Ops:
  0.0 0.1 pad_add_fusion.place
  0.1 0.0 copy-start
  0.1 1.0 %copy-done = bf16[2,256,512]{2,1,0:T(8,128)(2,1)S(1)} copy-done((bf16[2,256,512]{2,1,0:T(8,128)(2,1)S(1)}, bf16[2,256,512]{2,1,0:T(8,128)(2,1)}, u32[]{:S(2)}) %copy-start) | copy-done | bytes 524312
  1.1 0.0 copy-start.3
  1.1 1.2 %copy-done.3 = bf16[8,2,256,128]{3,2,1,0:T(8,128)(2,1)S(1)} copy-done((bf16[8,2,256,128]{3,2,1,0:T(8,128)(2,1)S(1)}, bf16[8,2,256,128]{3,2,1,0:T(8,128)(2,1)}, u32[]{:S(2)}) %copy-start.3) | copy-done | bytes 1048600
  2.3 1.0 %shard_map.56 = f32[9,128,256]{2,1,0:T(8,128)S(1)} custom-call(s32[4]{0:T(128)S(1)} %pad_add_fusion.place, bf16[8,2,256,128]{3,2,1,0:T(8,128)(2,1)S(1)} %copy-done.3, bf16[2,256,512]{2,1,0:T(8,128)(2,1)S(1)} %copy-done), custom_call_target="tpu_custom_call" | custom-call | flops 268435456 | bytes 2752512 | tf_op jit(solution)/shard_map/pallas_call | solution.py:205
  3.4 8.8 %collective-permute-start = (f32[9,128,256]{2,1,0:T(8,128)S(1)}, f32[9,128,256]{2,1,0:T(8,128)S(1)}, u32[]{:S(2)}, u32[]{:S(2)}) collective-permute-start(f32[9,128,256]{2,1,0:T(8,128)S(1)} %shard_map.56), channel_id=1, source_target_pairs={{0,1},{1,0},{2,3},{3,2},{4,5},{5,4},{6,7},{7,6},{8,9},{9,8},{10,11... | collective-permute-start | bytes 3538952 | tf_op jit(solution)/shard_map/ppermute | solution.py:182
  12.2 1.0 %shard_map.55.mine = f32[9,128,256]{2,1,0:T(8,128)S(1)} custom-call(s32[4]{0:T(128)S(1)} %pad_add_fusion.place, bf16[8,2,256,128]{3,2,1,0:T(8,128)(2,1)S(1)} %copy-done.3, bf16[2,256,512]{2,1,0:T(8,128)(2,1)S(1)} %copy-done), custom_call_target="tpu_custom_call" | custom-call | flops 268435456 | bytes 2752512 | tf_op jit(solution)/shard_map/pallas_call | solution.py:205
  13.2 0.0 copy-start.1
  13.2 1.4 %collective-permute-done.theirs = f32[9,128,256]{2,1,0:T(8,128)S(1)} collective-permute-done((f32[9,128,256]{2,1,0:T(8,128)S(1)}, f32[9,128,256]{2,1,0:T(8,128)S(1)}, u32[]{:S(2)}, u32[]{:S(2)}) %collective-permute-start) | collective-permute-done | bytes 1179680 | tf_op jit(solution)/shard_map/ppermute | solution.py:182
  14.6 0.9 %shard_map.57 = (bf16[16,7,2,8,128]{4,3,2,1,0:T(8,128)(2,1)}, bf16[2,128,256]{2,1,0:T(8,128)(2,1)S(1)}) custom-call(f32[9,128,256]{2,1,0:T(8,128)S(1)} %shard_map.55.mine, f32[9,128,256]{2,1,0:T(8,128)S(1)} %collective-permute-done.theirs), custom_call_target="tpu_custom_call" | custom-call | bytes 2949120 | tf_op jit(solution)/shard_map/pallas_call | solution.py:221
  15.5 5.7 %all-to-all-start = ((bf16[16,112,128]{2,1,0:T(8,128)(2,1)}), bf16[16,112,128]{2,1,0:T(8,128)(2,1)S(1)}, u32[]{:S(2)}, u32[]{:S(2)}) async-start(bf16[16,112,128]{2,1,0:T(8,128)(2,1)} %bitcast.4), calls=%async_computation | async-start | bytes 917504 | tf_op jit(solution)/shard_map/all_to_all | solution.py:215
  21.2 0.0 copy-done.1
  21.2 2.6 %collective-permute-start.2 = (bf16[2,256,512]{2,1,0:T(8,128)(2,1)S(1)}, bf16[2,256,512]{2,1,0:T(8,128)(2,1)S(1)}, u32[]{:S(2)}, u32[]{:S(2)}) collective-permute-start(bf16[2,256,512]{2,1,0:T(8,128)(2,1)S(1)} %copy-done.1), channel_id=1, source_target_pairs={{0,1},{1,0},{2,3},{3,2},{4,5},{5,4},{6,7},{7,6},{8,9},{9,8},{10,11... | collective-permute-start | bytes 1572872 | tf_op jit(solution)/shard_map/ppermute | solution.py:182
  23.8 3.5 %collective-permute-start.1 = (bf16[2,128,256]{2,1,0:T(8,128)(2,1)S(1)}, bf16[2,128,256]{2,1,0:T(8,128)(2,1)S(1)}, u32[]{:S(2)}, u32[]{:S(2)}) collective-permute-start(bf16[2,128,256]{2,1,0:T(8,128)(2,1)S(1)} %get-tuple-element.10.finest), channel_id=1, source_target_pairs={{0,2},{2,0},{1,3},{3,1},{4,6},{6,4},{5,7},{7,5},{8,10},{10,8},{9,1... | collective-permute-start | bytes 393224 | tf_op jit(solution)/shard_map/ppermute | solution.py:182
  27.4 0.0 collective-permute-done.2.rest_1_.by_core
  27.4 5.7 %collective-permute-done.1.rest_0_.finest_chip = bf16[2,128,256]{2,1,0:T(8,128)(2,1)S(1)} collective-permute-done((bf16[2,128,256]{2,1,0:T(8,128)(2,1)S(1)}, bf16[2,128,256]{2,1,0:T(8,128)(2,1)S(1)}, u32[]{:S(2)}, u32[]{:S(2)}) %collective-permute-start.1) | collective-permute-done | bytes 131104 | tf_op jit(solution)/shard_map/ppermute | solution.py:182
  33.0 2.9 %all-to-all-done = bf16[16,112,128]{2,1,0:T(8,128)(2,1)S(1)} async-done(((bf16[16,112,128]{2,1,0:T(8,128)(2,1)}), bf16[16,112,128]{2,1,0:T(8,128)(2,1)S(1)}, u32[]{:S(2)}, u32[]{:S(2)}) %all-to-all-start) | async-done | bytes 458784 | tf_op jit(solution)/shard_map/all_to_all | solution.py:215
  35.9 1.2 %shard_map.58 = f32[16,2,8,128]{3,2,1,0:T(8,128)} custom-call(s32[4]{0:T(128)S(1)} %pad_add_fusion.place, bf16[16,7,2,8,128]{4,3,2,1,0:T(8,128)(2,1)S(1)} %bitcast.10, bf16[2,128,256]{2,1,0:T(8,128)(2,1)S(1)} %collective-permute-done.1.rest_0_.finest_chip, bf16[2,256,512]{2,1,0:T(8,128)(2,1)S(1)} %collective-permute-done.2.rest_1_.by_core), custom_call_target="tpu_custom_call" | custom-call | bytes 458752 | tf_op jit(solution)/shard_map/pallas_call | solution.py:230
  37.2 9.1 %all-to-all-start.1 = ((f32[16,16,128]{2,1,0:T(8,128)}), f32[16,16,128]{2,1,0:T(8,128)S(1)}, u32[]{:S(2)}, u32[]{:S(2)}) async-start(f32[16,16,128]{2,1,0:T(8,128)} %bitcast.6), calls=%async_computation.1 | async-start | bytes 262144 | tf_op jit(solution)/shard_map/all_to_all | solution.py:215
  46.3 0.1 shard_map.59
  46.3 1.9 %collective-permute-start.3 = (bf16[2,256,512]{2,1,0:T(8,128)(2,1)S(1)}, bf16[2,256,512]{2,1,0:T(8,128)(2,1)S(1)}, u32[]{:S(2)}, u32[]{:S(2)}) collective-permute-start(bf16[2,256,512]{2,1,0:T(8,128)(2,1)S(1)} %get-tuple-element.12), channel_id=1, source_target_pairs={{0,2},{2,0},{1,3},{3,1},{4,6},{6,4},{5,7},{7,5},{8,10},{10,8},{9,1... | collective-permute-start | bytes 1572872 | tf_op jit(solution)/shard_map/ppermute | solution.py:182
  48.3 8.0 %all-to-all-done.1 = f32[16,16,128]{2,1,0:T(8,128)S(1)} async-done(((f32[16,16,128]{2,1,0:T(8,128)}), f32[16,16,128]{2,1,0:T(8,128)S(1)}, u32[]{:S(2)}, u32[]{:S(2)}) %all-to-all-start.1) | async-done | bytes 131104 | tf_op jit(solution)/shard_map/all_to_all | solution.py:215
  56.3 1.4 %shard_map.60 = bf16[16,7,2,8,128]{4,3,2,1,0:T(8,128)(2,1)} custom-call(s32[4]{0:T(128)S(1)} %pad_add_fusion.place, f32[16,2,8,128]{3,2,1,0:T(8,128)S(1)} %bitcast.13, bf16[8,3,2,8,128]{4,3,2,1,0:T(8,128)(2,1)S(1)} %get-tuple-element.11.low), custom_call_target="tpu_custom_call" | custom-call | bytes 917504 | tf_op jit(solution)/shard_map/pallas_call | solution.py:252
  57.6 0.0 copy-start.5
  57.6 5.9 %all-to-all-start.2 = ((bf16[16,112,128]{2,1,0:T(8,128)(2,1)}), bf16[16,112,128]{2,1,0:T(8,128)(2,1)S(1)}, u32[]{:S(2)}, u32[]{:S(2)}) async-start(bf16[16,112,128]{2,1,0:T(8,128)(2,1)} %bitcast.8), calls=%async_computation.2 | async-start | bytes 917504 | tf_op jit(solution)/shard_map/all_to_all | solution.py:215
  63.5 0.0 collective-permute-done.3.by_chip
  63.5 4.3 %collective-permute-start.4 = (bf16[2,256,512]{2,1,0:T(8,128)(2,1)S(1)}, bf16[2,256,512]{2,1,0:T(8,128)(2,1)S(1)}, u32[]{:S(2)}, u32[]{:S(2)}) collective-permute-start(bf16[2,256,512]{2,1,0:T(8,128)(2,1)S(1)} %collective-permute-done.3.by_chip), channel_id=1, source_target_pairs={{0,1},{1,0},{2,3},{3,2},{4,5},{5,4},{6,7},{7,6},{8,9},{9,8},{10,11... | collective-permute-start | bytes 1572872 | tf_op jit(solution)/shard_map/ppermute | solution.py:182
  67.8 1.5 %collective-permute-done.4.by_both = bf16[2,256,512]{2,1,0:T(8,128)(2,1)S(1)} collective-permute-done((bf16[2,256,512]{2,1,0:T(8,128)(2,1)S(1)}, bf16[2,256,512]{2,1,0:T(8,128)(2,1)S(1)}, u32[]{:S(2)}, u32[]{:S(2)}) %collective-permute-start.4) | collective-permute-done | bytes 524320 | tf_op jit(solution)/shard_map/ppermute | solution.py:182
  69.3 0.0 copy-start.4
  69.3 1.2 %copy-done.4 = bf16[2,256,1024]{2,1,0:T(8,128)(2,1)S(1)} copy-done((bf16[2,256,1024]{2,1,0:T(8,128)(2,1)S(1)}, bf16[2,256,1024]{2,1,0:T(8,128)(2,1)}, u32[]{:S(2)}) %copy-start.4) | copy-done | bytes 1048600
  70.5 1.3 %shard_map.61.dense = f32[2,256,512]{2,1,0:T(8,128)S(1)} custom-call(s32[4]{0:T(128)S(1)} %pad_add_fusion.place, bf16[2,256,1024]{2,1,0:T(8,128)(2,1)S(1)} %copy-done.4, bf16[2,256,512]{2,1,0:T(8,128)(2,1)S(1)} %copy-done.1, bf16[2,256,512]{2,1,0:T(8,128)(2,1)S(1)} %collective-permute-done.2.rest_1_.by_core, ...), custom_call_target="tpu_custom_call" | custom-call | flops 536870912 | bytes 4194304 | tf_op jit(solution)/shard_map/pallas_call | solution.py:245
  71.8 4.4 %all-to-all-done.2 = bf16[16,112,128]{2,1,0:T(8,128)(2,1)S(1)} async-done(((bf16[16,112,128]{2,1,0:T(8,128)(2,1)}), bf16[16,112,128]{2,1,0:T(8,128)(2,1)S(1)}, u32[]{:S(2)}, u32[]{:S(2)}) %all-to-all-start.2) | async-done | bytes 458784 | tf_op jit(solution)/shard_map/all_to_all | solution.py:215
  76.2 0.0 copy-done.5
  76.2 0.0 copy-start.2
  76.2 0.7 shard_map.62.coef
  76.9 6.2 %collective-permute-start.5 = (bf16[1152,256]{1,0:T(8,128)(2,1)S(1)}, bf16[1152,256]{1,0:T(8,128)(2,1)S(1)}, u32[]{:S(2)}, u32[]{:S(2)}) collective-permute-start(bf16[1152,256]{1,0:T(8,128)(2,1)S(1)} %shard_map.62.coef), channel_id=1, source_target_pairs={{0,1},{1,0},{2,3},{3,2},{4,5},{5,4},{6,7},{7,6},{8,9},{9,8},{10,11... | collective-permute-start | bytes 1769480 | tf_op jit(solution)/shard_map/ppermute | solution.py:182
  83.1 0.0 copy-done.2
  83.1 1.0 %shard_map.63.ready = bf16[2,256,256]{2,1,0:T(8,128)(2,1)S(1)} custom-call(s32[4]{0:T(128)S(1)} %pad_add_fusion.place, bf16[1152,256]{1,0:T(8,128)(2,1)S(1)} %shard_map.62.coef, bf16[8,2,256,128]{3,2,1,0:T(8,128)(2,1)S(1)} %copy-done.2, f32[2,256,512]{2,1,0:T(8,128)S(1)} %shard_map.61.dense), custom_call_target="tpu_custom_call" | custom-call | flops 268435456 | bytes 2686976 | tf_op jit(solution)/shard_map/pallas_call | solution.py:267
  84.1 0.6 collective-permute-done.5.coef
  84.7 1.8 %shard_map.64 = bf16[2,256,512]{2,1,0:T(8,128)(2,1)} custom-call(s32[4]{0:T(128)S(1)} %pad_add_fusion.place, bf16[1152,256]{1,0:T(8,128)(2,1)S(1)} %collective-permute-done.5.coef, bf16[8,2,256,128]{3,2,1,0:T(8,128)(2,1)S(1)} %copy-done.2, f32[2,256,512]{2,1,0:T(8,128)S(1)} %shard_map.61.dense, bf16[2,256,256]{2,1,0:T(8,128)(2,1)S(1)} %shard_map.63.ready), custom_call_target="tpu_custom_call" | custom-call | flops 268435456 | bytes 2686976 | tf_op jit(solution)/shard_map/pallas_call | solution.py:274
Async XLA Ops:
  0.1 1.0 %copy-start = (bf16[2,256,512]{2,1,0:T(8,128)(2,1)S(1)}, bf16[2,256,512]{2,1,0:T(8,128)(2,1)}, u32[]{:S(2)}) copy-start(bf16[2,256,512]{2,1,0:T(8,128)(2,1)} %own.1) | copy-start | bytes 1572868
  1.1 1.2 %copy-start.3 = (bf16[8,2,256,128]{3,2,1,0:T(8,128)(2,1)S(1)}, bf16[8,2,256,128]{3,2,1,0:T(8,128)(2,1)}, u32[]{:S(2)}) copy-start(bf16[8,2,256,128]{3,2,1,0:T(8,128)(2,1)} %basis.5) | copy-start | bytes 3145732
  3.4 11.3 %collective-permute-start = (f32[9,128,256]{2,1,0:T(8,128)S(1)}, f32[9,128,256]{2,1,0:T(8,128)S(1)}, u32[]{:S(2)}, u32[]{:S(2)}) collective-permute-start(f32[9,128,256]{2,1,0:T(8,128)S(1)} %shard_map.56), channel_id=1, source_target_pairs={{0,1},{1,0},{2,3},{3,2},{4,5},{5,4},{6,7},{7,6},{8,9},{9,8},{10,11... | collective-permute-start | bytes 3538952 | tf_op jit(solution)/shard_map/ppermute | solution.py:182
  13.2 8.0 %copy-start.1 = (bf16[2,256,512]{2,1,0:T(8,128)(2,1)S(1)}, bf16[2,256,512]{2,1,0:T(8,128)(2,1)}, u32[]{:S(2)}) copy-start(bf16[2,256,512]{2,1,0:T(8,128)(2,1)} %own.1) | copy-start | bytes 1572868
  15.5 20.4 %all-to-all-start = ((bf16[16,112,128]{2,1,0:T(8,128)(2,1)}), bf16[16,112,128]{2,1,0:T(8,128)(2,1)S(1)}, u32[]{:S(2)}, u32[]{:S(2)}) async-start(bf16[16,112,128]{2,1,0:T(8,128)(2,1)} %bitcast.4), calls=%async_computation | async-start | bytes 917504 | tf_op jit(solution)/shard_map/all_to_all | solution.py:215
  21.2 6.1 %collective-permute-start.2 = (bf16[2,256,512]{2,1,0:T(8,128)(2,1)S(1)}, bf16[2,256,512]{2,1,0:T(8,128)(2,1)S(1)}, u32[]{:S(2)}, u32[]{:S(2)}) collective-permute-start(bf16[2,256,512]{2,1,0:T(8,128)(2,1)S(1)} %copy-done.1), channel_id=1, source_target_pairs={{0,1},{1,0},{2,3},{3,2},{4,5},{5,4},{6,7},{7,6},{8,9},{9,8},{10,11... | collective-permute-start | bytes 1572872 | tf_op jit(solution)/shard_map/ppermute | solution.py:182
  23.8 9.2 %collective-permute-start.1 = (bf16[2,128,256]{2,1,0:T(8,128)(2,1)S(1)}, bf16[2,128,256]{2,1,0:T(8,128)(2,1)S(1)}, u32[]{:S(2)}, u32[]{:S(2)}) collective-permute-start(bf16[2,128,256]{2,1,0:T(8,128)(2,1)S(1)} %get-tuple-element.10.finest), channel_id=1, source_target_pairs={{0,2},{2,0},{1,3},{3,1},{4,6},{6,4},{5,7},{7,5},{8,10},{10,8},{9,1... | collective-permute-start | bytes 393224 | tf_op jit(solution)/shard_map/ppermute | solution.py:182
  37.2 19.1 %all-to-all-start.1 = ((f32[16,16,128]{2,1,0:T(8,128)}), f32[16,16,128]{2,1,0:T(8,128)S(1)}, u32[]{:S(2)}, u32[]{:S(2)}) async-start(f32[16,16,128]{2,1,0:T(8,128)} %bitcast.6), calls=%async_computation.1 | async-start | bytes 262144 | tf_op jit(solution)/shard_map/all_to_all | solution.py:215
  46.3 17.2 %collective-permute-start.3 = (bf16[2,256,512]{2,1,0:T(8,128)(2,1)S(1)}, bf16[2,256,512]{2,1,0:T(8,128)(2,1)S(1)}, u32[]{:S(2)}, u32[]{:S(2)}) collective-permute-start(bf16[2,256,512]{2,1,0:T(8,128)(2,1)S(1)} %get-tuple-element.12), channel_id=1, source_target_pairs={{0,2},{2,0},{1,3},{3,1},{4,6},{6,4},{5,7},{7,5},{8,10},{10,8},{9,1... | collective-permute-start | bytes 1572872 | tf_op jit(solution)/shard_map/ppermute | solution.py:182
  57.6 18.6 %copy-start.5 = (s32[510]{0:T(512)S(1)}, s32[510]{0:T(512)}, u32[]{:S(2)}) copy-start(s32[510]{0:T(512)} %ranks.1) | copy-start | bytes 6124
  57.6 18.5 %all-to-all-start.2 = ((bf16[16,112,128]{2,1,0:T(8,128)(2,1)}), bf16[16,112,128]{2,1,0:T(8,128)(2,1)S(1)}, u32[]{:S(2)}, u32[]{:S(2)}) async-start(bf16[16,112,128]{2,1,0:T(8,128)(2,1)} %bitcast.8), calls=%async_computation.2 | async-start | bytes 917504 | tf_op jit(solution)/shard_map/all_to_all | solution.py:215
  63.5 5.8 %collective-permute-start.4 = (bf16[2,256,512]{2,1,0:T(8,128)(2,1)S(1)}, bf16[2,256,512]{2,1,0:T(8,128)(2,1)S(1)}, u32[]{:S(2)}, u32[]{:S(2)}) collective-permute-start(bf16[2,256,512]{2,1,0:T(8,128)(2,1)S(1)} %collective-permute-done.3.by_chip), channel_id=1, source_target_pairs={{0,1},{1,0},{2,3},{3,2},{4,5},{5,4},{6,7},{7,6},{8,9},{9,8},{10,11... | collective-permute-start | bytes 1572872 | tf_op jit(solution)/shard_map/ppermute | solution.py:182
  69.3 1.2 %copy-start.4 = (bf16[2,256,1024]{2,1,0:T(8,128)(2,1)S(1)}, bf16[2,256,1024]{2,1,0:T(8,128)(2,1)}, u32[]{:S(2)}) copy-start(bf16[2,256,1024]{2,1,0:T(8,128)(2,1)} %blocks.1) | copy-start | bytes 3145732
  76.2 6.9 %copy-start.2 = (bf16[8,2,256,128]{3,2,1,0:T(8,128)(2,1)S(1)}, bf16[8,2,256,128]{3,2,1,0:T(8,128)(2,1)}, u32[]{:S(2)}) copy-start(bf16[8,2,256,128]{3,2,1,0:T(8,128)(2,1)} %basis.7) | copy-start | bytes 3145732
  76.9 7.8 %collective-permute-start.5 = (bf16[1152,256]{1,0:T(8,128)(2,1)S(1)}, bf16[1152,256]{1,0:T(8,128)(2,1)S(1)}, u32[]{:S(2)}, u32[]{:S(2)}) collective-permute-start(bf16[1152,256]{1,0:T(8,128)(2,1)S(1)} %shard_map.62.coef), channel_id=1, source_target_pairs={{0,1},{1,0},{2,3},{3,2},{4,5},{5,4},{6,7},{7,6},{8,9},{9,8},{10,11... | collective-permute-start | bytes 1769480 | tf_op jit(solution)/shard_map/ppermute | solution.py:182

commit v3 on v2

--- a/solution.py
+++ b/solution.py
@@ -1,5 +1,3 @@
-import functools
-
 import jax
 import jax.numpy as jnp
 from jax import lax
@@ -8,19 +6,23 @@
 from jax.sharding import Mesh, PartitionSpec as P
 
 VMEM_BYTES = 48 * 1024 * 1024
+LONG = 10**10
 F32 = jnp.float32
 BF16 = jnp.bfloat16
 
 
-def call(kernel, out_shape, in_specs, scratch=(), flops=0, moved=0):
+def call(
+    kernel, out_shape, in_specs, scratch=(), flops=0, moved=0, whole=None, aliases=None
+):
     many = isinstance(out_shape, (list, tuple))
-    whole = pl.BlockSpec(memory_space=pltpu.VMEM)
+    whole = whole or VMEM
     return pl.pallas_call(
         kernel,
         out_shape=out_shape,
         in_specs=in_specs,
         out_specs=[whole] * len(out_shape) if many else whole,
         scratch_shapes=list(scratch),
+        input_output_aliases=aliases or {},
         compiler_params=pltpu.CompilerParams(vmem_limit_bytes=VMEM_BYTES),
         cost_estimate=pl.CostEstimate(flops=flops, bytes_accessed=moved, transcendentals=0),
     )
@@ -31,38 +33,42 @@
 ANY = pl.BlockSpec(memory_space=pl.ANY)
 
 
-def project_kernel(other, place, basis, sides, out):
+def projections(place, basis, sides):
     levels, leaves, rows, rank = basis.shape
     half = sides.shape[2] // 2
-    core = place[1]
-    column = pl.multiple_of((1 - core if other else core) * half, half)
-    both = sides[:, :, pl.ds(column, half)]
+    both = sides[:, :, pl.ds(pl.multiple_of(place[1] * half, half), half)]
     contract = (((0,), (0,)), ((), ()))
     for level in range(levels - 1):
-        out[level] = lax.dot_general(
+        yield lax.dot_general(
             basis[level].reshape(leaves * rows, rank),
             both.reshape(leaves * rows, half),
             contract,
             preferred_element_type=F32,
         )
     for leaf in range(leaves):
-        out[levels - 1 + leaf] = lax.dot_general(
+        yield lax.dot_general(
             basis[levels - 1, leaf], both[leaf], contract, preferred_element_type=F32
         )
 
 
-def combine_kernel(mine, theirs, tiles, finest):
+def mine_kernel(place, basis, sides, out):
+    for slot, value in enumerate(projections(place, basis, sides)):
+        out[slot] = value
+
+
+def theirs_kernel(place, basis, sides, mine, tiles, finest):
     down, upper, across = tiles.shape[:3]
-    for level in range(upper):
-        total = mine[level] + theirs[level]
+    for slot, value in enumerate(projections(place, basis, sides)):
+        total = mine[slot] + value
+        if slot >= upper:
+            finest[slot - upper] = total.astype(BF16)
+            continue
         for col in range(across):
             part = total[:, col * 128 : (col + 1) * 128]
-            tiles[:, level, col] = part.reshape(down, 8, 128).astype(BF16)
-    finest[...] = (mine[upper:] + theirs[upper:]).astype(BF16)
-
-
-def ring_kernel(place, parts, *rest):
-    out = rest[-1]
+            tiles[:, slot, col] = part.reshape(down, 8, 128).astype(BF16)
+
+
+def ring_kernel(place, parts, out):
     high = place[3]
     bits = out.shape[0].bit_length() - 1
     total = [None] * bits
@@ -75,8 +81,9 @@
         out[jnp.bitwise_xor(high, step)] = total[bits - step.bit_length()]
 
 
-def low_kernel(parts, sides, out, sides_out):
+def low_kernel(parts, sides, finest, out, sides_out, finest_out):
     sides_out[...] = sides[...]
+    finest_out[...] = finest[...]
     count, low = out.shape[:2]
     first = parts.shape[1] - low
     for level in range(low):
@@ -91,7 +98,7 @@
             out[z, level] = sums[(z >> distance) ^ 1].astype(BF16)
 
 
-def back_kernel(place, high_parts, low, out):
+def back_kernel(place, high_parts, low, finest_chip, out):
     high = place[3]
     steps = high_parts.shape[0]
     bits = steps.bit_length() - 1
@@ -156,26 +163,32 @@
         store(leaf, (dense[leaf, :, pl.ds(column, half)] + term).astype(BF16))
 
 
-def own_kernel(place, coef, basis, dense, out):
-    half = out.shape[2]
-    column = pl.multiple_of(place[1] * half, half)
+def own_kernel(place, coef, basis, dense, out, held, sems):
+    half = held.shape[2]
+    place_half(place[1], coef, basis, dense, out, held, sems, half)
+
+
+def last_kernel(place, coef, basis, dense, begun, out, held, sems):
+    half = held.shape[2]
+    place_half(1 - place[1], coef, basis, dense, out, held, sems, half)
+
+
+def place_half(index, coef, basis, dense, out, held, sems, half):
+    column = pl.multiple_of(index * half, half)
+    copies = []
 
     def store(leaf, value):
-        out[leaf] = value
+        held[leaf] = value
+        copies.append(
+            pltpu.make_async_copy(
+                held.at[leaf], out.at[leaf, :, pl.ds(column, half)], sems.at[leaf]
+            )
+        )
+        copies[-1].start()
 
     update(coef, basis, dense, column, store)
-
-
-def last_kernel(place, coef, basis, dense, ready, out):
-    half = ready.shape[2]
-    mine = pl.multiple_of(place[1] * half, half)
-    column = pl.multiple_of((1 - place[1]) * half, half)
-    out[:, :, pl.ds(mine, half)] = ready[...]
-
-    def store(leaf, value):
-        out[leaf, :, pl.ds(column, half)] = value
-
-    update(coef, basis, dense, column, store)
+    for copy in copies:
+        copy.wait()
 
 
 def swap(block, axis):
@@ -201,46 +214,45 @@
     tile = (half // 128, 8, 128)
     flops = 2 * levels * leaves * rows * rank * half
 
-    def project(other):
-        return call(
-            functools.partial(project_kernel, other),
-            shape((slots, rank, half), F32),
-            [SMEM, VMEM, VMEM],
-            flops=flops,
-            moved=2 * (basis_right.size + right_sides.size) + 4 * slots * rank * half,
-        )(place, basis_right, right_sides)
-
     def exchange(block, axes):
         flat = block.reshape((block.shape[0], -1, 128))
         moved = lax.all_to_all(flat, axes, split_axis=0, concat_axis=0, tiled=True)
         return moved.reshape(block.shape)
 
-    sent = project(True)
-    theirs = swap(sent, "core")
-    mine = project(False)
+    basis_core = swap(basis_right, "core")
+    by_core = swap(right_sides, "core")
+    moved = 2 * (basis_right.size + right_sides.size) + 4 * slots * rank * half
+    mine = call(
+        mine_kernel,
+        shape((slots, rank, half), F32),
+        [SMEM, VMEM, VMEM],
+        flops=flops,
+        moved=moved,
+    )(place, basis_right, right_sides)
     tiles, finest = call(
-        combine_kernel,
+        theirs_kernel,
         [shape((owners, upper) + tile, BF16), shape((leaves, rank, half), BF16)],
-        [VMEM, VMEM],
-        moved=10 * slots * rank * half,
-    )(mine, theirs)
+        [SMEM, VMEM, VMEM, VMEM],
+        flops=flops,
+        moved=2 * moved,
+    )(place, basis_core, by_core, mine)
     parts = exchange(tiles, ("z", "chip"))
-    by_core = swap(right_sides, "core")
-    finest_chip = swap(finest, "chip")
     to_high = call(
-        ring_kernel,
-        shape((highs,) + tile, F32),
-        [SMEM, VMEM, ANY, ANY],
-        moved=2 * parts.size,
-    )(place, parts, finest_chip, by_core)
-    low, sides_late = call(
+        ring_kernel, shape((highs,) + tile, F32), [SMEM, VMEM], moved=2 * parts.size
+    )(place, parts)
+    low, sides_late, finest_late = call(
         low_kernel,
-        [shape((ring, low_levels) + tile, BF16), shape(right_sides.shape, BF16)],
-        [VMEM, VMEM],
+        [
+            shape((ring, low_levels) + tile, BF16),
+            shape(right_sides.shape, BF16),
+            shape(finest.shape, BF16),
+        ],
+        [VMEM, VMEM, VMEM],
         moved=2 * parts.size + 4 * right_sides.size,
-    )(parts, right_sides)
+    )(parts, right_sides, finest)
     from_high = exchange(to_high, ("high",))
     by_chip = swap(sides_late, "chip")
+    finest_chip = swap(finest_late, "chip")
     by_both = swap(by_chip, "core")
     dense = call(
         dense_kernel,
@@ -252,9 +264,10 @@
     coefs = call(
         back_kernel,
         shape(tiles.shape, BF16),
-        [SMEM, VMEM, VMEM],
+        [SMEM, VMEM, VMEM, VMEM],
+        flops=LONG,
         moved=4 * parts.size,
-    )(place, from_high, low)
+    )(place, from_high, low, finest_chip)
     coefs = exchange(coefs, ("z", "chip"))
     coef = call(
         gather_kernel,
@@ -263,21 +276,27 @@
         moved=4 * slots * rank * half,
     )(place, block_ranks, coefs, finest, finest_chip, dense)
     coef_other = swap(coef, "core")
+    held = [pltpu.VMEM((leaves, rows, half), BF16), pltpu.SemaphoreType.DMA((leaves,))]
     moved = 2 * (basis_left.size + coef.size) + 4 * right_sides.size
-    ready = call(
+    begun = call(
         own_kernel,
-        shape((leaves, rows, half), BF16),
+        shape((leaves, rows, width), BF16),
         [SMEM] + [VMEM] * 3,
+        scratch=held,
+        whole=ANY,
         flops=flops,
         moved=moved,
     )(place, coef, basis_left, dense)
     return call(
         last_kernel,
         shape((leaves, rows, width), BF16),
-        [SMEM] + [VMEM] * 4,
+        [SMEM] + [VMEM] * 3 + [ANY],
+        scratch=held,
+        whole=ANY,
+        aliases={4: 0},
         flops=flops,
         moved=moved,
-    )(place, coef_other, basis_left, dense, ready)
+    )(place, coef_other, basis_left, dense, begun)
 
 
 def solution(mesh):

time: 87.1 us -> 85.4 us (0.980)
  blocking collectives: 0 us -> 20.1 us
  waiting for transfers between devices: 24.5 us -> 9.6 us
  starting transfers between devices: 47.9 us -> 41.1 us
    all_to_all x0 -> x1, blocking collectives: none -> 20.1 us  [exchange(): moved = lax.all_to_all(flat, axes, split_axis=0, concat_axis=0, tiled=True)]
    all_to_all x3 -> x2, waiting for transfers between devices: 15.3 us -> 5.89 us  [exchange(): moved = lax.all_to_all(flat, axes, split_axis=0, concat_axis=0, tiled=True)]
    all_to_all x3 -> x2, starting transfers between devices: 20.7 us -> 13.8 us  [exchange(): moved = lax.all_to_all(flat, axes, split_axis=0, concat_axis=0, tiled=True)]
    ppermute x6, waiting for transfers between devices: 9.21 us -> 3.71 us  [swap(): return lax.ppermute(block, axis, [(0, 1), (1, 0)])]
    pallas_call x7 -> x6, Pallas kernels: 8.28 us -> 8.08 us  [the longest x1 1.7 us: local(): call(last_kernel, shape((leaves, rows, width), BF16), [SMEM] + [VMEM] * 3...]
  transfers between devices with their start and end apart: 9 -> 8, of which waited for: 7 -> 5; matrix products, arithmetic and copies ran while one was open for 0% -> 0% of each run, Pallas kernels for 5% -> 6%
where the time goes in v3:
time: 85.4 us; the launch traced here: 84.8 us
  starting transfers between devices  41.1 us (48%)
  blocking collectives  20.1 us (24%)
  Pallas kernels  10.1 us (12%)
  waiting for transfers between devices  9.6 us (11%)
  local copies, waits for them, and re-layouts  3.51 us (4%)
    ppermute x6, starting transfers between devices, swap(): return lax.ppermute(block, axis, [(0, 1), (1, 0)])  27.3 us
    all_to_all x1, blocking collectives, exchange(): moved = lax.all_to_all(flat, axes, split_axis=0, concat_axis=0, tiled=True)  20.1 us
    all_to_all x2, starting transfers between devices, exchange(): moved = lax.all_to_all(flat, axes, split_axis=0, concat_axis=0, tiled=True)  13.8 us
    all_to_all x2, waiting for transfers between devices, exchange(): moved = lax.all_to_all(flat, axes, split_axis=0, concat_axis=0, tiled=True)  5.89 us
    ppermute x6, waiting for transfers between devices, swap(): return lax.ppermute(block, axis, [(0, 1), (1, 0)])  3.71 us
    unnamed x12, local copies, waits for them, and re-layouts  3.51 us
  transfers between devices with their start and end apart: 8, of which 5 were waited for; matrix products, arithmetic and copies ran while one was open for 0% of the time, Pallas kernels for 6%

profile of v3, /device:TPU:1, one launch (start us, length us, event | category | flops | bytes accessed | tf_op | source)
XLA Modules:
  0.0 84.8 jit_solution(17249546045871995706)
XLA Ops:
  0.0 8.8 %collective-permute-start = (bf16[8,2,256,128]{3,2,1,0:T(8,128)(2,1)}, bf16[8,2,256,128]{3,2,1,0:T(8,128)(2,1)S(1)}, u32[]{:S(2)}, u32[]{:S(2)}) collective-permute-start(bf16[8,2,256,128]{3,2,1,0:T(8,128)(2,1)} %basis.3), channel_id=1, source_target_pairs={{0,1},{1,0},{2,3},{3,2},{4,5},{5,4},{6,7},{7,6},{8,9},{9,8},{10,11... | collective-permute-start | bytes 3145736 | tf_op jit(solution)/shard_map/ppermute | solution.py:195
  8.8 1.9 %collective-permute-start.1 = (bf16[2,256,512]{2,1,0:T(8,128)(2,1)}, bf16[2,256,512]{2,1,0:T(8,128)(2,1)S(1)}, u32[]{:S(2)}, u32[]{:S(2)}) collective-permute-start(bf16[2,256,512]{2,1,0:T(8,128)(2,1)} %own.1), channel_id=1, source_target_pairs={{0,1},{1,0},{2,3},{3,2},{4,5},{5,4},{6,7},{7,6},{8,9},{9,8},{10,11... | collective-permute-start | bytes 1572872 | tf_op jit(solution)/shard_map/ppermute | solution.py:195
  10.7 0.1 pad_add_fusion.place
  10.8 0.0 copy-start
  10.8 1.0 %copy-done = bf16[2,256,512]{2,1,0:T(8,128)(2,1)S(1)} copy-done((bf16[2,256,512]{2,1,0:T(8,128)(2,1)S(1)}, bf16[2,256,512]{2,1,0:T(8,128)(2,1)}, u32[]{:S(2)}) %copy-start) | copy-done | bytes 524312
  11.8 0.0 copy-start.4
  11.8 1.2 %copy-done.4 = bf16[8,2,256,128]{3,2,1,0:T(8,128)(2,1)S(1)} copy-done((bf16[8,2,256,128]{3,2,1,0:T(8,128)(2,1)S(1)}, bf16[8,2,256,128]{3,2,1,0:T(8,128)(2,1)}, u32[]{:S(2)}) %copy-start.4) | copy-done | bytes 1048600
  13.1 1.0 %shard_map.55.mine = f32[9,128,256]{2,1,0:T(8,128)S(1)} custom-call(s32[4]{0:T(128)S(1)} %pad_add_fusion.place, bf16[8,2,256,128]{3,2,1,0:T(8,128)(2,1)S(1)} %copy-done.4, bf16[2,256,512]{2,1,0:T(8,128)(2,1)S(1)} %copy-done), custom_call_target="tpu_custom_call" | custom-call | flops 268435456 | bytes 2752512 | tf_op jit(solution)/shard_map/pallas_call | solution.py:225
  14.1 0.0 collective-permute-done.1.sides.by_core
  14.1 0.0 collective-permute-done.basis
  14.1 1.1 %shard_map.56 = (bf16[16,7,2,8,128]{4,3,2,1,0:T(8,128)(2,1)S(1)}, bf16[2,128,256]{2,1,0:T(8,128)(2,1)S(1)}) custom-call(s32[4]{0:T(128)S(1)} %pad_add_fusion.place, bf16[8,2,256,128]{3,2,1,0:T(8,128)(2,1)S(1)} %collective-permute-done.basis, bf16[2,256,512]{2,1,0:T(8,128)(2,1)S(1)} %collective-permute-done.1.sides.by_core, f32[9,128,256]{2,1,0:T(8,128)S(1)} %shard_map.55.mine), custom_call_target="tpu_custom_call" | custom-call | flops 268435456 | bytes 5505024 | tf_op jit(solution)/shard_map/pallas_call | solution.py:232
  15.2 0.0 copy-start.1
  15.2 20.1 %all_to_all.15 = bf16[16,112,128]{2,1,0:T(8,128)(2,1)S(1)} all-to-all(bf16[16,112,128]{2,1,0:T(8,128)(2,1)S(1)} %bitcast.13), channel_id=1, replica_groups=mesh['high'=16,'z'=8,'chip'=2,'core'=2] {'z','chip'}, dimensions={0} | all-to-all | bytes 917504 | tf_op jit(solution)/shard_map/all_to_all | solution.py:219
  35.4 1.2 %shard_map.57 = f32[16,2,8,128]{3,2,1,0:T(8,128)} custom-call(s32[4]{0:T(128)S(1)} %pad_add_fusion.place, bf16[16,7,2,8,128]{4,3,2,1,0:T(8,128)(2,1)S(1)} %bitcast.10), custom_call_target="tpu_custom_call" | custom-call | bytes 458752 | tf_op jit(solution)/shard_map/pallas_call | solution.py:240
  36.6 9.1 %all-to-all-start.1 = ((f32[16,16,128]{2,1,0:T(8,128)}), f32[16,16,128]{2,1,0:T(8,128)S(1)}, u32[]{:S(2)}, u32[]{:S(2)}) async-start(f32[16,16,128]{2,1,0:T(8,128)} %bitcast.6), calls=%async_computation.1 | async-start | bytes 262144 | tf_op jit(solution)/shard_map/all_to_all | solution.py:219
  45.7 0.0 copy-done.1
  45.7 0.1 shard_map.58
  45.8 1.9 %collective-permute-start.2 = (bf16[2,128,256]{2,1,0:T(8,128)(2,1)S(1)}, bf16[2,128,256]{2,1,0:T(8,128)(2,1)S(1)}, u32[]{:S(2)}, u32[]{:S(2)}) collective-permute-start(bf16[2,128,256]{2,1,0:T(8,128)(2,1)S(1)} %get-tuple-element.13), channel_id=1, source_target_pairs={{0,2},{2,0},{1,3},{3,1},{4,6},{6,4},{5,7},{7,5},{8,10},{10,8},{9,1... | collective-permute-start | bytes 393224 | tf_op jit(solution)/shard_map/ppermute | solution.py:195
  47.7 3.4 %collective-permute-start.3 = (bf16[2,256,512]{2,1,0:T(8,128)(2,1)S(1)}, bf16[2,256,512]{2,1,0:T(8,128)(2,1)S(1)}, u32[]{:S(2)}, u32[]{:S(2)}) collective-permute-start(bf16[2,256,512]{2,1,0:T(8,128)(2,1)S(1)} %get-tuple-element.14), channel_id=1, source_target_pairs={{0,2},{2,0},{1,3},{3,1},{4,6},{6,4},{5,7},{7,5},{8,10},{10,8},{9,1... | collective-permute-start | bytes 1572872 | tf_op jit(solution)/shard_map/ppermute | solution.py:195
  51.1 0.9 %collective-permute-done.2.finest_chip = bf16[2,128,256]{2,1,0:T(8,128)(2,1)S(1)} collective-permute-done((bf16[2,128,256]{2,1,0:T(8,128)(2,1)S(1)}, bf16[2,128,256]{2,1,0:T(8,128)(2,1)S(1)}, u32[]{:S(2)}, u32[]{:S(2)}) %collective-permute-start.2) | collective-permute-done | bytes 131104 | tf_op jit(solution)/shard_map/ppermute | solution.py:195
  52.0 3.7 %all-to-all-done.1 = f32[16,16,128]{2,1,0:T(8,128)S(1)} async-done(((f32[16,16,128]{2,1,0:T(8,128)}), f32[16,16,128]{2,1,0:T(8,128)S(1)}, u32[]{:S(2)}, u32[]{:S(2)}) %all-to-all-start.1) | async-done | bytes 131104 | tf_op jit(solution)/shard_map/all_to_all | solution.py:219
  55.7 1.4 %shard_map.59 = bf16[16,7,2,8,128]{4,3,2,1,0:T(8,128)(2,1)} custom-call(s32[4]{0:T(128)S(1)} %pad_add_fusion.place, f32[16,2,8,128]{3,2,1,0:T(8,128)S(1)} %bitcast.14, bf16[8,3,2,8,128]{4,3,2,1,0:T(8,128)(2,1)S(1)} %get-tuple-element.12.low, bf16[2,128,256]{2,1,0:T(8,128)(2,1)S(1)} %collective-permute-done.2.finest_chip), custom_call_target="tpu_custom_call" | custom-call | flops 10000000000 | bytes 917504 | tf_op jit(solution)/shard_map/pallas_call | solution.py:264
  57.0 0.0 copy-start.5
  57.0 4.7 %all-to-all-start.2 = ((bf16[16,112,128]{2,1,0:T(8,128)(2,1)}), bf16[16,112,128]{2,1,0:T(8,128)(2,1)S(1)}, u32[]{:S(2)}, u32[]{:S(2)}) async-start(bf16[16,112,128]{2,1,0:T(8,128)(2,1)} %bitcast.8), calls=%async_computation.2 | async-start | bytes 917504 | tf_op jit(solution)/shard_map/all_to_all | solution.py:219
  61.8 1.3 %collective-permute-done.3.by_chip = bf16[2,256,512]{2,1,0:T(8,128)(2,1)S(1)} collective-permute-done((bf16[2,256,512]{2,1,0:T(8,128)(2,1)S(1)}, bf16[2,256,512]{2,1,0:T(8,128)(2,1)S(1)}, u32[]{:S(2)}, u32[]{:S(2)}) %collective-permute-start.3) | collective-permute-done | bytes 524320 | tf_op jit(solution)/shard_map/ppermute | solution.py:195
  63.1 4.9 %collective-permute-start.4 = (bf16[2,256,512]{2,1,0:T(8,128)(2,1)S(1)}, bf16[2,256,512]{2,1,0:T(8,128)(2,1)S(1)}, u32[]{:S(2)}, u32[]{:S(2)}) collective-permute-start(bf16[2,256,512]{2,1,0:T(8,128)(2,1)S(1)} %collective-permute-done.3.by_chip), channel_id=1, source_target_pairs={{0,1},{1,0},{2,3},{3,2},{4,5},{5,4},{6,7},{7,6},{8,9},{9,8},{10,11... | collective-permute-start | bytes 1572872 | tf_op jit(solution)/shard_map/ppermute | solution.py:195
  68.0 1.5 %collective-permute-done.4.by_both = bf16[2,256,512]{2,1,0:T(8,128)(2,1)S(1)} collective-permute-done((bf16[2,256,512]{2,1,0:T(8,128)(2,1)S(1)}, bf16[2,256,512]{2,1,0:T(8,128)(2,1)S(1)}, u32[]{:S(2)}, u32[]{:S(2)}) %collective-permute-start.4) | collective-permute-done | bytes 524320 | tf_op jit(solution)/shard_map/ppermute | solution.py:195
  69.5 0.0 copy-start.3
  69.5 1.2 %copy-done.3 = bf16[2,256,1024]{2,1,0:T(8,128)(2,1)S(1)} copy-done((bf16[2,256,1024]{2,1,0:T(8,128)(2,1)S(1)}, bf16[2,256,1024]{2,1,0:T(8,128)(2,1)}, u32[]{:S(2)}) %copy-start.3) | copy-done | bytes 1048600
  70.8 1.3 %shard_map.60.dense = f32[2,256,512]{2,1,0:T(8,128)S(1)} custom-call(s32[4]{0:T(128)S(1)} %pad_add_fusion.place, bf16[2,256,1024]{2,1,0:T(8,128)(2,1)S(1)} %copy-done.3, bf16[2,256,512]{2,1,0:T(8,128)(2,1)S(1)} %copy-done.1, bf16[2,256,512]{2,1,0:T(8,128)(2,1)S(1)} %collective-permute-done.1.sides.by_core, ...), custom_call_target="tpu_custom_call" | custom-call | flops 536870912 | bytes 4194304 | tf_op jit(solution)/shard_map/pallas_call | solution.py:257
  72.0 2.2 %all-to-all-done.2 = bf16[16,112,128]{2,1,0:T(8,128)(2,1)S(1)} async-done(((bf16[16,112,128]{2,1,0:T(8,128)(2,1)}), bf16[16,112,128]{2,1,0:T(8,128)(2,1)S(1)}, u32[]{:S(2)}, u32[]{:S(2)}) %all-to-all-start.2) | async-done | bytes 458784 | tf_op jit(solution)/shard_map/all_to_all | solution.py:219
  74.2 0.0 copy-done.5
  74.2 0.0 copy-start.2
  74.2 0.7 shard_map.61.coef
  74.9 6.4 %collective-permute-start.5 = (bf16[1152,256]{1,0:T(8,128)(2,1)S(1)}, bf16[1152,256]{1,0:T(8,128)(2,1)S(1)}, u32[]{:S(2)}, u32[]{:S(2)}) collective-permute-start(bf16[1152,256]{1,0:T(8,128)(2,1)S(1)} %shard_map.61.coef), channel_id=1, source_target_pairs={{0,1},{1,0},{2,3},{3,2},{4,5},{5,4},{6,7},{7,6},{8,9},{9,8},{10,11... | collective-permute-start | bytes 1769480 | tf_op jit(solution)/shard_map/ppermute | solution.py:195
  81.3 0.0 copy-done.2
  81.4 1.7 %shard_map.62.begun = bf16[2,256,512]{2,1,0:T(8,128)(2,1)} custom-call(s32[4]{0:T(128)S(1)} %pad_add_fusion.place, bf16[1152,256]{1,0:T(8,128)(2,1)S(1)} %shard_map.61.coef, bf16[8,2,256,128]{3,2,1,0:T(8,128)(2,1)S(1)} %copy-done.2, f32[2,256,512]{2,1,0:T(8,128)S(1)} %shard_map.60.dense), custom_call_target="tpu_custom_call" | custom-call | flops 268435456 | bytes 2686976 | tf_op jit(solution)/shard_map/pallas_call | solution.py:281
  83.1 0.0 collective-permute-done.5.coef
  83.1 1.7 %shard_map.63 = bf16[2,256,512]{2,1,0:T(8,128)(2,1)} custom-call(s32[4]{0:T(128)S(1)} %pad_add_fusion.place, bf16[1152,256]{1,0:T(8,128)(2,1)S(1)} %collective-permute-done.5.coef, bf16[8,2,256,128]{3,2,1,0:T(8,128)(2,1)S(1)} %copy-done.2, f32[2,256,512]{2,1,0:T(8,128)S(1)} %shard_map.60.dense, ...), custom_call_target="tpu_custom_call", output_to_operand_aliasing={{}: (4, {})} | custom-call | flops 268435456 | bytes 2686976 | tf_op jit(solution)/shard_map/pallas_call | solution.py:290
Async XLA Ops:
  0.0 14.1 %collective-permute-start = (bf16[8,2,256,128]{3,2,1,0:T(8,128)(2,1)}, bf16[8,2,256,128]{3,2,1,0:T(8,128)(2,1)S(1)}, u32[]{:S(2)}, u32[]{:S(2)}) collective-permute-start(bf16[8,2,256,128]{3,2,1,0:T(8,128)(2,1)} %basis.3), channel_id=1, source_target_pairs={{0,1},{1,0},{2,3},{3,2},{4,5},{5,4},{6,7},{7,6},{8,9},{9,8},{10,11... | collective-permute-start | bytes 3145736 | tf_op jit(solution)/shard_map/ppermute | solution.py:195
  8.8 5.3 %collective-permute-start.1 = (bf16[2,256,512]{2,1,0:T(8,128)(2,1)}, bf16[2,256,512]{2,1,0:T(8,128)(2,1)S(1)}, u32[]{:S(2)}, u32[]{:S(2)}) collective-permute-start(bf16[2,256,512]{2,1,0:T(8,128)(2,1)} %own.1), channel_id=1, source_target_pairs={{0,1},{1,0},{2,3},{3,2},{4,5},{5,4},{6,7},{7,6},{8,9},{9,8},{10,11... | collective-permute-start | bytes 1572872 | tf_op jit(solution)/shard_map/ppermute | solution.py:195
  10.8 1.0 %copy-start = (bf16[2,256,512]{2,1,0:T(8,128)(2,1)S(1)}, bf16[2,256,512]{2,1,0:T(8,128)(2,1)}, u32[]{:S(2)}) copy-start(bf16[2,256,512]{2,1,0:T(8,128)(2,1)} %own.1) | copy-start | bytes 1572868
  11.8 1.2 %copy-start.4 = (bf16[8,2,256,128]{3,2,1,0:T(8,128)(2,1)S(1)}, bf16[8,2,256,128]{3,2,1,0:T(8,128)(2,1)}, u32[]{:S(2)}) copy-start(bf16[8,2,256,128]{3,2,1,0:T(8,128)(2,1)} %basis.3) | copy-start | bytes 3145732
  15.2 30.5 %copy-start.1 = (bf16[2,256,512]{2,1,0:T(8,128)(2,1)S(1)}, bf16[2,256,512]{2,1,0:T(8,128)(2,1)}, u32[]{:S(2)}) copy-start(bf16[2,256,512]{2,1,0:T(8,128)(2,1)} %own.1) | copy-start | bytes 1572868
  36.6 19.1 %all-to-all-start.1 = ((f32[16,16,128]{2,1,0:T(8,128)}), f32[16,16,128]{2,1,0:T(8,128)S(1)}, u32[]{:S(2)}, u32[]{:S(2)}) async-start(f32[16,16,128]{2,1,0:T(8,128)} %bitcast.6), calls=%async_computation.1 | async-start | bytes 262144 | tf_op jit(solution)/shard_map/all_to_all | solution.py:219
  45.8 6.2 %collective-permute-start.2 = (bf16[2,128,256]{2,1,0:T(8,128)(2,1)S(1)}, bf16[2,128,256]{2,1,0:T(8,128)(2,1)S(1)}, u32[]{:S(2)}, u32[]{:S(2)}) collective-permute-start(bf16[2,128,256]{2,1,0:T(8,128)(2,1)S(1)} %get-tuple-element.13), channel_id=1, source_target_pairs={{0,2},{2,0},{1,3},{3,1},{4,6},{6,4},{5,7},{7,5},{8,10},{10,8},{9,1... | collective-permute-start | bytes 393224 | tf_op jit(solution)/shard_map/ppermute | solution.py:195
  47.7 15.3 %collective-permute-start.3 = (bf16[2,256,512]{2,1,0:T(8,128)(2,1)S(1)}, bf16[2,256,512]{2,1,0:T(8,128)(2,1)S(1)}, u32[]{:S(2)}, u32[]{:S(2)}) collective-permute-start(bf16[2,256,512]{2,1,0:T(8,128)(2,1)S(1)} %get-tuple-element.14), channel_id=1, source_target_pairs={{0,2},{2,0},{1,3},{3,1},{4,6},{6,4},{5,7},{7,5},{8,10},{10,8},{9,1... | collective-permute-start | bytes 1572872 | tf_op jit(solution)/shard_map/ppermute | solution.py:195
  57.0 17.1 %copy-start.5 = (s32[510]{0:T(512)S(1)}, s32[510]{0:T(512)}, u32[]{:S(2)}) copy-start(s32[510]{0:T(512)} %ranks.1) | copy-start | bytes 6124
  57.0 17.1 %all-to-all-start.2 = ((bf16[16,112,128]{2,1,0:T(8,128)(2,1)}), bf16[16,112,128]{2,1,0:T(8,128)(2,1)S(1)}, u32[]{:S(2)}, u32[]{:S(2)}) async-start(bf16[16,112,128]{2,1,0:T(8,128)(2,1)} %bitcast.8), calls=%async_computation.2 | async-start | bytes 917504 | tf_op jit(solution)/shard_map/all_to_all | solution.py:219
  63.1 6.5 %collective-permute-start.4 = (bf16[2,256,512]{2,1,0:T(8,128)(2,1)S(1)}, bf16[2,256,512]{2,1,0:T(8,128)(2,1)S(1)}, u32[]{:S(2)}, u32[]{:S(2)}) collective-permute-start(bf16[2,256,512]{2,1,0:T(8,128)(2,1)S(1)} %collective-permute-done.3.by_chip), channel_id=1, source_target_pairs={{0,1},{1,0},{2,3},{3,2},{4,5},{5,4},{6,7},{7,6},{8,9},{9,8},{10,11... | collective-permute-start | bytes 1572872 | tf_op jit(solution)/shard_map/ppermute | solution.py:195
  69.5 1.2 %copy-start.3 = (bf16[2,256,1024]{2,1,0:T(8,128)(2,1)S(1)}, bf16[2,256,1024]{2,1,0:T(8,128)(2,1)}, u32[]{:S(2)}) copy-start(bf16[2,256,1024]{2,1,0:T(8,128)(2,1)} %blocks.1) | copy-start | bytes 3145732
  74.2 7.2 %copy-start.2 = (bf16[8,2,256,128]{3,2,1,0:T(8,128)(2,1)S(1)}, bf16[8,2,256,128]{3,2,1,0:T(8,128)(2,1)}, u32[]{:S(2)}) copy-start(bf16[8,2,256,128]{3,2,1,0:T(8,128)(2,1)} %basis.5) | copy-start | bytes 3145732
  74.9 8.1 %collective-permute-start.5 = (bf16[1152,256]{1,0:T(8,128)(2,1)S(1)}, bf16[1152,256]{1,0:T(8,128)(2,1)S(1)}, u32[]{:S(2)}, u32[]{:S(2)}) collective-permute-start(bf16[1152,256]{1,0:T(8,128)(2,1)S(1)} %shard_map.61.coef), channel_id=1, source_target_pairs={{0,1},{1,0},{2,3},{3,2},{4,5},{5,4},{6,7},{7,6},{8,9},{9,8},{10,11... | collective-permute-start | bytes 1769480 | tf_op jit(solution)/shard_map/ppermute | solution.py:195

commit v4 on v3

--- a/solution.py
+++ b/solution.py
@@ -56,19 +56,20 @@
         out[slot] = value
 
 
-def theirs_kernel(place, basis, sides, mine, tiles, finest):
-    down, upper, across = tiles.shape[:3]
+def theirs_kernel(place, basis, sides, mine, wide, near):
+    down, wide_levels, across = wide.shape[:3]
     for slot, value in enumerate(projections(place, basis, sides)):
         total = mine[slot] + value
-        if slot >= upper:
-            finest[slot - upper] = total.astype(BF16)
+        if slot >= wide_levels:
+            near[slot - wide_levels] = total.astype(BF16)
             continue
         for col in range(across):
             part = total[:, col * 128 : (col + 1) * 128]
-            tiles[:, slot, col] = part.reshape(down, 8, 128).astype(BF16)
-
-
-def ring_kernel(place, parts, out):
+            wide[:, slot, col] = part.reshape(down, 8, 128).astype(BF16)
+
+
+def ring_kernel(place, parts, sides, out, sides_out):
+    sides_out[...] = sides[...]
     high = place[3]
     bits = out.shape[0].bit_length() - 1
     total = [None] * bits
@@ -81,37 +82,27 @@
         out[jnp.bitwise_xor(high, step)] = total[bits - step.bit_length()]
 
 
-def low_kernel(parts, sides, finest, out, sides_out, finest_out):
-    sides_out[...] = sides[...]
-    finest_out[...] = finest[...]
-    count, low = out.shape[:2]
-    first = parts.shape[1] - low
-    for level in range(low):
-        part = [
-            parts[2 * z, first + level].astype(F32) + parts[2 * z + 1, first + level].astype(F32)
-            for z in range(count)
-        ]
-        distance = low - 1 - level
-        size = 1 << distance
-        sums = [sum(part[g * size + 1 : (g + 1) * size], part[g * size]) for g in range(count // size)]
-        for z in range(count):
-            out[z, level] = sums[(z >> distance) ^ 1].astype(BF16)
-
-
-def back_kernel(place, high_parts, low, finest_chip, out):
+def back_kernel(place, high_parts, parts, near_7, out):
     high = place[3]
     steps = high_parts.shape[0]
     bits = steps.bit_length() - 1
+    members = out.shape[0]
     for level in range(bits):
         first = 1 << (bits - 1 - level)
         total = high_parts[jnp.bitwise_xor(high, first)]
         for step in range(first + 1, 2 * first):
             total = total + high_parts[jnp.bitwise_xor(high, step)]
         rounded = total.astype(BF16)
-        for member in range(out.shape[0]):
+        for member in range(members):
             out[member, level] = rounded
-    for member in range(out.shape[0]):
-        out[member, bits:] = low[member // 2]
+    for side in range(2):
+        first = (1 - side) * members // 2
+        total = parts[first, bits].astype(F32)
+        for member in range(first + 1, first + members // 2):
+            total = total + parts[member, bits].astype(F32)
+        rounded = total.astype(BF16)
+        for member in range(side * members // 2, (side + 1) * members // 2):
+            out[member, bits] = rounded
 
 
 def dense_kernel(place, blocks, own, by_core, by_chip, by_both, out):
@@ -128,27 +119,28 @@
         out[leaf] = total
 
 
-def gather_kernel(place, ranks, tiles, finest, finest_chip, dense, out):
-    rank = tiles.shape[0] * 8
-    upper, across = tiles.shape[1:3]
+def gather_kernel(place, ranks, wide, near_6, near_7, near, dense, out):
+    rank = wide.shape[0] * 8
+    wide_levels, across = wide.shape[1:3]
+    upper = wide_levels + 2
     position = place[0]
 
-    def keep(shape, heap):
-        return lax.broadcasted_iota(jnp.int32, shape, 0) < ranks[heap]
+    def put(row, column, value, heap):
+        kept = lax.broadcasted_iota(jnp.int32, value.shape, 0) < ranks[heap]
+        value = jnp.where(kept, value.astype(F32), 0.0).astype(BF16)
+        out[row : row + rank, column : column + value.shape[1]] = value
 
     for level in range(upper):
         heap = 2 ** (level + 1) - 2 + lax.shift_right_logical(position, upper - 1 - level)
-        for col in range(across):
-            part = tiles[:, level, col].astype(F32).reshape(rank, 128)
-            part = jnp.where(keep(part.shape, heap), part, 0.0)
-            row = (1 + level) * rank
-            out[row : row + rank, col * 128 : (col + 1) * 128] = part.astype(BF16)
+        row = (1 + level) * rank
+        if level < wide_levels:
+            for col in range(across):
+                put(row, col * 128, wide[:, level, col].astype(F32).reshape(rank, 128), heap)
+        else:
+            put(row, 0, near_6[...] if level == wide_levels else near_7[1], heap)
     for leaf in range(2):
         heap = 2 ** (upper + 1) - 2 + 2 * position + leaf
-        part = finest[1 - leaf].astype(F32) + finest_chip[1 - leaf].astype(F32)
-        part = jnp.where(keep(part.shape, heap), part, 0.0)
-        row = leaf * (1 + upper) * rank
-        out[row : row + rank, :] = part.astype(BF16)
+        put(leaf * (1 + upper) * rank, 0, near[3 - leaf], heap)
 
 
 def update(coef, basis, dense, column, store):
@@ -191,8 +183,8 @@
         copy.wait()
 
 
-def swap(block, axis):
-    return lax.ppermute(block, axis, [(0, 1), (1, 0)])
+def swap(block, axis, bit=1):
+    return lax.ppermute(block, axis, [(i, i ^ bit) for i in range(lax.axis_size(axis))])
 
 
 def local(right_sides, leaf_blocks, basis_left, basis_right, block_ranks):
@@ -202,7 +194,7 @@
     upper = levels - 1
     ring = lax.axis_size("z")
     highs = lax.axis_size("high")
-    low_levels = ring.bit_length() - 1
+    wide_levels = levels - 3
     owners = 2 * ring
     high = lax.axis_index("high")
     position = ring * high + lax.axis_index("z")
@@ -229,52 +221,50 @@
         flops=flops,
         moved=moved,
     )(place, basis_right, right_sides)
-    tiles, finest = call(
+    wide_shape = shape((owners, wide_levels) + tile, BF16)
+    near_shape = (slots - wide_levels, rank, half)
+    wide, near = call(
         theirs_kernel,
-        [shape((owners, upper) + tile, BF16), shape((leaves, rank, half), BF16)],
+        [wide_shape, shape(near_shape, BF16)],
         [SMEM, VMEM, VMEM, VMEM],
         flops=flops,
         moved=2 * moved,
     )(place, basis_core, by_core, mine)
-    parts = exchange(tiles, ("z", "chip"))
-    to_high = call(
-        ring_kernel, shape((highs,) + tile, F32), [SMEM, VMEM], moved=2 * parts.size
-    )(place, parts)
-    low, sides_late, finest_late = call(
-        low_kernel,
-        [
-            shape((ring, low_levels) + tile, BF16),
-            shape(right_sides.shape, BF16),
-            shape(finest.shape, BF16),
-        ],
-        [VMEM, VMEM, VMEM],
-        moved=2 * parts.size + 4 * right_sides.size,
-    )(parts, right_sides, finest)
+    wide = exchange(wide, ("z", "chip"))
+    near = (near.astype(F32) + swap(near, "chip").astype(F32)).astype(BF16)
+    near_7 = swap(near[:2], "z", 1)
+    near_6 = swap((near[0].astype(F32) + near_7[0].astype(F32)).astype(BF16), "z", 2)
+    to_high, sides_late = call(
+        ring_kernel,
+        [shape((highs,) + tile, F32), shape(right_sides.shape, BF16)],
+        [SMEM, VMEM, VMEM],
+        flops=LONG,
+        moved=2 * wide.size,
+    )(place, wide, right_sides)
     from_high = exchange(to_high, ("high",))
     by_chip = swap(sides_late, "chip")
-    finest_chip = swap(finest_late, "chip")
     by_both = swap(by_chip, "core")
+    wide = call(
+        back_kernel,
+        wide_shape,
+        [SMEM, VMEM, VMEM, VMEM],
+        flops=LONG,
+        moved=4 * wide.size,
+    )(place, from_high, wide, near_7)
+    wide = exchange(wide, ("z", "chip"))
     dense = call(
         dense_kernel,
         shape((leaves, rows, width), F32),
         [SMEM] + [VMEM] * 5,
         flops=2 * leaves * rows * leaf_blocks.shape[2] * width,
-        moved=2 * leaf_blocks.size + 8 * right_sides.size + 4 * right_sides.size,
+        moved=2 * leaf_blocks.size + 12 * right_sides.size,
     )(place, leaf_blocks, right_sides, by_core, by_chip, by_both)
-    coefs = call(
-        back_kernel,
-        shape(tiles.shape, BF16),
-        [SMEM, VMEM, VMEM, VMEM],
-        flops=LONG,
-        moved=4 * parts.size,
-    )(place, from_high, low, finest_chip)
-    coefs = exchange(coefs, ("z", "chip"))
     coef = call(
         gather_kernel,
         shape((slots * rank, half), BF16),
-        [SMEM, SMEM, VMEM, VMEM, VMEM, ANY],
+        [SMEM, SMEM] + [VMEM] * 4 + [ANY],
         moved=4 * slots * rank * half,
-    )(place, block_ranks, coefs, finest, finest_chip, dense)
+    )(place, block_ranks, wide, near_6, near_7, near, dense)
     coef_other = swap(coef, "core")
     held = [pltpu.VMEM((leaves, rows, half), BF16), pltpu.SemaphoreType.DMA((leaves,))]
     moved = 2 * (basis_left.size + coef.size) + 4 * right_sides.size

time: 85.4 us -> 81.9 us (0.959)
  blocking collectives: 20.1 us -> 0 us
  waiting for transfers between devices: 9.6 us -> 17.9 us
  starting transfers between devices: 41.1 us -> 48.4 us
    all_to_all x1 -> x0, blocking collectives: 20.1 us -> none  [exchange(): moved = lax.all_to_all(flat, axes, split_axis=0, concat_axis=0, tiled=True)]
    all_to_all x2 -> x3, waiting for transfers between devices: 5.89 us -> 13 us  [exchange(): moved = lax.all_to_all(flat, axes, split_axis=0, concat_axis=0, tiled=True)]
    all_to_all x2 -> x3, starting transfers between devices: 13.8 us -> 18.8 us  [exchange(): moved = lax.all_to_all(flat, axes, split_axis=0, concat_axis=0, tiled=True)]
    ppermute x6 -> x8, starting transfers between devices: 27.3 us -> 29.6 us  [swap(): lax.ppermute(block, axis, [(i, i ^ bit) for i in range(lax.axis_size(axis...]
    ppermute x6 -> x8, waiting for transfers between devices: 3.71 us -> 4.89 us  [swap(): lax.ppermute(block, axis, [(i, i ^ bit) for i in range(lax.axis_size(axis...]
    pallas_call x5 -> x4, Pallas kernels: 4.46 us -> 4.96 us  [the longest x1 1.7 us: local(): call(theirs_kernel, [wide_shape, shape(near_shape, BF16)], [SMEM, VMEM, V...]
  transfers between devices with their start and end apart: 8 -> 11, of which waited for: 5 -> 5; matrix products, arithmetic and copies ran while one was open for 0% -> 0% of each run, Pallas kernels for 6% -> 8%
where the time goes in v4:
time: 81.9 us; the launch traced here: 80.9 us
  starting transfers between devices  48.4 us (59%)
  waiting for transfers between devices  17.9 us (22%)
  Pallas kernels  10.6 us (13%)
  local copies, waits for them, and re-layouts  3.51 us (4%)
    ppermute x8, starting transfers between devices, swap(): lax.ppermute(block, axis, [(i, i ^ bit) for i in range(lax.axis_size(axis...  29.6 us
    all_to_all x3, starting transfers between devices, exchange(): moved = lax.all_to_all(flat, axes, split_axis=0, concat_axis=0, tiled=True)  18.8 us
    all_to_all x3, waiting for transfers between devices, exchange(): moved = lax.all_to_all(flat, axes, split_axis=0, concat_axis=0, tiled=True)  13 us
    ppermute x8, waiting for transfers between devices, swap(): lax.ppermute(block, axis, [(i, i ^ bit) for i in range(lax.axis_size(axis...  4.89 us
    unnamed x12, local copies, waits for them, and re-layouts  3.5 us
    pallas_call x1, Pallas kernels, local(): call(theirs_kernel, [wide_shape, shape(near_shape, BF16)], [SMEM, VMEM, V...  1.7 us
    pallas_call x1, Pallas kernels, local(): call(own_kernel, shape((leaves, rows, width), BF16), [SMEM] + [VMEM] * 3,...  1.7 us
    pallas_call x1, Pallas kernels, local(): call(last_kernel, shape((leaves, rows, width), BF16), [SMEM] + [VMEM] * 3...  1.7 us
  transfers between devices with their start and end apart: 11, of which 5 were waited for; matrix products, arithmetic and copies ran while one was open for 0% of the time, Pallas kernels for 8%

profile of v4, /device:TPU:1, one launch (start us, length us, event | category | flops | bytes accessed | tf_op | source)
XLA Modules:
  0.0 80.9 jit_solution(4143996437273344943)
XLA Ops:
  0.0 8.8 %collective-permute-start = (bf16[8,2,256,128]{3,2,1,0:T(8,128)(2,1)}, bf16[8,2,256,128]{3,2,1,0:T(8,128)(2,1)S(1)}, u32[]{:S(2)}, u32[]{:S(2)}) collective-permute-start(bf16[8,2,256,128]{3,2,1,0:T(8,128)(2,1)} %basis.3), channel_id=1, source_target_pairs={{0,1},{1,0},{2,3},{3,2},{4,5},{5,4},{6,7},{7,6},{8,9},{9,8},{10,11... | collective-permute-start | bytes 3145736 | tf_op jit(solution)/shard_map/ppermute | solution.py:187
  8.8 1.9 %collective-permute-start.1 = (bf16[2,256,512]{2,1,0:T(8,128)(2,1)}, bf16[2,256,512]{2,1,0:T(8,128)(2,1)S(1)}, u32[]{:S(2)}, u32[]{:S(2)}) collective-permute-start(bf16[2,256,512]{2,1,0:T(8,128)(2,1)} %own.1), channel_id=1, source_target_pairs={{0,1},{1,0},{2,3},{3,2},{4,5},{5,4},{6,7},{7,6},{8,9},{9,8},{10,11... | collective-permute-start | bytes 1572872 | tf_op jit(solution)/shard_map/ppermute | solution.py:187
  10.7 0.1 pad_add_fusion.place
  10.8 0.0 copy-start.1
  10.8 1.0 %copy-done.1 = bf16[2,256,512]{2,1,0:T(8,128)(2,1)S(1)} copy-done((bf16[2,256,512]{2,1,0:T(8,128)(2,1)S(1)}, bf16[2,256,512]{2,1,0:T(8,128)(2,1)}, u32[]{:S(2)}) %copy-start.1) | copy-done | bytes 524312
  11.8 0.0 copy-start.4
  11.8 1.2 %copy-done.4 = bf16[8,2,256,128]{3,2,1,0:T(8,128)(2,1)S(1)} copy-done((bf16[8,2,256,128]{3,2,1,0:T(8,128)(2,1)S(1)}, bf16[8,2,256,128]{3,2,1,0:T(8,128)(2,1)}, u32[]{:S(2)}) %copy-start.4) | copy-done | bytes 1048600
  13.1 1.0 %shard_map.55.mine = f32[9,128,256]{2,1,0:T(8,128)S(1)} custom-call(s32[4]{0:T(128)S(1)} %pad_add_fusion.place, bf16[8,2,256,128]{3,2,1,0:T(8,128)(2,1)S(1)} %copy-done.4, bf16[2,256,512]{2,1,0:T(8,128)(2,1)S(1)} %copy-done.1), custom_call_target="tpu_custom_call" | custom-call | flops 268435456 | bytes 2752512 | tf_op jit(solution)/shard_map/pallas_call | solution.py:217
  14.1 0.0 copy-start.2
  14.1 0.0 collective-permute-done.1.sides.by_core
  14.1 0.0 collective-permute-done.basis
  14.2 1.7 %shard_map.56 = (bf16[16,5,2,8,128]{4,3,2,1,0:T(8,128)(2,1)}, bf16[4,128,256]{2,1,0:T(8,128)(2,1)S(1)}) custom-call(s32[4]{0:T(128)S(1)} %pad_add_fusion.place, bf16[8,2,256,128]{3,2,1,0:T(8,128)(2,1)S(1)} %collective-permute-done.basis, bf16[2,256,512]{2,1,0:T(8,128)(2,1)S(1)} %collective-permute-done.1.sides.by_core, f32[9,128,256]{2,1,0:T(8,128)S(1)} %shard_map.55.mine), custom_call_target="tpu_custom_call" | custom-call | flops 268435456 | bytes 5505024 | tf_op jit(solution)/shard_map/pallas_call | solution.py:226
  15.9 5.7 %all-to-all-start = ((bf16[16,80,128]{2,1,0:T(8,128)(2,1)}), bf16[16,80,128]{2,1,0:T(8,128)(2,1)S(1)}, u32[]{:S(2)}, u32[]{:S(2)}) async-start(bf16[16,80,128]{2,1,0:T(8,128)(2,1)} %bitcast.4), calls=%async_computation | async-start | bytes 655360 | tf_op jit(solution)/shard_map/all_to_all | solution.py:211
  21.6 3.3 %collective-permute-start.2 = (bf16[4,128,256]{2,1,0:T(8,128)(2,1)S(1)}, bf16[4,128,256]{2,1,0:T(8,128)(2,1)S(1)}, u32[]{:S(2)}, u32[]{:S(2)}) collective-permute-start(bf16[4,128,256]{2,1,0:T(8,128)(2,1)S(1)} %get-tuple-element.11), channel_id=1, source_target_pairs={{0,2},{2,0},{1,3},{3,1},{4,6},{6,4},{5,7},{7,5},{8,10},{10,8},{9,1... | collective-permute-start | bytes 786440 | tf_op jit(solution)/shard_map/ppermute | solution.py:187
  24.8 8.9 %all-to-all-done = bf16[16,80,128]{2,1,0:T(8,128)(2,1)S(1)} async-done(((bf16[16,80,128]{2,1,0:T(8,128)(2,1)}), bf16[16,80,128]{2,1,0:T(8,128)(2,1)S(1)}, u32[]{:S(2)}, u32[]{:S(2)}) %all-to-all-start) | async-done | bytes 327712 | tf_op jit(solution)/shard_map/all_to_all | solution.py:211
  33.7 0.0 copy-done.2
  33.7 1.2 %shard_map.57 = (f32[16,2,8,128]{3,2,1,0:T(8,128)}, bf16[2,256,512]{2,1,0:T(8,128)(2,1)S(1)}) custom-call(s32[4]{0:T(128)S(1)} %pad_add_fusion.place, bf16[16,5,2,8,128]{4,3,2,1,0:T(8,128)(2,1)S(1)} %bitcast.13, bf16[2,256,512]{2,1,0:T(8,128)(2,1)S(1)} %copy-done.2), custom_call_target="tpu_custom_call" | custom-call | flops 10000000000 | bytes 327680 | tf_op jit(solution)/shard_map/pallas_call | solution.py:237
  35.0 9.1 %all-to-all-start.1 = ((f32[16,16,128]{2,1,0:T(8,128)}), f32[16,16,128]{2,1,0:T(8,128)S(1)}, u32[]{:S(2)}, u32[]{:S(2)}) async-start(f32[16,16,128]{2,1,0:T(8,128)} %bitcast.6), calls=%async_computation.1 | async-start | bytes 262144 | tf_op jit(solution)/shard_map/all_to_all | solution.py:211
  44.1 0.0 collective-permute-done.2
  44.1 0.1 add_convert_fusion.near
  44.2 2.8 %collective-permute-start.3 = (bf16[2,128,256]{2,1,0:T(8,128)(2,1)S(1)}, bf16[2,128,256]{2,1,0:T(8,128)(2,1)S(1)}, u32[]{:S(2)}, u32[]{:S(2)}) collective-permute-start(bf16[2,128,256]{2,1,0:T(8,128)(2,1)S(1)} %slice.12), channel_id=1, source_target_pairs={{0,4},{4,0},{8,12},{12,8},{16,20},{20,16},{24,28},{28,24},{1,5},{5... | collective-permute-start | bytes 393224 | tf_op jit(solution)/shard_map/ppermute | solution.py:187
  46.9 1.9 %collective-permute-start.5 = (bf16[2,256,512]{2,1,0:T(8,128)(2,1)S(1)}, bf16[2,256,512]{2,1,0:T(8,128)(2,1)S(1)}, u32[]{:S(2)}, u32[]{:S(2)}) collective-permute-start(bf16[2,256,512]{2,1,0:T(8,128)(2,1)S(1)} %get-tuple-element.12), channel_id=1, source_target_pairs={{0,2},{2,0},{1,3},{3,1},{4,6},{6,4},{5,7},{7,5},{8,10},{10,8},{9,1... | collective-permute-start | bytes 1572872 | tf_op jit(solution)/shard_map/ppermute | solution.py:187
  48.9 1.1 %collective-permute-done.3.near_7 = bf16[2,128,256]{2,1,0:T(8,128)(2,1)S(1)} collective-permute-done((bf16[2,128,256]{2,1,0:T(8,128)(2,1)S(1)}, bf16[2,128,256]{2,1,0:T(8,128)(2,1)S(1)}, u32[]{:S(2)}, u32[]{:S(2)}) %collective-permute-start.3) | collective-permute-done | bytes 131104 | tf_op jit(solution)/shard_map/ppermute | solution.py:187
  50.0 4.2 %all-to-all-done.1 = f32[16,16,128]{2,1,0:T(8,128)S(1)} async-done(((f32[16,16,128]{2,1,0:T(8,128)}), f32[16,16,128]{2,1,0:T(8,128)S(1)}, u32[]{:S(2)}, u32[]{:S(2)}) %all-to-all-start.1) | async-done | bytes 131104 | tf_op jit(solution)/shard_map/all_to_all | solution.py:211
  54.2 1.3 %shard_map.58 = bf16[16,5,2,8,128]{4,3,2,1,0:T(8,128)(2,1)} custom-call(s32[4]{0:T(128)S(1)} %pad_add_fusion.place, f32[16,2,8,128]{3,2,1,0:T(8,128)S(1)} %bitcast.15, bf16[16,5,2,8,128]{4,3,2,1,0:T(8,128)(2,1)S(1)} %bitcast.14, bf16[2,128,256]{2,1,0:T(8,128)(2,1)S(1)} %collective-permute-done.3.near_7), custom_call_target="tpu_custom_call" | custom-call | flops 10000000000 | bytes 655360 | tf_op jit(solution)/shard_map/pallas_call | solution.py:247
  55.5 4.0 %all-to-all-start.2 = ((bf16[16,80,128]{2,1,0:T(8,128)(2,1)}), bf16[16,80,128]{2,1,0:T(8,128)(2,1)S(1)}, u32[]{:S(2)}, u32[]{:S(2)}) async-start(bf16[16,80,128]{2,1,0:T(8,128)(2,1)} %bitcast.8), calls=%async_computation.2 | async-start | bytes 655360 | tf_op jit(solution)/shard_map/all_to_all | solution.py:211
  59.5 1.4 %collective-permute-done.5.by_chip = bf16[2,256,512]{2,1,0:T(8,128)(2,1)S(1)} collective-permute-done((bf16[2,256,512]{2,1,0:T(8,128)(2,1)S(1)}, bf16[2,256,512]{2,1,0:T(8,128)(2,1)S(1)}, u32[]{:S(2)}, u32[]{:S(2)}) %collective-permute-start.5) | collective-permute-done | bytes 524320 | tf_op jit(solution)/shard_map/ppermute | solution.py:187
  60.9 4.8 %collective-permute-start.6 = (bf16[2,256,512]{2,1,0:T(8,128)(2,1)S(1)}, bf16[2,256,512]{2,1,0:T(8,128)(2,1)S(1)}, u32[]{:S(2)}, u32[]{:S(2)}) collective-permute-start(bf16[2,256,512]{2,1,0:T(8,128)(2,1)S(1)} %collective-permute-done.5.by_chip), channel_id=1, source_target_pairs={{0,1},{1,0},{2,3},{3,2},{4,5},{5,4},{6,7},{7,6},{8,9},{9,8},{10,11... | collective-permute-start | bytes 1572872 | tf_op jit(solution)/shard_map/ppermute | solution.py:187
  65.6 0.0 copy-start.5
  65.7 3.7 %collective-permute-start.4 = (bf16[128,256]{1,0:T(8,128)(2,1)S(1)}, bf16[128,256]{1,0:T(8,128)(2,1)S(1)}, u32[]{:S(2)}, u32[]{:S(2)}) collective-permute-start(bf16[128,256]{1,0:T(8,128)(2,1)S(1)} %fusion), channel_id=1, source_target_pairs={{0,8},{4,12},{8,0},{12,4},{16,24},{20,28},{24,16},{28,20},{1,9},{5... | collective-permute-start | bytes 196616 | tf_op jit(solution)/shard_map/ppermute | solution.py:187
  69.4 0.0 collective-permute-done.6.by_both
  69.4 0.0 copy-start.3
  69.4 1.2 %copy-done.3 = bf16[2,256,1024]{2,1,0:T(8,128)(2,1)S(1)} copy-done((bf16[2,256,1024]{2,1,0:T(8,128)(2,1)S(1)}, bf16[2,256,1024]{2,1,0:T(8,128)(2,1)}, u32[]{:S(2)}) %copy-start.3) | copy-done | bytes 1048600
  70.7 1.3 %shard_map.59.dense = f32[2,256,512]{2,1,0:T(8,128)S(1)} custom-call(s32[4]{0:T(128)S(1)} %pad_add_fusion.place, bf16[2,256,1024]{2,1,0:T(8,128)(2,1)S(1)} %copy-done.3, bf16[2,256,512]{2,1,0:T(8,128)(2,1)S(1)} %copy-done.2, bf16[2,256,512]{2,1,0:T(8,128)(2,1)S(1)} %collective-permute-done.1.sides.by_core, ...), custom_call_target="tpu_custom_call" | custom-call | flops 536870912 | bytes 4194304 | tf_op jit(solution)/shard_map/pallas_call | solution.py:255
  71.9 2.4 %collective-permute-done.4.near_6 = bf16[128,256]{1,0:T(8,128)(2,1)S(1)} collective-permute-done((bf16[128,256]{1,0:T(8,128)(2,1)S(1)}, bf16[128,256]{1,0:T(8,128)(2,1)S(1)}, u32[]{:S(2)}, u32[]{:S(2)}) %collective-permute-start.4) | collective-permute-done | bytes 65568 | tf_op jit(solution)/shard_map/ppermute | solution.py:187
  74.3 0.0 all-to-all-done.2
  74.3 0.0 copy-done.5
  74.3 0.0 copy-start
  74.3 0.7 shard_map.60.coef
  75.0 2.5 %collective-permute-start.7 = (bf16[1152,256]{1,0:T(8,128)(2,1)S(1)}, bf16[1152,256]{1,0:T(8,128)(2,1)S(1)}, u32[]{:S(2)}, u32[]{:S(2)}) collective-permute-start(bf16[1152,256]{1,0:T(8,128)(2,1)S(1)} %shard_map.60.coef), channel_id=1, source_target_pairs={{0,1},{1,0},{2,3},{3,2},{4,5},{5,4},{6,7},{7,6},{8,9},{9,8},{10,11... | collective-permute-start | bytes 1769480 | tf_op jit(solution)/shard_map/ppermute | solution.py:187
  77.5 0.0 copy-done
  77.5 1.7 %shard_map.61.begun = bf16[2,256,512]{2,1,0:T(8,128)(2,1)} custom-call(s32[4]{0:T(128)S(1)} %pad_add_fusion.place, bf16[1152,256]{1,0:T(8,128)(2,1)S(1)} %shard_map.60.coef, bf16[8,2,256,128]{3,2,1,0:T(8,128)(2,1)S(1)} %copy-done, f32[2,256,512]{2,1,0:T(8,128)S(1)} %shard_map.59.dense), custom_call_target="tpu_custom_call" | custom-call | flops 268435456 | bytes 2686976 | tf_op jit(solution)/shard_map/pallas_call | solution.py:271
  79.2 0.0 collective-permute-done.7.coef
  79.2 1.7 %shard_map.62 = bf16[2,256,512]{2,1,0:T(8,128)(2,1)} custom-call(s32[4]{0:T(128)S(1)} %pad_add_fusion.place, bf16[1152,256]{1,0:T(8,128)(2,1)S(1)} %collective-permute-done.7.coef, bf16[8,2,256,128]{3,2,1,0:T(8,128)(2,1)S(1)} %copy-done, f32[2,256,512]{2,1,0:T(8,128)S(1)} %shard_map.59.dense, ...), custom_call_target="tpu_custom_call", output_to_operand_aliasing={{}: (4, {})} | custom-call | flops 268435456 | bytes 2686976 | tf_op jit(solution)/shard_map/pallas_call | solution.py:280
  (2 shorter events, 0.0 us)
Async XLA Ops:
  0.0 14.1 %collective-permute-start = (bf16[8,2,256,128]{3,2,1,0:T(8,128)(2,1)}, bf16[8,2,256,128]{3,2,1,0:T(8,128)(2,1)S(1)}, u32[]{:S(2)}, u32[]{:S(2)}) collective-permute-start(bf16[8,2,256,128]{3,2,1,0:T(8,128)(2,1)} %basis.3), channel_id=1, source_target_pairs={{0,1},{1,0},{2,3},{3,2},{4,5},{5,4},{6,7},{7,6},{8,9},{9,8},{10,11... | collective-permute-start | bytes 3145736 | tf_op jit(solution)/shard_map/ppermute | solution.py:187
  8.8 5.3 %collective-permute-start.1 = (bf16[2,256,512]{2,1,0:T(8,128)(2,1)}, bf16[2,256,512]{2,1,0:T(8,128)(2,1)S(1)}, u32[]{:S(2)}, u32[]{:S(2)}) collective-permute-start(bf16[2,256,512]{2,1,0:T(8,128)(2,1)} %own.1), channel_id=1, source_target_pairs={{0,1},{1,0},{2,3},{3,2},{4,5},{5,4},{6,7},{7,6},{8,9},{9,8},{10,11... | collective-permute-start | bytes 1572872 | tf_op jit(solution)/shard_map/ppermute | solution.py:187
  10.8 1.0 %copy-start.1 = (bf16[2,256,512]{2,1,0:T(8,128)(2,1)S(1)}, bf16[2,256,512]{2,1,0:T(8,128)(2,1)}, u32[]{:S(2)}) copy-start(bf16[2,256,512]{2,1,0:T(8,128)(2,1)} %own.1) | copy-start | bytes 1572868
  11.8 1.2 %copy-start.4 = (bf16[8,2,256,128]{3,2,1,0:T(8,128)(2,1)S(1)}, bf16[8,2,256,128]{3,2,1,0:T(8,128)(2,1)}, u32[]{:S(2)}) copy-start(bf16[8,2,256,128]{3,2,1,0:T(8,128)(2,1)} %basis.3) | copy-start | bytes 3145732
  14.1 19.6 %copy-start.2 = (bf16[2,256,512]{2,1,0:T(8,128)(2,1)S(1)}, bf16[2,256,512]{2,1,0:T(8,128)(2,1)}, u32[]{:S(2)}) copy-start(bf16[2,256,512]{2,1,0:T(8,128)(2,1)} %own.1) | copy-start | bytes 1572868
  15.9 17.9 %all-to-all-start = ((bf16[16,80,128]{2,1,0:T(8,128)(2,1)}), bf16[16,80,128]{2,1,0:T(8,128)(2,1)S(1)}, u32[]{:S(2)}, u32[]{:S(2)}) async-start(bf16[16,80,128]{2,1,0:T(8,128)(2,1)} %bitcast.4), calls=%async_computation | async-start | bytes 655360 | tf_op jit(solution)/shard_map/all_to_all | solution.py:211
  21.6 22.5 %collective-permute-start.2 = (bf16[4,128,256]{2,1,0:T(8,128)(2,1)S(1)}, bf16[4,128,256]{2,1,0:T(8,128)(2,1)S(1)}, u32[]{:S(2)}, u32[]{:S(2)}) collective-permute-start(bf16[4,128,256]{2,1,0:T(8,128)(2,1)S(1)} %get-tuple-element.11), channel_id=1, source_target_pairs={{0,2},{2,0},{1,3},{3,1},{4,6},{6,4},{5,7},{7,5},{8,10},{10,8},{9,1... | collective-permute-start | bytes 786440 | tf_op jit(solution)/shard_map/ppermute | solution.py:187
  35.0 19.2 %all-to-all-start.1 = ((f32[16,16,128]{2,1,0:T(8,128)}), f32[16,16,128]{2,1,0:T(8,128)S(1)}, u32[]{:S(2)}, u32[]{:S(2)}) async-start(f32[16,16,128]{2,1,0:T(8,128)} %bitcast.6), calls=%async_computation.1 | async-start | bytes 262144 | tf_op jit(solution)/shard_map/all_to_all | solution.py:211
  44.2 5.8 %collective-permute-start.3 = (bf16[2,128,256]{2,1,0:T(8,128)(2,1)S(1)}, bf16[2,128,256]{2,1,0:T(8,128)(2,1)S(1)}, u32[]{:S(2)}, u32[]{:S(2)}) collective-permute-start(bf16[2,128,256]{2,1,0:T(8,128)(2,1)S(1)} %slice.12), channel_id=1, source_target_pairs={{0,4},{4,0},{8,12},{12,8},{16,20},{20,16},{24,28},{28,24},{1,5},{5... | collective-permute-start | bytes 393224 | tf_op jit(solution)/shard_map/ppermute | solution.py:187
  46.9 13.9 %collective-permute-start.5 = (bf16[2,256,512]{2,1,0:T(8,128)(2,1)S(1)}, bf16[2,256,512]{2,1,0:T(8,128)(2,1)S(1)}, u32[]{:S(2)}, u32[]{:S(2)}) collective-permute-start(bf16[2,256,512]{2,1,0:T(8,128)(2,1)S(1)} %get-tuple-element.12), channel_id=1, source_target_pairs={{0,2},{2,0},{1,3},{3,1},{4,6},{6,4},{5,7},{7,5},{8,10},{10,8},{9,1... | collective-permute-start | bytes 1572872 | tf_op jit(solution)/shard_map/ppermute | solution.py:187
  55.5 18.8 %all-to-all-start.2 = ((bf16[16,80,128]{2,1,0:T(8,128)(2,1)}), bf16[16,80,128]{2,1,0:T(8,128)(2,1)S(1)}, u32[]{:S(2)}, u32[]{:S(2)}) async-start(bf16[16,80,128]{2,1,0:T(8,128)(2,1)} %bitcast.8), calls=%async_computation.2 | async-start | bytes 655360 | tf_op jit(solution)/shard_map/all_to_all | solution.py:211
  60.9 8.6 %collective-permute-start.6 = (bf16[2,256,512]{2,1,0:T(8,128)(2,1)S(1)}, bf16[2,256,512]{2,1,0:T(8,128)(2,1)S(1)}, u32[]{:S(2)}, u32[]{:S(2)}) collective-permute-start(bf16[2,256,512]{2,1,0:T(8,128)(2,1)S(1)} %collective-permute-done.5.by_chip), channel_id=1, source_target_pairs={{0,1},{1,0},{2,3},{3,2},{4,5},{5,4},{6,7},{7,6},{8,9},{9,8},{10,11... | collective-permute-start | bytes 1572872 | tf_op jit(solution)/shard_map/ppermute | solution.py:187
  65.6 8.6 %copy-start.5 = (s32[510]{0:T(512)S(1)}, s32[510]{0:T(512)}, u32[]{:S(2)}) copy-start(s32[510]{0:T(512)} %ranks.1) | copy-start | bytes 6124
  65.7 8.6 %collective-permute-start.4 = (bf16[128,256]{1,0:T(8,128)(2,1)S(1)}, bf16[128,256]{1,0:T(8,128)(2,1)S(1)}, u32[]{:S(2)}, u32[]{:S(2)}) collective-permute-start(bf16[128,256]{1,0:T(8,128)(2,1)S(1)} %fusion), channel_id=1, source_target_pairs={{0,8},{4,12},{8,0},{12,4},{16,24},{20,28},{24,16},{28,20},{1,9},{5... | collective-permute-start | bytes 196616 | tf_op jit(solution)/shard_map/ppermute | solution.py:187
  69.4 1.2 %copy-start.3 = (bf16[2,256,1024]{2,1,0:T(8,128)(2,1)S(1)}, bf16[2,256,1024]{2,1,0:T(8,128)(2,1)}, u32[]{:S(2)}) copy-start(bf16[2,256,1024]{2,1,0:T(8,128)(2,1)} %blocks.1) | copy-start | bytes 3145732
  74.3 3.2 %copy-start = (bf16[8,2,256,128]{3,2,1,0:T(8,128)(2,1)S(1)}, bf16[8,2,256,128]{3,2,1,0:T(8,128)(2,1)}, u32[]{:S(2)}) copy-start(bf16[8,2,256,128]{3,2,1,0:T(8,128)(2,1)} %basis.5) | copy-start | bytes 3145732
  75.0 4.2 %collective-permute-start.7 = (bf16[1152,256]{1,0:T(8,128)(2,1)S(1)}, bf16[1152,256]{1,0:T(8,128)(2,1)S(1)}, u32[]{:S(2)}, u32[]{:S(2)}) collective-permute-start(bf16[1152,256]{1,0:T(8,128)(2,1)S(1)} %shard_map.60.coef), channel_id=1, source_target_pairs={{0,1},{1,0},{2,3},{3,2},{4,5},{5,4},{6,7},{7,6},{8,9},{9,8},{10,11... | collective-permute-start | bytes 1769480 | tf_op jit(solution)/shard_map/ppermute | solution.py:187

commit v5 on v4

v5 whole, which is shorter than its diff:
```python
import jax
import jax.numpy as jnp
from jax import lax
from jax.experimental import pallas as pl
from jax.experimental.pallas import tpu as pltpu
from jax.sharding import Mesh, PartitionSpec as P

VMEM_BYTES = 48 * 1024 * 1024
LONG = 20 * 10**8
LONG2 = 20 * 10**8
LONG3 = 30 * 10**8
F32 = jnp.float32
BF16 = jnp.bfloat16


def call(
    kernel, out_shape, in_specs, scratch=(), flops=0, moved=0, whole=None, aliases=None
):
    many = isinstance(out_shape, (list, tuple))
    whole = whole or VMEM
    return pl.pallas_call(
        kernel,
        out_shape=out_shape,
        in_specs=in_specs,
        out_specs=[whole] * len(out_shape) if many else whole,
        scratch_shapes=list(scratch),
        input_output_aliases=aliases or {},
        compiler_params=pltpu.CompilerParams(vmem_limit_bytes=VMEM_BYTES),
        cost_estimate=pl.CostEstimate(flops=flops, bytes_accessed=moved, transcendentals=0),
    )


SMEM = pl.BlockSpec(memory_space=pltpu.SMEM)
VMEM = pl.BlockSpec(memory_space=pltpu.VMEM)
ANY = pl.BlockSpec(memory_space=pl.ANY)


def place():
    high, chip, core = (lax.axis_index(axis) for axis in ("high", "chip", "core"))
    return lax.axis_size("z") * high + lax.axis_index("z"), core, 2 * chip + core, high


def projections( basis, sides):
    levels, leaves, rows, rank = basis.shape
    half = sides.shape[2] // 2
    both = sides[:, :, pl.ds(pl.multiple_of(place()[1] * half, half), half)]
    contract = (((0,), (0,)), ((), ()))
    for level in range(levels - 1):
        yield lax.dot_general(
            basis[level].reshape(leaves * rows, rank),
            both.reshape(leaves * rows, half),
            contract,
            preferred_element_type=F32,
        )
    for leaf in range(leaves):
        yield lax.dot_general(
            basis[levels - 1, leaf], both[leaf], contract, preferred_element_type=F32
        )


def mine_kernel(basis, sides, out):
    for slot, value in enumerate(projections(basis, sides)):
        out[slot] = value


def theirs_kernel(basis, sides, mine, wide, near):
    down, wide_levels, across = wide.shape[:3]
    for slot, value in enumerate(projections(basis, sides)):
        total = mine[slot] + value
        if slot >= wide_levels:
            near[slot - wide_levels] = total.astype(BF16)
            continue
        for col in range(across):
            part = total[:, col * 128 : (col + 1) * 128]
            wide[:, slot, col] = part.reshape(down, 8, 128).astype(BF16)


def ring_kernel(parts, out):
    high = place()[3]
    bits = out.shape[0].bit_length() - 1
    total = [None] * bits
    for level in range(bits):
        for member in range(parts.shape[0]):
            part = parts[member, level].astype(F32)
            total[level] = part if total[level] is None else total[level] + part
    out[high] = jnp.zeros(out.shape[1:], F32)
    for step in range(1, out.shape[0]):
        out[jnp.bitwise_xor(high, step)] = total[bits - step.bit_length()]


def back_kernel(high_parts, parts, near_7, out):
    high = place()[3]
    steps = high_parts.shape[0]
    bits = steps.bit_length() - 1
    members = out.shape[0]
    for level in range(bits):
        first = 1 << (bits - 1 - level)
        total = high_parts[jnp.bitwise_xor(high, first)]
        for step in range(first + 1, 2 * first):
            total = total + high_parts[jnp.bitwise_xor(high, step)]
        rounded = total.astype(BF16)
        for member in range(members):
            out[member, level] = rounded
    for side in range(2):
        first = (1 - side) * members // 2
        total = parts[first, bits].astype(F32)
        for member in range(first + 1, first + members // 2):
            total = total + parts[member, bits].astype(F32)
        rounded = total.astype(BF16)
        for member in range(side * members // 2, (side + 1) * members // 2):
            out[member, bits] = rounded


def dense_kernel(ranks, blocks, own, by_core, by_chip, by_both, basis, out, left):
    leaves, rows, _ = blocks.shape
    levels, _, _, rank = basis.shape
    position, _, row, _ = place()
    for leaf in range(leaves):
        total = None
        for step, sides in enumerate((own, by_core, by_chip, by_both)):
            column = pl.multiple_of(jnp.bitwise_xor(row, step) * rows, rows)
            term = jnp.dot(
                blocks[leaf, :, pl.ds(column, rows)], sides[leaf], preferred_element_type=F32
            )
            total = term if total is None else total + term
        out[leaf] = total
    columns = lax.broadcasted_iota(jnp.int32, (rows, rank), 1)
    for level in range(levels):
        for leaf in range(leaves):
            if level < levels - 1:
                heap = 2 ** (level + 1) - 2 + lax.shift_right_logical(position, levels - 2 - level)
                slot = level + 1 - leaf
            else:
                heap = 2**levels - 2 + leaves * position + leaf
                slot = level * leaf
            kept = jnp.where(columns < ranks[heap], basis[level, leaf].astype(F32), 0.0)
            left[leaf, :, slot * rank : (slot + 1) * rank] = kept.astype(BF16)


def gather_kernel(wide, near_6, near_7, near, late, out):
    rank = wide.shape[0] * 8
    wide_levels, across = wide.shape[1:3]
    for level in range(wide_levels):
        for col in range(across):
            part = wide[:, level, col].astype(F32).reshape(rank, 128).astype(BF16)
            out[(1 + level) * rank : (2 + level) * rank, col * 128 : (col + 1) * 128] = part
    row = (1 + wide_levels) * rank
    out[:rank] = near[3]
    for part in (near_6[...], near_7[1], near[2]):
        out[row : row + rank] = part
        row += rank


def update(coef, left, dense, column, store):
    leaves, _, depth = left.shape
    half = coef.shape[1]
    rank = coef.shape[0] - depth
    for leaf in range(leaves):
        term = jnp.dot(
            left[leaf], coef[leaf * rank : leaf * rank + depth], preferred_element_type=F32
        )
        store(leaf, (dense[leaf, :, pl.ds(column, half)] + term).astype(BF16))


def own_kernel(coef, left, dense, out, held, sems):
    half = held.shape[2]
    place_half(place()[1], coef, left, dense, out, held, sems, half)


def last_kernel(coef, left, dense, begun, out, held, sems):
    half = held.shape[2]
    place_half(1 - place()[1], coef, left, dense, out, held, sems, half)


def place_half(index, coef, left, dense, out, held, sems, half):
    column = pl.multiple_of(index * half, half)
    copies = []

    def store(leaf, value):
        held[leaf] = value
        copies.append(
            pltpu.make_async_copy(
                held.at[leaf], out.at[leaf, :, pl.ds(column, half)], sems.at[leaf]
            )
        )
        copies[-1].start()

    update(coef, left, dense, column, store)
    for copy in copies:
        copy.wait()


def swap(block, axis, bit=1):
    return lax.ppermute(block, axis, [(i, i ^ bit) for i in range(lax.axis_size(axis))])


def local(right_sides, leaf_blocks, basis_left, basis_right, block_ranks):
    leaves, rows, width = right_sides.shape
    levels, _, _, rank = basis_left.shape
    half = width // 2
    upper = levels - 1
    ring = lax.axis_size("z")
    highs = lax.axis_size("high")
    wide_levels = levels - 3
    owners = 2 * ring
    shape = jax.ShapeDtypeStruct
    slots = upper + leaves
    tile = (half // 128, 8, 128)
    flops = 2 * levels * leaves * rows * rank * half

    def exchange(block, axes):
        flat = block.reshape((block.shape[0], -1, 128))
        moved = lax.all_to_all(flat, axes, split_axis=0, concat_axis=0, tiled=True)
        return moved.reshape(block.shape)

    basis_core = swap(basis_right, "core")
    by_core = swap(right_sides, "core")
    moved = 2 * (basis_right.size + right_sides.size) + 4 * slots * rank * half
    mine = call(
        mine_kernel,
        shape((slots, rank, half), F32),
        [VMEM, VMEM],
        flops=flops,
        moved=moved,
    )(basis_right, right_sides)
    wide_shape = shape((owners, wide_levels) + tile, BF16)
    near_shape = (slots - wide_levels, rank, half)
    wide, near = call(
        theirs_kernel,
        [wide_shape, shape(near_shape, BF16)],
        [VMEM, VMEM, VMEM],
        flops=flops,
        moved=2 * moved,
    )(basis_core, by_core, mine)
    wide = exchange(wide, ("z", "chip"))
    near = (near.astype(F32) + swap(near, "chip").astype(F32)).astype(BF16)
    near_7 = swap(near[:2], "z", 1)
    near_6 = swap((near[0].astype(F32) + near_7[0].astype(F32)).astype(BF16), "z", 2)
    to_high = call(
        ring_kernel,
        shape((highs,) + tile, F32),
        [VMEM],
        flops=LONG,
        moved=2 * wide.size,
    )(wide)
    from_high = exchange(to_high, ("high",))
    by_chip = swap(right_sides, "chip")
    by_both = swap(by_chip, "core")
    wide = call(
        back_kernel,
        wide_shape,
        [VMEM, VMEM, VMEM],
        flops=LONG2,
        moved=4 * wide.size,
    )(from_high, wide, near_7)
    wide = exchange(wide, ("z", "chip"))
    dense, left = call(
        dense_kernel,
        [
            shape((leaves, rows, width), F32),
            shape((leaves, rows, levels * rank), BF16),
        ],
        [SMEM] + [VMEM] * 6,
        flops=LONG3,
        moved=2 * leaf_blocks.size + 12 * right_sides.size + 4 * basis_left.size,
    )(block_ranks, leaf_blocks, right_sides, by_core, by_chip, by_both, basis_left)
    coef = call(
        gather_kernel,
        shape((slots * rank, half), BF16),
        [VMEM] * 4 + [ANY],
        moved=4 * slots * rank * half,
    )(wide, near_6, near_7, near, dense)
    coef_other = swap(coef, "core")
    held = [pltpu.VMEM((leaves, rows, half), BF16), pltpu.SemaphoreType.DMA((leaves,))]
    moved = 2 * (basis_left.size + coef.size) + 4 * right_sides.size
    begun = call(
        own_kernel,
        shape((leaves, rows, width), BF16),
        [VMEM] * 3,
        scratch=held,
        whole=ANY,
        flops=flops,
        moved=moved,
    )(coef, left, dense)
    return call(
        last_kernel,
        shape((leaves, rows, width), BF16),
        [VMEM] * 3 + [ANY],
        scratch=held,
        whole=ANY,
        aliases={3: 0},
        flops=flops,
        moved=moved,
    )(coef_other, left, dense, begun)


def solution(mesh):
    clusters = mesh.shape["clus"]
    ring = 8
    fine = Mesh(
        mesh.devices.reshape(clusters // ring, ring, 2, 2), ("high", "z", "chip", "core")
    )
    places, rows = ("high", "z"), ("chip", "core")
    in_specs = (
        P(places, rows, None),
        P(places, rows, None),
        P(None, places, rows, None),
        P(None, places, rows, None),
        P(),
    )
    return jax.shard_map(
        local, mesh=fine, in_specs=in_specs, out_specs=P(places, rows, None), check_vma=False
    )
```

time: 81.9 us -> 78.4 us (0.957)
  waiting for transfers between devices: 17.9 us -> 10.5 us
  local copies, waits for them, and re-layouts: 3.51 us -> 7.43 us
  starting transfers between devices: 48.4 us -> 51.4 us
  Pallas kernels: 10.6 us -> 7.77 us
    ppermute x8, waiting for transfers between devices: 4.89 us -> 0.46 us  [swap(): lax.ppermute(block, axis, [(i, i ^ bit) for i in range(lax.axis_size(axis...]
    unnamed x12 -> x22, local copies, waits for them, and re-layouts: 3.5 us -> 7.42 us
    ppermute x8, starting transfers between devices: 29.6 us -> 32.6 us  [swap(): lax.ppermute(block, axis, [(i, i ^ bit) for i in range(lax.axis_size(axis...]
    all_to_all x3, waiting for transfers between devices: 13 us -> 10.1 us  [exchange(): moved = lax.all_to_all(flat, axes, split_axis=0, concat_axis=0, tiled=True)]
    pallas_call x8, Pallas kernels: 10.6 us -> 7.77 us  [the longest x1 2.23 us: local(): call(dense_kernel, [shape((leaves, rows, width), F32), shape((leaves, row...]
  transfers between devices with their start and end apart: 11 -> 11, of which waited for: 5 -> 3; matrix products, arithmetic and copies ran while one was open for 0% -> 0% of each run, Pallas kernels for 8% -> 7%
where the time goes in v5:
time: 78.4 us; the launch traced here: 77.5 us
  starting transfers between devices  51.4 us (66%)
  waiting for transfers between devices  10.5 us (13%)
  Pallas kernels  7.77 us (10%)
  local copies, waits for them, and re-layouts  7.43 us (9%)
    ppermute x8, starting transfers between devices, swap(): lax.ppermute(block, axis, [(i, i ^ bit) for i in range(lax.axis_size(axis...  32.6 us
    all_to_all x3, starting transfers between devices, exchange(): moved = lax.all_to_all(flat, axes, split_axis=0, concat_axis=0, tiled=True)  18.8 us
    all_to_all x3, waiting for transfers between devices, exchange(): moved = lax.all_to_all(flat, axes, split_axis=0, concat_axis=0, tiled=True)  10.1 us
    unnamed x22, local copies, waits for them, and re-layouts  7.42 us
    pallas_call x1, Pallas kernels, local(): call(dense_kernel, [shape((leaves, rows, width), F32), shape((leaves, row...  2.23 us
  transfers between devices with their start and end apart: 11, of which 3 were waited for; matrix products, arithmetic and copies ran while one was open for 0% of the time, Pallas kernels for 7%

profile of v5, /device:TPU:1, one launch (start us, length us, event | category | flops | bytes accessed | tf_op | source)
XLA Modules:
  0.0 77.5 jit_solution(9137322392341200517)
XLA Ops:
  0.0 8.8 %collective-permute-start = (bf16[8,2,256,128]{3,2,1,0:T(8,128)(2,1)}, bf16[8,2,256,128]{3,2,1,0:T(8,128)(2,1)S(1)}, u32[]{:S(2)}, u32[]{:S(2)}) collective-permute-start(bf16[8,2,256,128]{3,2,1,0:T(8,128)(2,1)} %basis.2), channel_id=1, source_target_pairs={{0,1},{1,0},{2,3},{3,2},{4,5},{5,4},{6,7},{7,6},{8,9},{9,8},{10,11... | collective-permute-start | bytes 3145736 | tf_op jit(solution)/shard_map/ppermute | solution.py:194
  8.8 1.9 %collective-permute-start.1 = (bf16[2,256,512]{2,1,0:T(8,128)(2,1)}, bf16[2,256,512]{2,1,0:T(8,128)(2,1)S(1)}, u32[]{:S(2)}, u32[]{:S(2)}) collective-permute-start(bf16[2,256,512]{2,1,0:T(8,128)(2,1)} %own.1), channel_id=1, source_target_pairs={{0,1},{1,0},{2,3},{3,2},{4,5},{5,4},{6,7},{7,6},{8,9},{9,8},{10,11... | collective-permute-start | bytes 1572872 | tf_op jit(solution)/shard_map/ppermute | solution.py:194
  10.7 0.0 copy-start
  10.7 1.2 %copy-done = bf16[8,2,256,128]{3,2,1,0:T(8,128)(2,1)S(1)} copy-done((bf16[8,2,256,128]{3,2,1,0:T(8,128)(2,1)S(1)}, bf16[8,2,256,128]{3,2,1,0:T(8,128)(2,1)}, u32[]{:S(2)}) %copy-start) | copy-done | bytes 1048600
  11.9 0.0 copy-start.1
  11.9 1.0 %copy-done.1 = bf16[2,256,512]{2,1,0:T(8,128)(2,1)S(1)} copy-done((bf16[2,256,512]{2,1,0:T(8,128)(2,1)S(1)}, bf16[2,256,512]{2,1,0:T(8,128)(2,1)}, u32[]{:S(2)}) %copy-start.1) | copy-done | bytes 524312
  13.0 0.5 shard_map.55.mine
  13.5 0.0 copy-start.2
  13.5 0.0 collective-permute-done.1.sides.by_core
  13.5 0.0 copy-start.3
  13.5 0.0 collective-permute-done.basis
  13.5 1.2 %shard_map.56 = (bf16[16,5,2,8,128]{4,3,2,1,0:T(8,128)(2,1)}, bf16[4,128,256]{2,1,0:T(8,128)(2,1)S(1)}) custom-call(bf16[8,2,256,128]{3,2,1,0:T(8,128)(2,1)S(1)} %collective-permute-done.basis, bf16[2,256,512]{2,1,0:T(8,128)(2,1)S(1)} %collective-permute-done.1.sides.by_core, f32[9,128,256]{2,1,0:T(8,128)S(1)} %shard_map.55.mine), custom_call_target="tpu_custom_call" | custom-call | flops 268435456 | bytes 5505024 | tf_op jit(solution)/shard_map/pallas_call | solution.py:228
  14.7 0.0 copy-done.3
  14.7 5.7 %all-to-all-start = ((bf16[16,80,128]{2,1,0:T(8,128)(2,1)}), bf16[16,80,128]{2,1,0:T(8,128)(2,1)S(1)}, u32[]{:S(2)}, u32[]{:S(2)}) async-start(bf16[16,80,128]{2,1,0:T(8,128)(2,1)} %bitcast), calls=%async_computation | async-start | bytes 655360 | tf_op jit(solution)/shard_map/all_to_all | solution.py:213
  20.4 3.3 %collective-permute-start.2 = (bf16[4,128,256]{2,1,0:T(8,128)(2,1)S(1)}, bf16[4,128,256]{2,1,0:T(8,128)(2,1)S(1)}, u32[]{:S(2)}, u32[]{:S(2)}) collective-permute-start(bf16[4,128,256]{2,1,0:T(8,128)(2,1)S(1)} %get-tuple-element.10), channel_id=1, source_target_pairs={{0,2},{2,0},{1,3},{3,1},{4,6},{6,4},{5,7},{7,5},{8,10},{10,8},{9,1... | collective-permute-start | bytes 786440 | tf_op jit(solution)/shard_map/ppermute | solution.py:194
  23.7 0.0 copy-done.2
  23.7 2.0 %collective-permute-start.5 = (bf16[2,256,512]{2,1,0:T(8,128)(2,1)S(1)}, bf16[2,256,512]{2,1,0:T(8,128)(2,1)S(1)}, u32[]{:S(2)}, u32[]{:S(2)}) collective-permute-start(bf16[2,256,512]{2,1,0:T(8,128)(2,1)S(1)} %copy-done.2), channel_id=1, source_target_pairs={{0,2},{2,0},{1,3},{3,1},{4,6},{6,4},{5,7},{7,5},{8,10},{10,8},{9,1... | collective-permute-start | bytes 1572872 | tf_op jit(solution)/shard_map/ppermute | solution.py:194
  25.7 6.9 %all-to-all-done = bf16[16,80,128]{2,1,0:T(8,128)(2,1)S(1)} async-done(((bf16[16,80,128]{2,1,0:T(8,128)(2,1)}), bf16[16,80,128]{2,1,0:T(8,128)(2,1)S(1)}, u32[]{:S(2)}, u32[]{:S(2)}) %all-to-all-start) | async-done | bytes 327712 | tf_op jit(solution)/shard_map/all_to_all | solution.py:213
  32.6 0.7 shard_map.57
  33.3 9.1 %all-to-all-start.1 = ((f32[16,16,128]{2,1,0:T(8,128)}), f32[16,16,128]{2,1,0:T(8,128)S(1)}, u32[]{:S(2)}, u32[]{:S(2)}) async-start(f32[16,16,128]{2,1,0:T(8,128)} %bitcast.2), calls=%async_computation.1 | async-start | bytes 262144 | tf_op jit(solution)/shard_map/all_to_all | solution.py:213
  42.4 0.0 collective-permute-done.2
  42.4 0.1 add_convert_fusion.near
  42.5 2.7 %collective-permute-start.3 = (bf16[2,128,256]{2,1,0:T(8,128)(2,1)S(1)}, bf16[2,128,256]{2,1,0:T(8,128)(2,1)S(1)}, u32[]{:S(2)}, u32[]{:S(2)}) collective-permute-start(bf16[2,128,256]{2,1,0:T(8,128)(2,1)S(1)} %slice.12), channel_id=1, source_target_pairs={{0,4},{4,0},{8,12},{12,8},{16,20},{20,16},{24,28},{28,24},{1,5},{5... | collective-permute-start | bytes 393224 | tf_op jit(solution)/shard_map/ppermute | solution.py:194
  45.3 0.0 collective-permute-done.5.by_chip
  45.3 0.0 copy-start.6
  45.3 3.9 %collective-permute-start.6 = (bf16[2,256,512]{2,1,0:T(8,128)(2,1)S(1)}, bf16[2,256,512]{2,1,0:T(8,128)(2,1)S(1)}, u32[]{:S(2)}, u32[]{:S(2)}) collective-permute-start(bf16[2,256,512]{2,1,0:T(8,128)(2,1)S(1)} %collective-permute-done.5.by_chip), channel_id=1, source_target_pairs={{0,1},{1,0},{2,3},{3,2},{4,5},{5,4},{6,7},{7,6},{8,9},{9,8},{10,11... | collective-permute-start | bytes 1572872 | tf_op jit(solution)/shard_map/ppermute | solution.py:194
  49.2 0.0 collective-permute-done.3.near_7
  49.2 3.2 %all-to-all-done.1 = f32[16,16,128]{2,1,0:T(8,128)S(1)} async-done(((f32[16,16,128]{2,1,0:T(8,128)}), f32[16,16,128]{2,1,0:T(8,128)S(1)}, u32[]{:S(2)}, u32[]{:S(2)}) %all-to-all-start.1) | async-done | bytes 131104 | tf_op jit(solution)/shard_map/all_to_all | solution.py:213
  52.4 0.8 %shard_map.58 = bf16[16,5,2,8,128]{4,3,2,1,0:T(8,128)(2,1)} custom-call(f32[16,2,8,128]{3,2,1,0:T(8,128)S(1)} %bitcast.11, bf16[16,5,2,8,128]{4,3,2,1,0:T(8,128)(2,1)S(1)} %bitcast.10, bf16[2,128,256]{2,1,0:T(8,128)(2,1)S(1)} %collective-permute-done.3.near_7), custom_call_target="tpu_custom_call" | custom-call | flops 2000000000 | bytes 655360 | tf_op jit(solution)/shard_map/pallas_call | solution.py:249
  53.2 0.0 copy-done.6
  53.2 4.0 %all-to-all-start.2 = ((bf16[16,80,128]{2,1,0:T(8,128)(2,1)}), bf16[16,80,128]{2,1,0:T(8,128)(2,1)S(1)}, u32[]{:S(2)}, u32[]{:S(2)}) async-start(bf16[16,80,128]{2,1,0:T(8,128)(2,1)} %bitcast.4), calls=%async_computation.2 | async-start | bytes 655360 | tf_op jit(solution)/shard_map/all_to_all | solution.py:213
  57.2 4.2 %collective-permute-start.4 = (bf16[128,256]{1,0:T(8,128)(2,1)S(1)}, bf16[128,256]{1,0:T(8,128)(2,1)S(1)}, u32[]{:S(2)}, u32[]{:S(2)}) collective-permute-start(bf16[128,256]{1,0:T(8,128)(2,1)S(1)} %fusion), channel_id=1, source_target_pairs={{0,8},{4,12},{8,0},{12,4},{16,24},{20,28},{24,16},{28,20},{1,9},{5... | collective-permute-start | bytes 196616 | tf_op jit(solution)/shard_map/ppermute | solution.py:194
  61.4 0.0 collective-permute-done.6.by_both
  61.4 0.0 copy-start.8
  61.4 0.8 %copy-done.8 = bf16[2,256,512]{2,1,0:T(8,128)(2,1)} copy-done((bf16[2,256,512]{2,1,0:T(8,128)(2,1)}, bf16[2,256,512]{2,1,0:T(8,128)(2,1)S(1)}, u32[]{:S(2)}) %copy-start.8) | copy-done | bytes 524312
  62.2 0.0 copy-done.10
  62.2 1.0 %copy-done.4 = bf16[2,256,512]{2,1,0:T(8,128)(2,1)S(1)} copy-done((bf16[2,256,512]{2,1,0:T(8,128)(2,1)S(1)}, bf16[2,256,512]{2,1,0:T(8,128)(2,1)}, u32[]{:S(2)}) %copy-start.4) | copy-done | bytes 524312
  63.3 1.2 %copy-done.5 = bf16[2,256,1024]{2,1,0:T(8,128)(2,1)S(1)} copy-done((bf16[2,256,1024]{2,1,0:T(8,128)(2,1)S(1)}, bf16[2,256,1024]{2,1,0:T(8,128)(2,1)}, u32[]{:S(2)}) %copy-start.5) | copy-done | bytes 1048600
  64.5 1.0 %copy-done.7 = bf16[2,256,512]{2,1,0:T(8,128)(2,1)S(1)} copy-done((bf16[2,256,512]{2,1,0:T(8,128)(2,1)S(1)}, bf16[2,256,512]{2,1,0:T(8,128)(2,1)}, u32[]{:S(2)}) %copy-start.7) | copy-done | bytes 524312
  65.5 1.0 %copy-done.9 = bf16[2,256,512]{2,1,0:T(8,128)(2,1)S(1)} copy-done((bf16[2,256,512]{2,1,0:T(8,128)(2,1)S(1)}, bf16[2,256,512]{2,1,0:T(8,128)(2,1)}, u32[]{:S(2)}) %copy-start.9) | copy-done | bytes 524312
  66.6 2.2 %shard_map.59 = (f32[2,256,512]{2,1,0:T(8,128)S(1)}, bf16[2,256,1024]{2,1,0:T(8,128)(2,1)S(1)}) custom-call(s32[510]{0:T(512)S(1)} %copy-done.10, bf16[2,256,1024]{2,1,0:T(8,128)(2,1)S(1)} %copy-done.5, bf16[2,256,512]{2,1,0:T(8,128)(2,1)S(1)} %copy-done.2, bf16[2,256,512]{2,1,0:T(8,128)(2,1)S(1)} %copy-done.4, bf16[2,256,512]{2,1,0:T(8,128)(2,1)S(1)} %copy-done.7, ...), custom_call_target="tpu_custom_call" | custom-call | flops 3000000000 | bytes 6291456 | tf_op jit(solution)/shard_map/pallas_call | solution.py:257
  68.8 0.0 collective-permute-done.4.near_6
  68.8 0.0 all-to-all-done.2
  68.8 0.1 shard_map.60.coef
  68.9 5.8 %collective-permute-start.7 = (bf16[1152,256]{1,0:T(8,128)(2,1)S(1)}, bf16[1152,256]{1,0:T(8,128)(2,1)S(1)}, u32[]{:S(2)}, u32[]{:S(2)}) collective-permute-start(bf16[1152,256]{1,0:T(8,128)(2,1)S(1)} %shard_map.60.coef), channel_id=1, source_target_pairs={{0,1},{1,0},{2,3},{3,2},{4,5},{5,4},{6,7},{7,6},{8,9},{9,8},{10,11... | collective-permute-start | bytes 1769480 | tf_op jit(solution)/shard_map/ppermute | solution.py:194
  74.7 1.2 %shard_map.61.begun = bf16[2,256,512]{2,1,0:T(8,128)(2,1)} custom-call(bf16[1152,256]{1,0:T(8,128)(2,1)S(1)} %shard_map.60.coef, bf16[2,256,1024]{2,1,0:T(8,128)(2,1)S(1)} %get-tuple-element.12.left, f32[2,256,512]{2,1,0:T(8,128)S(1)} %get-tuple-element.11.late.dense), custom_call_target="tpu_custom_call" | custom-call | flops 268435456 | bytes 2686976 | tf_op jit(solution)/shard_map/pallas_call | solution.py:276
  75.9 0.4 collective-permute-done.7.coef
  76.4 1.2 %shard_map.62 = bf16[2,256,512]{2,1,0:T(8,128)(2,1)} custom-call(bf16[1152,256]{1,0:T(8,128)(2,1)S(1)} %collective-permute-done.7.coef, bf16[2,256,1024]{2,1,0:T(8,128)(2,1)S(1)} %get-tuple-element.12.left, f32[2,256,512]{2,1,0:T(8,128)S(1)} %get-tuple-element.11.late.dense, bf16[2,256,512]{2,1,0:T(8,128)(2,1)} %shard_map.61.begun), custom_call_target="tpu_custom_call", output_to_operand_aliasing={{}: (3, {})} | custom-call | flops 268435456 | bytes 2686976 | tf_op jit(solution)/shard_map/pallas_call | solution.py:285
  (7 shorter events, 0.0 us)
Async XLA Ops:
  0.0 13.5 %collective-permute-start = (bf16[8,2,256,128]{3,2,1,0:T(8,128)(2,1)}, bf16[8,2,256,128]{3,2,1,0:T(8,128)(2,1)S(1)}, u32[]{:S(2)}, u32[]{:S(2)}) collective-permute-start(bf16[8,2,256,128]{3,2,1,0:T(8,128)(2,1)} %basis.2), channel_id=1, source_target_pairs={{0,1},{1,0},{2,3},{3,2},{4,5},{5,4},{6,7},{7,6},{8,9},{9,8},{10,11... | collective-permute-start | bytes 3145736 | tf_op jit(solution)/shard_map/ppermute | solution.py:194
  8.8 4.7 %collective-permute-start.1 = (bf16[2,256,512]{2,1,0:T(8,128)(2,1)}, bf16[2,256,512]{2,1,0:T(8,128)(2,1)S(1)}, u32[]{:S(2)}, u32[]{:S(2)}) collective-permute-start(bf16[2,256,512]{2,1,0:T(8,128)(2,1)} %own.1), channel_id=1, source_target_pairs={{0,1},{1,0},{2,3},{3,2},{4,5},{5,4},{6,7},{7,6},{8,9},{9,8},{10,11... | collective-permute-start | bytes 1572872 | tf_op jit(solution)/shard_map/ppermute | solution.py:194
  10.7 1.2 %copy-start = (bf16[8,2,256,128]{3,2,1,0:T(8,128)(2,1)S(1)}, bf16[8,2,256,128]{3,2,1,0:T(8,128)(2,1)}, u32[]{:S(2)}) copy-start(bf16[8,2,256,128]{3,2,1,0:T(8,128)(2,1)} %basis.2) | copy-start | bytes 3145732
  11.9 1.0 %copy-start.1 = (bf16[2,256,512]{2,1,0:T(8,128)(2,1)S(1)}, bf16[2,256,512]{2,1,0:T(8,128)(2,1)}, u32[]{:S(2)}) copy-start(bf16[2,256,512]{2,1,0:T(8,128)(2,1)} %own.1) | copy-start | bytes 1572868
  13.5 10.2 %copy-start.2 = (bf16[2,256,512]{2,1,0:T(8,128)(2,1)S(1)}, bf16[2,256,512]{2,1,0:T(8,128)(2,1)}, u32[]{:S(2)}) copy-start(bf16[2,256,512]{2,1,0:T(8,128)(2,1)} %own.1) | copy-start | bytes 1572868
  13.5 1.2 %copy-start.3 = (bf16[2,256,512]{2,1,0:T(8,128)(2,1)}, bf16[2,256,512]{2,1,0:T(8,128)(2,1)S(1)}, u32[]{:S(2)}) copy-start(bf16[2,256,512]{2,1,0:T(8,128)(2,1)S(1)} %collective-permute-done.1.sides.by_core) | copy-start | bytes 1572868
  14.7 17.9 %all-to-all-start = ((bf16[16,80,128]{2,1,0:T(8,128)(2,1)}), bf16[16,80,128]{2,1,0:T(8,128)(2,1)S(1)}, u32[]{:S(2)}, u32[]{:S(2)}) async-start(bf16[16,80,128]{2,1,0:T(8,128)(2,1)} %bitcast), calls=%async_computation | async-start | bytes 655360 | tf_op jit(solution)/shard_map/all_to_all | solution.py:213
  20.4 22.0 %collective-permute-start.2 = (bf16[4,128,256]{2,1,0:T(8,128)(2,1)S(1)}, bf16[4,128,256]{2,1,0:T(8,128)(2,1)S(1)}, u32[]{:S(2)}, u32[]{:S(2)}) collective-permute-start(bf16[4,128,256]{2,1,0:T(8,128)(2,1)S(1)} %get-tuple-element.10), channel_id=1, source_target_pairs={{0,2},{2,0},{1,3},{3,1},{4,6},{6,4},{5,7},{7,5},{8,10},{10,8},{9,1... | collective-permute-start | bytes 786440 | tf_op jit(solution)/shard_map/ppermute | solution.py:194
  23.7 21.6 %collective-permute-start.5 = (bf16[2,256,512]{2,1,0:T(8,128)(2,1)S(1)}, bf16[2,256,512]{2,1,0:T(8,128)(2,1)S(1)}, u32[]{:S(2)}, u32[]{:S(2)}) collective-permute-start(bf16[2,256,512]{2,1,0:T(8,128)(2,1)S(1)} %copy-done.2), channel_id=1, source_target_pairs={{0,2},{2,0},{1,3},{3,1},{4,6},{6,4},{5,7},{7,5},{8,10},{10,8},{9,1... | collective-permute-start | bytes 1572872 | tf_op jit(solution)/shard_map/ppermute | solution.py:194
  33.3 19.1 %all-to-all-start.1 = ((f32[16,16,128]{2,1,0:T(8,128)}), f32[16,16,128]{2,1,0:T(8,128)S(1)}, u32[]{:S(2)}, u32[]{:S(2)}) async-start(f32[16,16,128]{2,1,0:T(8,128)} %bitcast.2), calls=%async_computation.1 | async-start | bytes 262144 | tf_op jit(solution)/shard_map/all_to_all | solution.py:213
  42.5 6.7 %collective-permute-start.3 = (bf16[2,128,256]{2,1,0:T(8,128)(2,1)S(1)}, bf16[2,128,256]{2,1,0:T(8,128)(2,1)S(1)}, u32[]{:S(2)}, u32[]{:S(2)}) collective-permute-start(bf16[2,128,256]{2,1,0:T(8,128)(2,1)S(1)} %slice.12), channel_id=1, source_target_pairs={{0,4},{4,0},{8,12},{12,8},{16,20},{20,16},{24,28},{28,24},{1,5},{5... | collective-permute-start | bytes 393224 | tf_op jit(solution)/shard_map/ppermute | solution.py:194
  45.3 7.9 %copy-start.6 = (bf16[2,256,512]{2,1,0:T(8,128)(2,1)}, bf16[2,256,512]{2,1,0:T(8,128)(2,1)S(1)}, u32[]{:S(2)}) copy-start(bf16[2,256,512]{2,1,0:T(8,128)(2,1)S(1)} %collective-permute-done.5.by_chip) | copy-start | bytes 1572868
  45.3 16.1 %collective-permute-start.6 = (bf16[2,256,512]{2,1,0:T(8,128)(2,1)S(1)}, bf16[2,256,512]{2,1,0:T(8,128)(2,1)S(1)}, u32[]{:S(2)}, u32[]{:S(2)}) collective-permute-start(bf16[2,256,512]{2,1,0:T(8,128)(2,1)S(1)} %collective-permute-done.5.by_chip), channel_id=1, source_target_pairs={{0,1},{1,0},{2,3},{3,2},{4,5},{5,4},{6,7},{7,6},{8,9},{9,8},{10,11... | collective-permute-start | bytes 1572872 | tf_op jit(solution)/shard_map/ppermute | solution.py:194
  52.4 9.8 %copy-start.10 = (s32[510]{0:T(512)S(1)}, s32[510]{0:T(512)}, u32[]{:S(2)}) copy-start(s32[510]{0:T(512)} %ranks.1) | copy-start | bytes 6124
  53.2 15.6 %all-to-all-start.2 = ((bf16[16,80,128]{2,1,0:T(8,128)(2,1)}), bf16[16,80,128]{2,1,0:T(8,128)(2,1)S(1)}, u32[]{:S(2)}, u32[]{:S(2)}) async-start(bf16[16,80,128]{2,1,0:T(8,128)(2,1)} %bitcast.4), calls=%async_computation.2 | async-start | bytes 655360 | tf_op jit(solution)/shard_map/all_to_all | solution.py:213
  57.2 11.6 %collective-permute-start.4 = (bf16[128,256]{1,0:T(8,128)(2,1)S(1)}, bf16[128,256]{1,0:T(8,128)(2,1)S(1)}, u32[]{:S(2)}, u32[]{:S(2)}) collective-permute-start(bf16[128,256]{1,0:T(8,128)(2,1)S(1)} %fusion), channel_id=1, source_target_pairs={{0,8},{4,12},{8,0},{12,4},{16,24},{20,28},{24,16},{28,20},{1,9},{5... | collective-permute-start | bytes 196616 | tf_op jit(solution)/shard_map/ppermute | solution.py:194
  61.4 0.8 %copy-start.8 = (bf16[2,256,512]{2,1,0:T(8,128)(2,1)}, bf16[2,256,512]{2,1,0:T(8,128)(2,1)S(1)}, u32[]{:S(2)}) copy-start(bf16[2,256,512]{2,1,0:T(8,128)(2,1)S(1)} %collective-permute-done.6.by_both) | copy-start | bytes 1572868
  62.2 1.0 %copy-start.4 = (bf16[2,256,512]{2,1,0:T(8,128)(2,1)S(1)}, bf16[2,256,512]{2,1,0:T(8,128)(2,1)}, u32[]{:S(2)}) copy-start(bf16[2,256,512]{2,1,0:T(8,128)(2,1)} %copy-done.3) | copy-start | bytes 1572868
  63.2 1.2 %copy-start.5 = (bf16[2,256,1024]{2,1,0:T(8,128)(2,1)S(1)}, bf16[2,256,1024]{2,1,0:T(8,128)(2,1)}, u32[]{:S(2)}) copy-start(bf16[2,256,1024]{2,1,0:T(8,128)(2,1)} %blocks.1) | copy-start | bytes 3145732
  64.5 1.0 %copy-start.7 = (bf16[2,256,512]{2,1,0:T(8,128)(2,1)S(1)}, bf16[2,256,512]{2,1,0:T(8,128)(2,1)}, u32[]{:S(2)}) copy-start(bf16[2,256,512]{2,1,0:T(8,128)(2,1)} %copy-done.6) | copy-start | bytes 1572868
  65.5 1.0 %copy-start.9 = (bf16[2,256,512]{2,1,0:T(8,128)(2,1)S(1)}, bf16[2,256,512]{2,1,0:T(8,128)(2,1)}, u32[]{:S(2)}) copy-start(bf16[2,256,512]{2,1,0:T(8,128)(2,1)} %copy-done.8) | copy-start | bytes 1572868
  68.9 7.4 %collective-permute-start.7 = (bf16[1152,256]{1,0:T(8,128)(2,1)S(1)}, bf16[1152,256]{1,0:T(8,128)(2,1)S(1)}, u32[]{:S(2)}, u32[]{:S(2)}) collective-permute-start(bf16[1152,256]{1,0:T(8,128)(2,1)S(1)} %shard_map.60.coef), channel_id=1, source_target_pairs={{0,1},{1,0},{2,3},{3,2},{4,5},{5,4},{6,7},{7,6},{8,9},{9,8},{10,11... | collective-permute-start | bytes 1769480 | tf_op jit(solution)/shard_map/ppermute | solution.py:194

commit v6 on v5

--- a/solution.py
+++ b/solution.py
@@ -101,20 +101,21 @@
         rounded = total.astype(BF16)
         for member in range(members):
             out[member, level] = rounded
+    ring = members // 2
     for side in range(2):
-        first = (1 - side) * members // 2
-        total = parts[first, bits].astype(F32)
-        for member in range(first + 1, first + members // 2):
+        sources = [z + chip * ring for chip in range(2) for z in range(ring) if z // (ring // 2) != side]
+        total = parts[sources[0], bits].astype(F32)
+        for member in sources[1:]:
             total = total + parts[member, bits].astype(F32)
         rounded = total.astype(BF16)
-        for member in range(side * members // 2, (side + 1) * members // 2):
-            out[member, bits] = rounded
-
-
-def dense_kernel(ranks, blocks, own, by_core, by_chip, by_both, basis, out, left):
+        for member in range(members):
+            if member not in sources:
+                out[member, bits] = rounded
+
+
+def dense_kernel(blocks, own, by_core, by_chip, by_both, out):
     leaves, rows, _ = blocks.shape
-    levels, _, _, rank = basis.shape
-    position, _, row, _ = place()
+    row = place()[2]
     for leaf in range(leaves):
         total = None
         for step, sides in enumerate((own, by_core, by_chip, by_both)):
@@ -124,55 +125,55 @@
             )
             total = term if total is None else total + term
         out[leaf] = total
-    columns = lax.broadcasted_iota(jnp.int32, (rows, rank), 1)
-    for level in range(levels):
-        for leaf in range(leaves):
-            if level < levels - 1:
-                heap = 2 ** (level + 1) - 2 + lax.shift_right_logical(position, levels - 2 - level)
-                slot = level + 1 - leaf
-            else:
-                heap = 2**levels - 2 + leaves * position + leaf
-                slot = level * leaf
-            kept = jnp.where(columns < ranks[heap], basis[level, leaf].astype(F32), 0.0)
-            left[leaf, :, slot * rank : (slot + 1) * rank] = kept.astype(BF16)
-
-
-def gather_kernel(wide, near_6, near_7, near, late, out):
+
+
+def gather_kernel(limits, wide, near_6, near_7, near, late, out):
     rank = wide.shape[0] * 8
     wide_levels, across = wide.shape[1:3]
+    upper = wide_levels + 2
+    rows = lax.broadcasted_iota(jnp.int32, (rank, 128), 0)
+
+    def put(row, slot, parts):
+        kept = rows < limits[slot, :1]
+        for col, part in enumerate(parts):
+            part = jnp.where(kept, part.astype(F32), 0.0).astype(BF16)
+            out[row : row + rank, col * 128 : (col + 1) * 128] = part
+
+    def halves(value):
+        return [value[:, col * 128 : (col + 1) * 128] for col in range(across)]
+
     for level in range(wide_levels):
-        for col in range(across):
-            part = wide[:, level, col].astype(F32).reshape(rank, 128).astype(BF16)
-            out[(1 + level) * rank : (2 + level) * rank, col * 128 : (col + 1) * 128] = part
-    row = (1 + wide_levels) * rank
-    out[:rank] = near[3]
-    for part in (near_6[...], near_7[1], near[2]):
-        out[row : row + rank] = part
-        row += rank
-
-
-def update(coef, left, dense, column, store):
-    leaves, _, depth = left.shape
+        parts = [wide[:, level, col].astype(F32).reshape(rank, 128) for col in range(across)]
+        put((1 + level) * rank, level, parts)
+    put((1 + wide_levels) * rank, wide_levels, halves(near_6[...]))
+    put(upper * rank, upper - 1, halves(near_7[1]))
+    put(0, upper, halves(near[3]))
+    put((1 + upper) * rank, upper + 1, halves(near[2]))
+
+
+def update(coef, basis, dense, column, store):
+    levels, leaves, _, rank = basis.shape
     half = coef.shape[1]
-    rank = coef.shape[0] - depth
     for leaf in range(leaves):
-        term = jnp.dot(
-            left[leaf], coef[leaf * rank : leaf * rank + depth], preferred_element_type=F32
-        )
+        order = list(range(levels - 1))
+        order = order + [levels - 1] if leaf else [levels - 1] + order
+        left = jnp.concatenate([basis[level, leaf] for level in order], axis=1)
+        right = coef[leaf * rank : (leaf + levels) * rank, :]
+        term = jnp.dot(left, right, preferred_element_type=F32)
         store(leaf, (dense[leaf, :, pl.ds(column, half)] + term).astype(BF16))
 
 
-def own_kernel(coef, left, dense, out, held, sems):
+def own_kernel(coef, basis, dense, out, held, sems):
     half = held.shape[2]
-    place_half(place()[1], coef, left, dense, out, held, sems, half)
-
-
-def last_kernel(coef, left, dense, begun, out, held, sems):
+    place_half(place()[1], coef, basis, dense, out, held, sems, half)
+
+
+def last_kernel(coef, basis, dense, begun, out, held, sems):
     half = held.shape[2]
-    place_half(1 - place()[1], coef, left, dense, out, held, sems, half)
-
-
-def place_half(index, coef, left, dense, out, held, sems, half):
+    place_half(1 - place()[1], coef, basis, dense, out, held, sems, half)
+
+
+def place_half(index, coef, basis, dense, out, held, sems, half):
     column = pl.multiple_of(index * half, half)
     copies = []
 
@@ -185,7 +186,7 @@
         )
         copies[-1].start()
 
-    update(coef, left, dense, column, store)
+    update(coef, basis, dense, column, store)
     for copy in copies:
         copy.wait()
 
@@ -213,6 +214,12 @@
         moved = lax.all_to_all(flat, axes, split_axis=0, concat_axis=0, tiled=True)
         return moved.reshape(block.shape)
 
+    position = ring * lax.axis_index("high") + lax.axis_index("z")
+    heaps = [2 ** (i + 1) - 2 + jnp.right_shift(position, upper - 1 - i) for i in range(upper)]
+    heaps += [2**levels - 2 + leaves * position + leaf for leaf in range(leaves)]
+    chosen = jnp.stack(heaps)[:, None] == jnp.arange(block_ranks.shape[0], dtype=jnp.int32)
+    limits = jnp.sum(jnp.where(chosen, block_ranks, 0), axis=1)
+    limits = jnp.broadcast_to(limits[:, None, None], (slots, 8, 128))
     basis_core = swap(basis_right, "core")
     by_core = swap(right_sides, "core")
     moved = 2 * (basis_right.size + right_sides.size) + 4 * slots * rank * half
@@ -232,7 +239,7 @@
         flops=flops,
         moved=2 * moved,
     )(basis_core, by_core, mine)
-    wide = exchange(wide, ("z", "chip"))
+    wide = exchange(wide, ("chip", "z"))
     near = (near.astype(F32) + swap(near, "chip").astype(F32)).astype(BF16)
     near_7 = swap(near[:2], "z", 1)
     near_6 = swap((near[0].astype(F32) + near_7[0].astype(F32)).astype(BF16), "z", 2)
@@ -253,23 +260,20 @@
         flops=LONG2,
         moved=4 * wide.size,
     )(from_high, wide, near_7)
-    wide = exchange(wide, ("z", "chip"))
-    dense, left = call(
+    wide = exchange(wide, ("chip", "z"))
+    dense = call(
         dense_kernel,
-        [
-            shape((leaves, rows, width), F32),
-            shape((leaves, rows, levels * rank), BF16),
-        ],
-        [SMEM] + [VMEM] * 6,
+        shape((leaves, rows, width), F32),
+        [VMEM] * 5,
         flops=LONG3,
-        moved=2 * leaf_blocks.size + 12 * right_sides.size + 4 * basis_left.size,
-    )(block_ranks, leaf_blocks, right_sides, by_core, by_chip, by_both, basis_left)
+        moved=2 * leaf_blocks.size + 12 * right_sides.size,
+    )(leaf_blocks, right_sides, by_core, by_chip, by_both)
     coef = call(
         gather_kernel,
         shape((slots * rank, half), BF16),
-        [VMEM] * 4 + [ANY],
+        [VMEM] * 5 + [ANY],
         moved=4 * slots * rank * half,
-    )(wide, near_6, near_7, near, dense)
+    )(limits, wide, near_6, near_7, near, dense)
     coef_other = swap(coef, "core")
     held = [pltpu.VMEM((leaves, rows, half), BF16), pltpu.SemaphoreType.DMA((leaves,))]
     moved = 2 * (basis_left.size + coef.size) + 4 * right_sides.size
@@ -281,7 +285,7 @@
         whole=ANY,
         flops=flops,
         moved=moved,
-    )(coef, left, dense)
+    )(coef, basis_left, dense)
     return call(
         last_kernel,
         shape((leaves, rows, width), BF16),
@@ -291,7 +295,7 @@
         aliases={3: 0},
         flops=flops,
         moved=moved,
-    )(coef_other, left, dense, begun)
+    )(coef_other, basis_left, dense, begun)
 
 
 def solution(mesh):

time: 78.4 us -> 75.9 us (0.968)
  starting transfers between devices: 51.4 us -> 55.8 us
  waiting for transfers between devices: 10.5 us -> 7.02 us
  local copies, waits for them, and re-layouts: 7.43 us -> 5.49 us
  Pallas kernels: 7.77 us -> 6.3 us
    all_to_all x3, waiting for transfers between devices: 10.1 us -> 6.57 us  [exchange(): moved = lax.all_to_all(flat, axes, split_axis=0, concat_axis=0, tiled=True)]
    ppermute x8, starting transfers between devices: 32.6 us -> 36 us  [swap(): lax.ppermute(block, axis, [(i, i ^ bit) for i in range(lax.axis_size(axis...]
    unnamed x22 -> x16, local copies, waits for them, and re-layouts: 7.42 us -> 5.33 us
    pallas_call x2, Pallas kernels: 2.31 us -> 0.84 us  [the longest x1 0.7 us: local(): call(dense_kernel, shape((leaves, rows, width), F32), [VMEM] * 5, flops=L...]
    all_to_all x3, starting transfers between devices: 18.8 us -> 19.8 us  [exchange(): moved = lax.all_to_all(flat, axes, split_axis=0, concat_axis=0, tiled=True)]
  transfers between devices with their start and end apart: 11 -> 11, of which waited for: 3 -> 3; matrix products, arithmetic and copies ran while one was open for 0% -> 0% of each run, Pallas kernels for 7% -> 5%
where the time goes in v6:
time: 75.9 us; the launch traced here: 75.1 us
  starting transfers between devices  55.8 us (74%)
  waiting for transfers between devices  7.02 us (9%)
  Pallas kernels  6.3 us (8%)
  local copies, waits for them, and re-layouts  5.49 us (7%)
    ppermute x8, starting transfers between devices, swap(): lax.ppermute(block, axis, [(i, i ^ bit) for i in range(lax.axis_size(axis...  36 us
    all_to_all x3, starting transfers between devices, exchange(): moved = lax.all_to_all(flat, axes, split_axis=0, concat_axis=0, tiled=True)  19.8 us
    all_to_all x3, waiting for transfers between devices, exchange(): moved = lax.all_to_all(flat, axes, split_axis=0, concat_axis=0, tiled=True)  6.57 us
    unnamed x16, local copies, waits for them, and re-layouts  5.33 us
  transfers between devices with their start and end apart: 11, of which 3 were waited for; matrix products, arithmetic and copies ran while one was open for 0% of the time, Pallas kernels for 5%

profile of v6, /device:TPU:1, one launch (start us, length us, event | category | flops | bytes accessed | tf_op | source)
XLA Modules:
  0.0 75.1 jit_solution(11739459772980112292)
XLA Ops:
  0.0 8.8 %collective-permute-start = (bf16[8,2,256,128]{3,2,1,0:T(8,128)(2,1)}, bf16[8,2,256,128]{3,2,1,0:T(8,128)(2,1)S(1)}, u32[]{:S(2)}, u32[]{:S(2)}) collective-permute-start(bf16[8,2,256,128]{3,2,1,0:T(8,128)(2,1)} %basis.3), channel_id=1, source_target_pairs={{0,1},{1,0},{2,3},{3,2},{4,5},{5,4},{6,7},{7,6},{8,9},{9,8},{10,11... | collective-permute-start | bytes 3145736 | tf_op jit(solution)/shard_map/ppermute | solution.py:195
  8.8 1.9 %collective-permute-start.1 = (bf16[2,256,512]{2,1,0:T(8,128)(2,1)}, bf16[2,256,512]{2,1,0:T(8,128)(2,1)S(1)}, u32[]{:S(2)}, u32[]{:S(2)}) collective-permute-start(bf16[2,256,512]{2,1,0:T(8,128)(2,1)} %own.1), channel_id=1, source_target_pairs={{0,1},{1,0},{2,3},{3,2},{4,5},{5,4},{6,7},{7,6},{8,9},{9,8},{10,11... | collective-permute-start | bytes 1572872 | tf_op jit(solution)/shard_map/ppermute | solution.py:195
  10.7 0.0 copy-start.1
  10.7 1.2 %copy-done.1 = bf16[8,2,256,128]{3,2,1,0:T(8,128)(2,1)S(1)} copy-done((bf16[8,2,256,128]{3,2,1,0:T(8,128)(2,1)S(1)}, bf16[8,2,256,128]{3,2,1,0:T(8,128)(2,1)}, u32[]{:S(2)}) %copy-start.1) | copy-done | bytes 1048600
  11.9 0.0 copy-start.2
  11.9 1.0 %copy-done.2 = bf16[2,256,512]{2,1,0:T(8,128)(2,1)S(1)} copy-done((bf16[2,256,512]{2,1,0:T(8,128)(2,1)S(1)}, bf16[2,256,512]{2,1,0:T(8,128)(2,1)}, u32[]{:S(2)}) %copy-start.2) | copy-done | bytes 524312
  13.0 0.5 shard_map.55.mine
  13.5 0.0 copy-start.3
  13.5 0.0 collective-permute-done.1.sides.by_core
  13.5 0.0 collective-permute-done.basis
  13.5 1.2 %shard_map.56 = (bf16[16,5,2,8,128]{4,3,2,1,0:T(8,128)(2,1)}, bf16[4,128,256]{2,1,0:T(8,128)(2,1)S(1)}) custom-call(bf16[8,2,256,128]{3,2,1,0:T(8,128)(2,1)S(1)} %collective-permute-done.basis, bf16[2,256,512]{2,1,0:T(8,128)(2,1)S(1)} %collective-permute-done.1.sides.by_core, f32[9,128,256]{2,1,0:T(8,128)S(1)} %shard_map.55.mine), custom_call_target="tpu_custom_call" | custom-call | flops 268435456 | bytes 5505024 | tf_op jit(solution)/shard_map/pallas_call | solution.py:235
  14.7 5.7 %all-to-all-start = ((bf16[16,80,128]{2,1,0:T(8,128)(2,1)}), bf16[16,80,128]{2,1,0:T(8,128)(2,1)S(1)}, u32[]{:S(2)}, u32[]{:S(2)}) async-start(bf16[16,80,128]{2,1,0:T(8,128)(2,1)} %bitcast.9), calls=%async_computation | async-start | bytes 655360 | tf_op jit(solution)/shard_map/all_to_all | solution.py:214
  20.4 3.3 %collective-permute-start.2 = (bf16[4,128,256]{2,1,0:T(8,128)(2,1)S(1)}, bf16[4,128,256]{2,1,0:T(8,128)(2,1)S(1)}, u32[]{:S(2)}, u32[]{:S(2)}) collective-permute-start(bf16[4,128,256]{2,1,0:T(8,128)(2,1)S(1)} %get-tuple-element.8), channel_id=1, source_target_pairs={{0,2},{2,0},{1,3},{3,1},{4,6},{6,4},{5,7},{7,5},{8,10},{10,8},{9,1... | collective-permute-start | bytes 786440 | tf_op jit(solution)/shard_map/ppermute | solution.py:195
  23.6 0.0 copy-done.3
  23.7 2.0 %collective-permute-start.5 = (bf16[2,256,512]{2,1,0:T(8,128)(2,1)S(1)}, bf16[2,256,512]{2,1,0:T(8,128)(2,1)S(1)}, u32[]{:S(2)}, u32[]{:S(2)}) collective-permute-start(bf16[2,256,512]{2,1,0:T(8,128)(2,1)S(1)} %copy-done.3), channel_id=1, source_target_pairs={{0,2},{2,0},{1,3},{3,1},{4,6},{6,4},{5,7},{7,5},{8,10},{10,8},{9,1... | collective-permute-start | bytes 1572872 | tf_op jit(solution)/shard_map/ppermute | solution.py:195
  25.7 4.9 %all-to-all-done = bf16[16,80,128]{2,1,0:T(8,128)(2,1)S(1)} async-done(((bf16[16,80,128]{2,1,0:T(8,128)(2,1)}), bf16[16,80,128]{2,1,0:T(8,128)(2,1)S(1)}, u32[]{:S(2)}, u32[]{:S(2)}) %all-to-all-start) | async-done | bytes 327712 | tf_op jit(solution)/shard_map/all_to_all | solution.py:214
  30.6 0.7 shard_map.57
  31.3 9.1 %all-to-all-start.1 = ((f32[16,16,128]{2,1,0:T(8,128)}), f32[16,16,128]{2,1,0:T(8,128)S(1)}, u32[]{:S(2)}, u32[]{:S(2)}) async-start(f32[16,16,128]{2,1,0:T(8,128)} %bitcast.11), calls=%async_computation.1 | async-start | bytes 262144 | tf_op jit(solution)/shard_map/all_to_all | solution.py:214
  40.4 0.0 collective-permute-done.2
  40.4 0.1 add_convert_fusion.near
  40.5 3.9 %collective-permute-start.3 = (bf16[2,128,256]{2,1,0:T(8,128)(2,1)S(1)}, bf16[2,128,256]{2,1,0:T(8,128)(2,1)S(1)}, u32[]{:S(2)}, u32[]{:S(2)}) collective-permute-start(bf16[2,128,256]{2,1,0:T(8,128)(2,1)S(1)} %slice.12), channel_id=1, source_target_pairs={{0,4},{4,0},{8,12},{12,8},{16,20},{20,16},{24,28},{28,24},{1,5},{5... | collective-permute-start | bytes 393224 | tf_op jit(solution)/shard_map/ppermute | solution.py:195
  44.4 0.1 stack.39
  44.5 0.0 collective-permute-done.5.by_chip
  44.5 4.2 %collective-permute-start.6 = (bf16[2,256,512]{2,1,0:T(8,128)(2,1)S(1)}, bf16[2,256,512]{2,1,0:T(8,128)(2,1)S(1)}, u32[]{:S(2)}, u32[]{:S(2)}) collective-permute-start(bf16[2,256,512]{2,1,0:T(8,128)(2,1)S(1)} %collective-permute-done.5.by_chip), channel_id=1, source_target_pairs={{0,1},{1,0},{2,3},{3,2},{4,5},{5,4},{6,7},{7,6},{8,9},{9,8},{10,11... | collective-permute-start | bytes 1572872 | tf_op jit(solution)/shard_map/ppermute | solution.py:195
  48.7 0.0 collective-permute-done.3.near_7
  48.7 1.7 %all-to-all-done.1 = f32[16,16,128]{2,1,0:T(8,128)S(1)} async-done(((f32[16,16,128]{2,1,0:T(8,128)}), f32[16,16,128]{2,1,0:T(8,128)S(1)}, u32[]{:S(2)}, u32[]{:S(2)}) %all-to-all-start.1) | async-done | bytes 131104 | tf_op jit(solution)/shard_map/all_to_all | solution.py:214
  50.4 0.0 copy-start.7
  50.4 0.8 %shard_map.58 = bf16[16,5,2,8,128]{4,3,2,1,0:T(8,128)(2,1)} custom-call(f32[16,2,8,128]{3,2,1,0:T(8,128)S(1)} %bitcast.20, bf16[16,5,2,8,128]{4,3,2,1,0:T(8,128)(2,1)S(1)} %bitcast.19, bf16[2,128,256]{2,1,0:T(8,128)(2,1)S(1)} %collective-permute-done.3.near_7), custom_call_target="tpu_custom_call" | custom-call | flops 2000000000 | bytes 655360 | tf_op jit(solution)/shard_map/pallas_call | solution.py:256
  51.1 5.0 %all-to-all-start.2 = ((bf16[16,80,128]{2,1,0:T(8,128)(2,1)}), bf16[16,80,128]{2,1,0:T(8,128)(2,1)S(1)}, u32[]{:S(2)}, u32[]{:S(2)}) async-start(bf16[16,80,128]{2,1,0:T(8,128)(2,1)} %bitcast.13), calls=%async_computation.2 | async-start | bytes 655360 | tf_op jit(solution)/shard_map/all_to_all | solution.py:214
  56.1 0.0 copy-done.7
  56.2 0.2 select_reduce_fusion
  56.4 4.2 %collective-permute-start.4 = (bf16[128,256]{1,0:T(8,128)(2,1)S(1)}, bf16[128,256]{1,0:T(8,128)(2,1)S(1)}, u32[]{:S(2)}, u32[]{:S(2)}) collective-permute-start(bf16[128,256]{1,0:T(8,128)(2,1)S(1)} %fusion), channel_id=1, source_target_pairs={{0,8},{4,12},{8,0},{12,4},{16,24},{20,28},{24,16},{28,20},{1,9},{5... | collective-permute-start | bytes 196616 | tf_op jit(solution)/shard_map/ppermute | solution.py:195
  60.5 0.0 collective-permute-done.6.by_both
  60.6 0.0 copy-start.5
  60.6 0.8 %copy-done.5 = bf16[2,256,512]{2,1,0:T(8,128)(2,1)} copy-done((bf16[2,256,512]{2,1,0:T(8,128)(2,1)}, bf16[2,256,512]{2,1,0:T(8,128)(2,1)S(1)}, u32[]{:S(2)}) %copy-start.5) | copy-done | bytes 524312
  61.3 0.0 copy-start.4
  61.4 1.2 %copy-done.4 = bf16[2,256,1024]{2,1,0:T(8,128)(2,1)S(1)} copy-done((bf16[2,256,1024]{2,1,0:T(8,128)(2,1)S(1)}, bf16[2,256,1024]{2,1,0:T(8,128)(2,1)}, u32[]{:S(2)}) %copy-start.4) | copy-done | bytes 1048600
  62.6 1.0 %copy-done.6 = bf16[2,256,512]{2,1,0:T(8,128)(2,1)S(1)} copy-done((bf16[2,256,512]{2,1,0:T(8,128)(2,1)S(1)}, bf16[2,256,512]{2,1,0:T(8,128)(2,1)}, u32[]{:S(2)}) %copy-start.6) | copy-done | bytes 524312
  63.6 0.7 shard_map.59.late.dense
  64.3 0.0 collective-permute-done.4.near_6
  64.3 0.0 all-to-all-done.2
  64.3 0.1 broadcast_in_dim.18.limits
  64.4 0.1 shard_map.60.coef
  64.6 7.8 %collective-permute-start.7 = (bf16[1152,256]{1,0:T(8,128)(2,1)S(1)}, bf16[1152,256]{1,0:T(8,128)(2,1)S(1)}, u32[]{:S(2)}, u32[]{:S(2)}) collective-permute-start(bf16[1152,256]{1,0:T(8,128)(2,1)S(1)} %shard_map.60.coef), channel_id=1, source_target_pairs={{0,1},{1,0},{2,3},{3,2},{4,5},{5,4},{6,7},{7,6},{8,9},{9,8},{10,11... | collective-permute-start | bytes 1769480 | tf_op jit(solution)/shard_map/ppermute | solution.py:195
  72.4 0.0 copy-done
  72.4 1.2 %shard_map.61.begun = bf16[2,256,512]{2,1,0:T(8,128)(2,1)} custom-call(bf16[1152,256]{1,0:T(8,128)(2,1)S(1)} %shard_map.60.coef, bf16[8,2,256,128]{3,2,1,0:T(8,128)(2,1)S(1)} %copy-done, f32[2,256,512]{2,1,0:T(8,128)S(1)} %shard_map.59.late.dense), custom_call_target="tpu_custom_call" | custom-call | flops 268435456 | bytes 2686976 | tf_op jit(solution)/shard_map/pallas_call | solution.py:280
  73.5 0.4 collective-permute-done.7.coef
  74.0 1.2 %shard_map.62 = bf16[2,256,512]{2,1,0:T(8,128)(2,1)} custom-call(bf16[1152,256]{1,0:T(8,128)(2,1)S(1)} %collective-permute-done.7.coef, bf16[8,2,256,128]{3,2,1,0:T(8,128)(2,1)S(1)} %copy-done, f32[2,256,512]{2,1,0:T(8,128)S(1)} %shard_map.59.late.dense, bf16[2,256,512]{2,1,0:T(8,128)(2,1)} %shard_map.61.begun), custom_call_target="tpu_custom_call", output_to_operand_aliasing={{}: (3, {})} | custom-call | flops 268435456 | bytes 2686976 | tf_op jit(solution)/shard_map/pallas_call | solution.py:289
  (4 shorter events, 0.0 us)
Async XLA Ops:
  0.0 13.5 %collective-permute-start = (bf16[8,2,256,128]{3,2,1,0:T(8,128)(2,1)}, bf16[8,2,256,128]{3,2,1,0:T(8,128)(2,1)S(1)}, u32[]{:S(2)}, u32[]{:S(2)}) collective-permute-start(bf16[8,2,256,128]{3,2,1,0:T(8,128)(2,1)} %basis.3), channel_id=1, source_target_pairs={{0,1},{1,0},{2,3},{3,2},{4,5},{5,4},{6,7},{7,6},{8,9},{9,8},{10,11... | collective-permute-start | bytes 3145736 | tf_op jit(solution)/shard_map/ppermute | solution.py:195
  8.8 4.7 %collective-permute-start.1 = (bf16[2,256,512]{2,1,0:T(8,128)(2,1)}, bf16[2,256,512]{2,1,0:T(8,128)(2,1)S(1)}, u32[]{:S(2)}, u32[]{:S(2)}) collective-permute-start(bf16[2,256,512]{2,1,0:T(8,128)(2,1)} %own.1), channel_id=1, source_target_pairs={{0,1},{1,0},{2,3},{3,2},{4,5},{5,4},{6,7},{7,6},{8,9},{9,8},{10,11... | collective-permute-start | bytes 1572872 | tf_op jit(solution)/shard_map/ppermute | solution.py:195
  10.7 1.2 %copy-start.1 = (bf16[8,2,256,128]{3,2,1,0:T(8,128)(2,1)S(1)}, bf16[8,2,256,128]{3,2,1,0:T(8,128)(2,1)}, u32[]{:S(2)}) copy-start(bf16[8,2,256,128]{3,2,1,0:T(8,128)(2,1)} %basis.3) | copy-start | bytes 3145732
  11.9 1.0 %copy-start.2 = (bf16[2,256,512]{2,1,0:T(8,128)(2,1)S(1)}, bf16[2,256,512]{2,1,0:T(8,128)(2,1)}, u32[]{:S(2)}) copy-start(bf16[2,256,512]{2,1,0:T(8,128)(2,1)} %own.1) | copy-start | bytes 1572868
  13.5 10.2 %copy-start.3 = (bf16[2,256,512]{2,1,0:T(8,128)(2,1)S(1)}, bf16[2,256,512]{2,1,0:T(8,128)(2,1)}, u32[]{:S(2)}) copy-start(bf16[2,256,512]{2,1,0:T(8,128)(2,1)} %own.1) | copy-start | bytes 1572868
  14.7 15.9 %all-to-all-start = ((bf16[16,80,128]{2,1,0:T(8,128)(2,1)}), bf16[16,80,128]{2,1,0:T(8,128)(2,1)S(1)}, u32[]{:S(2)}, u32[]{:S(2)}) async-start(bf16[16,80,128]{2,1,0:T(8,128)(2,1)} %bitcast.9), calls=%async_computation | async-start | bytes 655360 | tf_op jit(solution)/shard_map/all_to_all | solution.py:214
  20.4 20.0 %collective-permute-start.2 = (bf16[4,128,256]{2,1,0:T(8,128)(2,1)S(1)}, bf16[4,128,256]{2,1,0:T(8,128)(2,1)S(1)}, u32[]{:S(2)}, u32[]{:S(2)}) collective-permute-start(bf16[4,128,256]{2,1,0:T(8,128)(2,1)S(1)} %get-tuple-element.8), channel_id=1, source_target_pairs={{0,2},{2,0},{1,3},{3,1},{4,6},{6,4},{5,7},{7,5},{8,10},{10,8},{9,1... | collective-permute-start | bytes 786440 | tf_op jit(solution)/shard_map/ppermute | solution.py:195
  23.7 20.8 %collective-permute-start.5 = (bf16[2,256,512]{2,1,0:T(8,128)(2,1)S(1)}, bf16[2,256,512]{2,1,0:T(8,128)(2,1)S(1)}, u32[]{:S(2)}, u32[]{:S(2)}) collective-permute-start(bf16[2,256,512]{2,1,0:T(8,128)(2,1)S(1)} %copy-done.3), channel_id=1, source_target_pairs={{0,2},{2,0},{1,3},{3,1},{4,6},{6,4},{5,7},{7,5},{8,10},{10,8},{9,1... | collective-permute-start | bytes 1572872 | tf_op jit(solution)/shard_map/ppermute | solution.py:195
  31.3 19.1 %all-to-all-start.1 = ((f32[16,16,128]{2,1,0:T(8,128)}), f32[16,16,128]{2,1,0:T(8,128)S(1)}, u32[]{:S(2)}, u32[]{:S(2)}) async-start(f32[16,16,128]{2,1,0:T(8,128)} %bitcast.11), calls=%async_computation.1 | async-start | bytes 262144 | tf_op jit(solution)/shard_map/all_to_all | solution.py:214
  40.5 8.2 %collective-permute-start.3 = (bf16[2,128,256]{2,1,0:T(8,128)(2,1)S(1)}, bf16[2,128,256]{2,1,0:T(8,128)(2,1)S(1)}, u32[]{:S(2)}, u32[]{:S(2)}) collective-permute-start(bf16[2,128,256]{2,1,0:T(8,128)(2,1)S(1)} %slice.12), channel_id=1, source_target_pairs={{0,4},{4,0},{8,12},{12,8},{16,20},{20,16},{24,28},{28,24},{1,5},{5... | collective-permute-start | bytes 393224 | tf_op jit(solution)/shard_map/ppermute | solution.py:195
  44.5 16.0 %collective-permute-start.6 = (bf16[2,256,512]{2,1,0:T(8,128)(2,1)S(1)}, bf16[2,256,512]{2,1,0:T(8,128)(2,1)S(1)}, u32[]{:S(2)}, u32[]{:S(2)}) collective-permute-start(bf16[2,256,512]{2,1,0:T(8,128)(2,1)S(1)} %collective-permute-done.5.by_chip), channel_id=1, source_target_pairs={{0,1},{1,0},{2,3},{3,2},{4,5},{5,4},{6,7},{7,6},{8,9},{9,8},{10,11... | collective-permute-start | bytes 1572872 | tf_op jit(solution)/shard_map/ppermute | solution.py:195
  50.4 5.8 %copy-start.7 = (s32[510]{0:T(512)S(1)}, s32[510]{0:T(512)}, u32[]{:S(2)}) copy-start(s32[510]{0:T(512)} %param.9) | copy-start | bytes 6124
  51.1 13.2 %all-to-all-start.2 = ((bf16[16,80,128]{2,1,0:T(8,128)(2,1)}), bf16[16,80,128]{2,1,0:T(8,128)(2,1)S(1)}, u32[]{:S(2)}, u32[]{:S(2)}) async-start(bf16[16,80,128]{2,1,0:T(8,128)(2,1)} %bitcast.13), calls=%async_computation.2 | async-start | bytes 655360 | tf_op jit(solution)/shard_map/all_to_all | solution.py:214
  56.4 8.0 %collective-permute-start.4 = (bf16[128,256]{1,0:T(8,128)(2,1)S(1)}, bf16[128,256]{1,0:T(8,128)(2,1)S(1)}, u32[]{:S(2)}, u32[]{:S(2)}) collective-permute-start(bf16[128,256]{1,0:T(8,128)(2,1)S(1)} %fusion), channel_id=1, source_target_pairs={{0,8},{4,12},{8,0},{12,4},{16,24},{20,28},{24,16},{28,20},{1,9},{5... | collective-permute-start | bytes 196616 | tf_op jit(solution)/shard_map/ppermute | solution.py:195
  60.6 0.8 %copy-start.5 = (bf16[2,256,512]{2,1,0:T(8,128)(2,1)}, bf16[2,256,512]{2,1,0:T(8,128)(2,1)S(1)}, u32[]{:S(2)}) copy-start(bf16[2,256,512]{2,1,0:T(8,128)(2,1)S(1)} %collective-permute-done.6.by_both) | copy-start | bytes 1572868
  61.3 1.2 %copy-start.4 = (bf16[2,256,1024]{2,1,0:T(8,128)(2,1)S(1)}, bf16[2,256,1024]{2,1,0:T(8,128)(2,1)}, u32[]{:S(2)}) copy-start(bf16[2,256,1024]{2,1,0:T(8,128)(2,1)} %blocks.1) | copy-start | bytes 3145732
  62.6 1.0 %copy-start.6 = (bf16[2,256,512]{2,1,0:T(8,128)(2,1)S(1)}, bf16[2,256,512]{2,1,0:T(8,128)(2,1)}, u32[]{:S(2)}) copy-start(bf16[2,256,512]{2,1,0:T(8,128)(2,1)} %copy-done.5) | copy-start | bytes 1572868
  64.4 7.9 %copy-start = (bf16[8,2,256,128]{3,2,1,0:T(8,128)(2,1)S(1)}, bf16[8,2,256,128]{3,2,1,0:T(8,128)(2,1)}, u32[]{:S(2)}) copy-start(bf16[8,2,256,128]{3,2,1,0:T(8,128)(2,1)} %basis.5) | copy-start | bytes 3145732
  64.6 9.4 %collective-permute-start.7 = (bf16[1152,256]{1,0:T(8,128)(2,1)S(1)}, bf16[1152,256]{1,0:T(8,128)(2,1)S(1)}, u32[]{:S(2)}, u32[]{:S(2)}) collective-permute-start(bf16[1152,256]{1,0:T(8,128)(2,1)S(1)} %shard_map.60.coef), channel_id=1, source_target_pairs={{0,1},{1,0},{2,3},{3,2},{4,5},{5,4},{6,7},{7,6},{8,9},{9,8},{10,11... | collective-permute-start | bytes 1769480 | tf_op jit(solution)/shard_map/ppermute | solution.py:195

commit v7 on v6

--- a/solution.py
+++ b/solution.py
@@ -36,7 +36,7 @@
 
 
 def place():
-    high, chip, core = (lax.axis_index(axis) for axis in ("high", "chip", "core"))
+    high, chip, core = (lax.axis_index(axis) for axis in (("y", "far"), "chip", "core"))
     return lax.axis_size("z") * high + lax.axis_index("z"), core, 2 * chip + core, high
 
 
@@ -75,6 +75,10 @@
             wide[:, slot, col] = part.reshape(down, 8, 128).astype(BF16)
 
 
+def far_major(high, count):
+    return (high & 1) * (count // 2) + (high >> 1)
+
+
 def ring_kernel(parts, out):
     high = place()[3]
     bits = out.shape[0].bit_length() - 1
@@ -83,9 +87,9 @@
         for member in range(parts.shape[0]):
             part = parts[member, level].astype(F32)
             total[level] = part if total[level] is None else total[level] + part
-    out[high] = jnp.zeros(out.shape[1:], F32)
+    out[far_major(high, out.shape[0])] = jnp.zeros(out.shape[1:], F32)
     for step in range(1, out.shape[0]):
-        out[jnp.bitwise_xor(high, step)] = total[bits - step.bit_length()]
+        out[far_major(high ^ step, out.shape[0])] = total[bits - step.bit_length()]
 
 
 def back_kernel(high_parts, parts, near_7, out):
@@ -95,9 +99,9 @@
     members = out.shape[0]
     for level in range(bits):
         first = 1 << (bits - 1 - level)
-        total = high_parts[jnp.bitwise_xor(high, first)]
+        total = high_parts[far_major(high ^ first, steps)]
         for step in range(first + 1, 2 * first):
-            total = total + high_parts[jnp.bitwise_xor(high, step)]
+            total = total + high_parts[far_major(high ^ step, steps)]
         rounded = total.astype(BF16)
         for member in range(members):
             out[member, level] = rounded
@@ -201,7 +205,7 @@
     half = width // 2
     upper = levels - 1
     ring = lax.axis_size("z")
-    highs = lax.axis_size("high")
+    highs = lax.axis_size(("y", "far"))
     wide_levels = levels - 3
     owners = 2 * ring
     shape = jax.ShapeDtypeStruct
@@ -214,7 +218,7 @@
         moved = lax.all_to_all(flat, axes, split_axis=0, concat_axis=0, tiled=True)
         return moved.reshape(block.shape)
 
-    position = ring * lax.axis_index("high") + lax.axis_index("z")
+    position = ring * lax.axis_index(("y", "far")) + lax.axis_index("z")
     heaps = [2 ** (i + 1) - 2 + jnp.right_shift(position, upper - 1 - i) for i in range(upper)]
     heaps += [2**levels - 2 + leaves * position + leaf for leaf in range(leaves)]
     chosen = jnp.stack(heaps)[:, None] == jnp.arange(block_ranks.shape[0], dtype=jnp.int32)
@@ -250,7 +254,7 @@
         flops=LONG,
         moved=2 * wide.size,
     )(wide)
-    from_high = exchange(to_high, ("high",))
+    from_high = exchange(to_high, ("far", "y"))
     by_chip = swap(right_sides, "chip")
     by_both = swap(by_chip, "core")
     wide = call(
@@ -302,9 +306,10 @@
     clusters = mesh.shape["clus"]
     ring = 8
     fine = Mesh(
-        mesh.devices.reshape(clusters // ring, ring, 2, 2), ("high", "z", "chip", "core")
+        mesh.devices.reshape(clusters // (2 * ring), 2, ring, 2, 2),
+        ("y", "far", "z", "chip", "core"),
     )
-    places, rows = ("high", "z"), ("chip", "core")
+    places, rows = ("y", "far", "z"), ("chip", "core")
     in_specs = (
         P(places, rows, None),
         P(places, rows, None),

time: 75.9 us -> 75 us (0.988)
  waiting for transfers between devices: 7.02 us -> 5.97 us
    all_to_all x3, waiting for transfers between devices: 6.57 us -> 5.52 us  [exchange(): moved = lax.all_to_all(flat, axes, split_axis=0, concat_axis=0, tiled=True)]
where the time goes in v7:
time: 75 us; the launch traced here: 74.3 us
  starting transfers between devices  56 us (75%)
  Pallas kernels  6.3 us (8%)
  waiting for transfers between devices  5.97 us (8%)
  local copies, waits for them, and re-layouts  5.49 us (7%)
    ppermute x8, starting transfers between devices, swap(): lax.ppermute(block, axis, [(i, i ^ bit) for i in range(lax.axis_size(axis...  36.1 us
    all_to_all x3, starting transfers between devices, exchange(): moved = lax.all_to_all(flat, axes, split_axis=0, concat_axis=0, tiled=True)  19.8 us
    all_to_all x3, waiting for transfers between devices, exchange(): moved = lax.all_to_all(flat, axes, split_axis=0, concat_axis=0, tiled=True)  5.52 us
    unnamed x16, local copies, waits for them, and re-layouts  5.33 us
  transfers between devices with their start and end apart: 11, of which 3 were waited for; matrix products, arithmetic and copies ran while one was open for 0% of the time, Pallas kernels for 5%

profile of v7, /device:TPU:1, one launch (start us, length us, event | category | flops | bytes accessed | tf_op | source)
XLA Modules:
  0.0 74.3 jit_solution(16216993246109424201)
XLA Ops:
  0.0 8.8 %collective-permute-start = (bf16[8,2,256,128]{3,2,1,0:T(8,128)(2,1)}, bf16[8,2,256,128]{3,2,1,0:T(8,128)(2,1)S(1)}, u32[]{:S(2)}, u32[]{:S(2)}) collective-permute-start(bf16[8,2,256,128]{3,2,1,0:T(8,128)(2,1)} %basis.3), channel_id=1, source_target_pairs={{0,1},{1,0},{2,3},{3,2},{4,5},{5,4},{6,7},{7,6},{8,9},{9,8},{10,11... | collective-permute-start | bytes 3145736 | tf_op jit(solution)/shard_map/ppermute | solution.py:199
  8.8 1.9 %collective-permute-start.1 = (bf16[2,256,512]{2,1,0:T(8,128)(2,1)}, bf16[2,256,512]{2,1,0:T(8,128)(2,1)S(1)}, u32[]{:S(2)}, u32[]{:S(2)}) collective-permute-start(bf16[2,256,512]{2,1,0:T(8,128)(2,1)} %own.1), channel_id=1, source_target_pairs={{0,1},{1,0},{2,3},{3,2},{4,5},{5,4},{6,7},{7,6},{8,9},{9,8},{10,11... | collective-permute-start | bytes 1572872 | tf_op jit(solution)/shard_map/ppermute | solution.py:199
  10.7 0.0 copy-start.1
  10.7 1.2 %copy-done.1 = bf16[8,2,256,128]{3,2,1,0:T(8,128)(2,1)S(1)} copy-done((bf16[8,2,256,128]{3,2,1,0:T(8,128)(2,1)S(1)}, bf16[8,2,256,128]{3,2,1,0:T(8,128)(2,1)}, u32[]{:S(2)}) %copy-start.1) | copy-done | bytes 1048600
  11.9 1.0 %copy-done.2 = bf16[2,256,512]{2,1,0:T(8,128)(2,1)S(1)} copy-done((bf16[2,256,512]{2,1,0:T(8,128)(2,1)S(1)}, bf16[2,256,512]{2,1,0:T(8,128)(2,1)}, u32[]{:S(2)}) %copy-start.2) | copy-done | bytes 524312
  13.0 0.5 shard_map.55.mine
  13.5 0.0 copy-start.3
  13.5 0.0 collective-permute-done.1.sides.by_core
  13.5 0.0 collective-permute-done.basis
  13.5 1.2 %shard_map.56 = (bf16[16,5,2,8,128]{4,3,2,1,0:T(8,128)(2,1)}, bf16[4,128,256]{2,1,0:T(8,128)(2,1)S(1)}) custom-call(bf16[8,2,256,128]{3,2,1,0:T(8,128)(2,1)S(1)} %collective-permute-done.basis, bf16[2,256,512]{2,1,0:T(8,128)(2,1)S(1)} %collective-permute-done.1.sides.by_core, f32[9,128,256]{2,1,0:T(8,128)S(1)} %shard_map.55.mine), custom_call_target="tpu_custom_call" | custom-call | flops 268435456 | bytes 5505024 | tf_op jit(solution)/shard_map/pallas_call | solution.py:239
  14.7 5.7 %all-to-all-start = ((bf16[16,80,128]{2,1,0:T(8,128)(2,1)}), bf16[16,80,128]{2,1,0:T(8,128)(2,1)S(1)}, u32[]{:S(2)}, u32[]{:S(2)}) async-start(bf16[16,80,128]{2,1,0:T(8,128)(2,1)} %bitcast.9), calls=%async_computation | async-start | bytes 655360 | tf_op jit(solution)/shard_map/all_to_all | solution.py:218
  20.4 3.3 %collective-permute-start.2 = (bf16[4,128,256]{2,1,0:T(8,128)(2,1)S(1)}, bf16[4,128,256]{2,1,0:T(8,128)(2,1)S(1)}, u32[]{:S(2)}, u32[]{:S(2)}) collective-permute-start(bf16[4,128,256]{2,1,0:T(8,128)(2,1)S(1)} %get-tuple-element.8), channel_id=1, source_target_pairs={{0,2},{2,0},{1,3},{3,1},{4,6},{6,4},{5,7},{7,5},{8,10},{10,8},{9,1... | collective-permute-start | bytes 786440 | tf_op jit(solution)/shard_map/ppermute | solution.py:199
  23.6 0.0 copy-done.3
  23.7 2.0 %collective-permute-start.5 = (bf16[2,256,512]{2,1,0:T(8,128)(2,1)S(1)}, bf16[2,256,512]{2,1,0:T(8,128)(2,1)S(1)}, u32[]{:S(2)}, u32[]{:S(2)}) collective-permute-start(bf16[2,256,512]{2,1,0:T(8,128)(2,1)S(1)} %copy-done.3), channel_id=1, source_target_pairs={{0,2},{2,0},{1,3},{3,1},{4,6},{6,4},{5,7},{7,5},{8,10},{10,8},{9,1... | collective-permute-start | bytes 1572872 | tf_op jit(solution)/shard_map/ppermute | solution.py:199
  25.7 4.9 %all-to-all-done = bf16[16,80,128]{2,1,0:T(8,128)(2,1)S(1)} async-done(((bf16[16,80,128]{2,1,0:T(8,128)(2,1)}), bf16[16,80,128]{2,1,0:T(8,128)(2,1)S(1)}, u32[]{:S(2)}, u32[]{:S(2)}) %all-to-all-start) | async-done | bytes 327712 | tf_op jit(solution)/shard_map/all_to_all | solution.py:218
  30.6 0.7 shard_map.57
  31.3 9.1 %all-to-all-start.1 = ((f32[16,16,128]{2,1,0:T(8,128)}), f32[16,16,128]{2,1,0:T(8,128)S(1)}, u32[]{:S(2)}, u32[]{:S(2)}) async-start(f32[16,16,128]{2,1,0:T(8,128)} %bitcast.11), calls=%async_computation.1 | async-start | bytes 262144 | tf_op jit(solution)/shard_map/all_to_all | solution.py:218
  40.4 0.0 collective-permute-done.2
  40.4 0.1 add_convert_fusion.near
  40.5 3.9 %collective-permute-start.3 = (bf16[2,128,256]{2,1,0:T(8,128)(2,1)S(1)}, bf16[2,128,256]{2,1,0:T(8,128)(2,1)S(1)}, u32[]{:S(2)}, u32[]{:S(2)}) collective-permute-start(bf16[2,128,256]{2,1,0:T(8,128)(2,1)S(1)} %slice.12), channel_id=1, source_target_pairs={{0,4},{4,0},{8,12},{12,8},{16,20},{20,16},{24,28},{28,24},{1,5},{5... | collective-permute-start | bytes 393224 | tf_op jit(solution)/shard_map/ppermute | solution.py:199
  44.4 0.1 stack.39
  44.5 0.0 collective-permute-done.5.by_chip
  44.5 4.2 %collective-permute-start.6 = (bf16[2,256,512]{2,1,0:T(8,128)(2,1)S(1)}, bf16[2,256,512]{2,1,0:T(8,128)(2,1)S(1)}, u32[]{:S(2)}, u32[]{:S(2)}) collective-permute-start(bf16[2,256,512]{2,1,0:T(8,128)(2,1)S(1)} %collective-permute-done.5.by_chip), channel_id=1, source_target_pairs={{0,1},{1,0},{2,3},{3,2},{4,5},{5,4},{6,7},{7,6},{8,9},{9,8},{10,11... | collective-permute-start | bytes 1572872 | tf_op jit(solution)/shard_map/ppermute | solution.py:199
  48.7 0.0 collective-permute-done.3.near_7
  48.7 0.6 all-to-all-done.1
  49.3 0.0 copy-start.7
  49.3 0.8 %shard_map.58 = bf16[16,5,2,8,128]{4,3,2,1,0:T(8,128)(2,1)} custom-call(f32[16,2,8,128]{3,2,1,0:T(8,128)S(1)} %bitcast.20, bf16[16,5,2,8,128]{4,3,2,1,0:T(8,128)(2,1)S(1)} %bitcast.19, bf16[2,128,256]{2,1,0:T(8,128)(2,1)S(1)} %collective-permute-done.3.near_7), custom_call_target="tpu_custom_call" | custom-call | flops 2000000000 | bytes 655360 | tf_op jit(solution)/shard_map/pallas_call | solution.py:260
  50.1 5.1 %all-to-all-start.2 = ((bf16[16,80,128]{2,1,0:T(8,128)(2,1)}), bf16[16,80,128]{2,1,0:T(8,128)(2,1)S(1)}, u32[]{:S(2)}, u32[]{:S(2)}) async-start(bf16[16,80,128]{2,1,0:T(8,128)(2,1)} %bitcast.13), calls=%async_computation.2 | async-start | bytes 655360 | tf_op jit(solution)/shard_map/all_to_all | solution.py:218
  55.2 0.0 copy-done.7
  55.2 0.2 select_reduce_fusion
  55.4 4.2 %collective-permute-start.4 = (bf16[128,256]{1,0:T(8,128)(2,1)S(1)}, bf16[128,256]{1,0:T(8,128)(2,1)S(1)}, u32[]{:S(2)}, u32[]{:S(2)}) collective-permute-start(bf16[128,256]{1,0:T(8,128)(2,1)S(1)} %fusion), channel_id=1, source_target_pairs={{0,8},{4,12},{8,0},{12,4},{16,24},{20,28},{24,16},{28,20},{1,9},{5... | collective-permute-start | bytes 196616 | tf_op jit(solution)/shard_map/ppermute | solution.py:199
  59.6 0.0 collective-permute-done.6.by_both
  59.6 0.0 copy-start.5
  59.6 0.8 %copy-done.5 = bf16[2,256,512]{2,1,0:T(8,128)(2,1)} copy-done((bf16[2,256,512]{2,1,0:T(8,128)(2,1)}, bf16[2,256,512]{2,1,0:T(8,128)(2,1)S(1)}, u32[]{:S(2)}) %copy-start.5) | copy-done | bytes 524312
  60.4 0.0 copy-start.4
  60.4 1.2 %copy-done.4 = bf16[2,256,1024]{2,1,0:T(8,128)(2,1)S(1)} copy-done((bf16[2,256,1024]{2,1,0:T(8,128)(2,1)S(1)}, bf16[2,256,1024]{2,1,0:T(8,128)(2,1)}, u32[]{:S(2)}) %copy-start.4) | copy-done | bytes 1048600
  61.6 0.0 copy-start.6
  61.6 1.0 %copy-done.6 = bf16[2,256,512]{2,1,0:T(8,128)(2,1)S(1)} copy-done((bf16[2,256,512]{2,1,0:T(8,128)(2,1)S(1)}, bf16[2,256,512]{2,1,0:T(8,128)(2,1)}, u32[]{:S(2)}) %copy-start.6) | copy-done | bytes 524312
  62.7 0.7 shard_map.59.late.dense
  63.4 0.0 collective-permute-done.4.near_6
  63.4 0.0 all-to-all-done.2
  63.4 0.1 broadcast_in_dim.18.limits
  63.5 0.1 shard_map.60.coef
  63.6 7.9 %collective-permute-start.7 = (bf16[1152,256]{1,0:T(8,128)(2,1)S(1)}, bf16[1152,256]{1,0:T(8,128)(2,1)S(1)}, u32[]{:S(2)}, u32[]{:S(2)}) collective-permute-start(bf16[1152,256]{1,0:T(8,128)(2,1)S(1)} %shard_map.60.coef), channel_id=1, source_target_pairs={{0,1},{1,0},{2,3},{3,2},{4,5},{5,4},{6,7},{7,6},{8,9},{9,8},{10,11... | collective-permute-start | bytes 1769480 | tf_op jit(solution)/shard_map/ppermute | solution.py:199
  71.5 0.0 copy-done
  71.5 1.2 %shard_map.61.begun = bf16[2,256,512]{2,1,0:T(8,128)(2,1)} custom-call(bf16[1152,256]{1,0:T(8,128)(2,1)S(1)} %shard_map.60.coef, bf16[8,2,256,128]{3,2,1,0:T(8,128)(2,1)S(1)} %copy-done, f32[2,256,512]{2,1,0:T(8,128)S(1)} %shard_map.59.late.dense), custom_call_target="tpu_custom_call" | custom-call | flops 268435456 | bytes 2686976 | tf_op jit(solution)/shard_map/pallas_call | solution.py:284
  72.7 0.4 collective-permute-done.7.coef
  73.1 1.2 %shard_map.62 = bf16[2,256,512]{2,1,0:T(8,128)(2,1)} custom-call(bf16[1152,256]{1,0:T(8,128)(2,1)S(1)} %collective-permute-done.7.coef, bf16[8,2,256,128]{3,2,1,0:T(8,128)(2,1)S(1)} %copy-done, f32[2,256,512]{2,1,0:T(8,128)S(1)} %shard_map.59.late.dense, bf16[2,256,512]{2,1,0:T(8,128)(2,1)} %shard_map.61.begun), custom_call_target="tpu_custom_call", output_to_operand_aliasing={{}: (3, {})} | custom-call | flops 268435456 | bytes 2686976 | tf_op jit(solution)/shard_map/pallas_call | solution.py:293
  (4 shorter events, 0.0 us)
Async XLA Ops:
  0.0 13.5 %collective-permute-start = (bf16[8,2,256,128]{3,2,1,0:T(8,128)(2,1)}, bf16[8,2,256,128]{3,2,1,0:T(8,128)(2,1)S(1)}, u32[]{:S(2)}, u32[]{:S(2)}) collective-permute-start(bf16[8,2,256,128]{3,2,1,0:T(8,128)(2,1)} %basis.3), channel_id=1, source_target_pairs={{0,1},{1,0},{2,3},{3,2},{4,5},{5,4},{6,7},{7,6},{8,9},{9,8},{10,11... | collective-permute-start | bytes 3145736 | tf_op jit(solution)/shard_map/ppermute | solution.py:199
  8.8 4.7 %collective-permute-start.1 = (bf16[2,256,512]{2,1,0:T(8,128)(2,1)}, bf16[2,256,512]{2,1,0:T(8,128)(2,1)S(1)}, u32[]{:S(2)}, u32[]{:S(2)}) collective-permute-start(bf16[2,256,512]{2,1,0:T(8,128)(2,1)} %own.1), channel_id=1, source_target_pairs={{0,1},{1,0},{2,3},{3,2},{4,5},{5,4},{6,7},{7,6},{8,9},{9,8},{10,11... | collective-permute-start | bytes 1572872 | tf_op jit(solution)/shard_map/ppermute | solution.py:199
  10.7 1.2 %copy-start.1 = (bf16[8,2,256,128]{3,2,1,0:T(8,128)(2,1)S(1)}, bf16[8,2,256,128]{3,2,1,0:T(8,128)(2,1)}, u32[]{:S(2)}) copy-start(bf16[8,2,256,128]{3,2,1,0:T(8,128)(2,1)} %basis.3) | copy-start | bytes 3145732
  11.9 1.0 %copy-start.2 = (bf16[2,256,512]{2,1,0:T(8,128)(2,1)S(1)}, bf16[2,256,512]{2,1,0:T(8,128)(2,1)}, u32[]{:S(2)}) copy-start(bf16[2,256,512]{2,1,0:T(8,128)(2,1)} %own.1) | copy-start | bytes 1572868
  13.5 10.2 %copy-start.3 = (bf16[2,256,512]{2,1,0:T(8,128)(2,1)S(1)}, bf16[2,256,512]{2,1,0:T(8,128)(2,1)}, u32[]{:S(2)}) copy-start(bf16[2,256,512]{2,1,0:T(8,128)(2,1)} %own.1) | copy-start | bytes 1572868
  14.7 15.9 %all-to-all-start = ((bf16[16,80,128]{2,1,0:T(8,128)(2,1)}), bf16[16,80,128]{2,1,0:T(8,128)(2,1)S(1)}, u32[]{:S(2)}, u32[]{:S(2)}) async-start(bf16[16,80,128]{2,1,0:T(8,128)(2,1)} %bitcast.9), calls=%async_computation | async-start | bytes 655360 | tf_op jit(solution)/shard_map/all_to_all | solution.py:218
  20.4 20.0 %collective-permute-start.2 = (bf16[4,128,256]{2,1,0:T(8,128)(2,1)S(1)}, bf16[4,128,256]{2,1,0:T(8,128)(2,1)S(1)}, u32[]{:S(2)}, u32[]{:S(2)}) collective-permute-start(bf16[4,128,256]{2,1,0:T(8,128)(2,1)S(1)} %get-tuple-element.8), channel_id=1, source_target_pairs={{0,2},{2,0},{1,3},{3,1},{4,6},{6,4},{5,7},{7,5},{8,10},{10,8},{9,1... | collective-permute-start | bytes 786440 | tf_op jit(solution)/shard_map/ppermute | solution.py:199
  23.7 20.8 %collective-permute-start.5 = (bf16[2,256,512]{2,1,0:T(8,128)(2,1)S(1)}, bf16[2,256,512]{2,1,0:T(8,128)(2,1)S(1)}, u32[]{:S(2)}, u32[]{:S(2)}) collective-permute-start(bf16[2,256,512]{2,1,0:T(8,128)(2,1)S(1)} %copy-done.3), channel_id=1, source_target_pairs={{0,2},{2,0},{1,3},{3,1},{4,6},{6,4},{5,7},{7,5},{8,10},{10,8},{9,1... | collective-permute-start | bytes 1572872 | tf_op jit(solution)/shard_map/ppermute | solution.py:199
  31.3 18.0 %all-to-all-start.1 = ((f32[16,16,128]{2,1,0:T(8,128)}), f32[16,16,128]{2,1,0:T(8,128)S(1)}, u32[]{:S(2)}, u32[]{:S(2)}) async-start(f32[16,16,128]{2,1,0:T(8,128)} %bitcast.11), calls=%async_computation.1 | async-start | bytes 262144 | tf_op jit(solution)/shard_map/all_to_all | solution.py:218
  40.5 8.2 %collective-permute-start.3 = (bf16[2,128,256]{2,1,0:T(8,128)(2,1)S(1)}, bf16[2,128,256]{2,1,0:T(8,128)(2,1)S(1)}, u32[]{:S(2)}, u32[]{:S(2)}) collective-permute-start(bf16[2,128,256]{2,1,0:T(8,128)(2,1)S(1)} %slice.12), channel_id=1, source_target_pairs={{0,4},{4,0},{8,12},{12,8},{16,20},{20,16},{24,28},{28,24},{1,5},{5... | collective-permute-start | bytes 393224 | tf_op jit(solution)/shard_map/ppermute | solution.py:199
  44.5 15.1 %collective-permute-start.6 = (bf16[2,256,512]{2,1,0:T(8,128)(2,1)S(1)}, bf16[2,256,512]{2,1,0:T(8,128)(2,1)S(1)}, u32[]{:S(2)}, u32[]{:S(2)}) collective-permute-start(bf16[2,256,512]{2,1,0:T(8,128)(2,1)S(1)} %collective-permute-done.5.by_chip), channel_id=1, source_target_pairs={{0,1},{1,0},{2,3},{3,2},{4,5},{5,4},{6,7},{7,6},{8,9},{9,8},{10,11... | collective-permute-start | bytes 1572872 | tf_op jit(solution)/shard_map/ppermute | solution.py:199
  49.3 5.9 %copy-start.7 = (s32[510]{0:T(512)S(1)}, s32[510]{0:T(512)}, u32[]{:S(2)}) copy-start(s32[510]{0:T(512)} %param.9) | copy-start | bytes 6124
  50.1 13.3 %all-to-all-start.2 = ((bf16[16,80,128]{2,1,0:T(8,128)(2,1)}), bf16[16,80,128]{2,1,0:T(8,128)(2,1)S(1)}, u32[]{:S(2)}, u32[]{:S(2)}) async-start(bf16[16,80,128]{2,1,0:T(8,128)(2,1)} %bitcast.13), calls=%async_computation.2 | async-start | bytes 655360 | tf_op jit(solution)/shard_map/all_to_all | solution.py:218
  55.4 8.0 %collective-permute-start.4 = (bf16[128,256]{1,0:T(8,128)(2,1)S(1)}, bf16[128,256]{1,0:T(8,128)(2,1)S(1)}, u32[]{:S(2)}, u32[]{:S(2)}) collective-permute-start(bf16[128,256]{1,0:T(8,128)(2,1)S(1)} %fusion), channel_id=1, source_target_pairs={{0,8},{4,12},{8,0},{12,4},{16,24},{20,28},{24,16},{28,20},{1,9},{5... | collective-permute-start | bytes 196616 | tf_op jit(solution)/shard_map/ppermute | solution.py:199
  59.6 0.8 %copy-start.5 = (bf16[2,256,512]{2,1,0:T(8,128)(2,1)}, bf16[2,256,512]{2,1,0:T(8,128)(2,1)S(1)}, u32[]{:S(2)}) copy-start(bf16[2,256,512]{2,1,0:T(8,128)(2,1)S(1)} %collective-permute-done.6.by_both) | copy-start | bytes 1572868
  60.4 1.2 %copy-start.4 = (bf16[2,256,1024]{2,1,0:T(8,128)(2,1)S(1)}, bf16[2,256,1024]{2,1,0:T(8,128)(2,1)}, u32[]{:S(2)}) copy-start(bf16[2,256,1024]{2,1,0:T(8,128)(2,1)} %blocks.1) | copy-start | bytes 3145732
  61.6 1.0 %copy-start.6 = (bf16[2,256,512]{2,1,0:T(8,128)(2,1)S(1)}, bf16[2,256,512]{2,1,0:T(8,128)(2,1)}, u32[]{:S(2)}) copy-start(bf16[2,256,512]{2,1,0:T(8,128)(2,1)} %copy-done.5) | copy-start | bytes 1572868
  63.5 8.1 %copy-start = (bf16[8,2,256,128]{3,2,1,0:T(8,128)(2,1)S(1)}, bf16[8,2,256,128]{3,2,1,0:T(8,128)(2,1)}, u32[]{:S(2)}) copy-start(bf16[8,2,256,128]{3,2,1,0:T(8,128)(2,1)} %basis.5) | copy-start | bytes 3145732
  63.6 9.5 %collective-permute-start.7 = (bf16[1152,256]{1,0:T(8,128)(2,1)S(1)}, bf16[1152,256]{1,0:T(8,128)(2,1)S(1)}, u32[]{:S(2)}, u32[]{:S(2)}) collective-permute-start(bf16[1152,256]{1,0:T(8,128)(2,1)S(1)} %shard_map.60.coef), channel_id=1, source_target_pairs={{0,1},{1,0},{2,3},{3,2},{4,5},{5,4},{6,7},{7,6},{8,9},{9,8},{10,11... | collective-permute-start | bytes 1769480 | tf_op jit(solution)/shard_map/ppermute | solution.py:199

commit v8 on v7

--- a/solution.py
+++ b/solution.py
@@ -22,7 +22,7 @@
         kernel,
         out_shape=out_shape,
         in_specs=in_specs,
-        out_specs=[whole] * len(out_shape) if many else whole,
+        out_specs=[whole] * len(out_shape) if many and not isinstance(whole, list) else whole,
         scratch_shapes=list(scratch),
         input_output_aliases=aliases or {},
         compiler_params=pltpu.CompilerParams(vmem_limit_bytes=VMEM_BYTES),
@@ -63,8 +63,9 @@
         out[slot] = value
 
 
-def theirs_kernel(basis, sides, mine, wide, near):
+def theirs_kernel(basis, sides, mine, wide, near, tiles, sems):
     down, wide_levels, across = wide.shape[:3]
+    copies = []
     for slot, value in enumerate(projections(basis, sides)):
         total = mine[slot] + value
         if slot >= wide_levels:
@@ -72,7 +73,11 @@
             continue
         for col in range(across):
             part = total[:, col * 128 : (col + 1) * 128]
-            wide[:, slot, col] = part.reshape(down, 8, 128).astype(BF16)
+            tiles[slot, :, col] = part.reshape(down, 8, 128).astype(BF16)
+        copies.append(pltpu.make_async_copy(tiles.at[slot], wide.at[:, slot], sems.at[slot]))
+        copies[-1].start()
+    for copy in copies:
+        copy.wait()
 
 
 def far_major(high, count):
@@ -148,22 +153,27 @@
 
     for level in range(wide_levels):
         parts = [wide[:, level, col].astype(F32).reshape(rank, 128) for col in range(across)]
-        put((1 + level) * rank, level, parts)
-    put((1 + wide_levels) * rank, wide_levels, halves(near_6[...]))
+        put(level * rank, level, parts)
+    put(wide_levels * rank, wide_levels, halves(near_6[...]))
     put(upper * rank, upper - 1, halves(near_7[1]))
-    put(0, upper, halves(near[3]))
-    put((1 + upper) * rank, upper + 1, halves(near[2]))
+    put((upper - 1) * rank, upper, halves(near[3]))
+    put((upper + 1) * rank, upper + 1, halves(near[2]))
 
 
 def update(coef, basis, dense, column, store):
-    levels, leaves, _, rank = basis.shape
+    levels, leaves, rows, rank = basis.shape
     half = coef.shape[1]
+    shared = levels - 2
+    left = jnp.concatenate(
+        [basis[level].reshape(leaves * rows, rank) for level in range(shared)], axis=1
+    )
+    both = jnp.dot(left, coef[: shared * rank, :], preferred_element_type=F32)
     for leaf in range(leaves):
-        order = list(range(levels - 1))
-        order = order + [levels - 1] if leaf else [levels - 1] + order
+        order = (levels - 2, levels - 1) if leaf else (levels - 1, levels - 2)
         left = jnp.concatenate([basis[level, leaf] for level in order], axis=1)
-        right = coef[leaf * rank : (leaf + levels) * rank, :]
+        right = coef[(shared + leaf) * rank : (shared + leaf + 2) * rank, :]
         term = jnp.dot(left, right, preferred_element_type=F32)
+        term = term + both[leaf * rows : (leaf + 1) * rows]
         store(leaf, (dense[leaf, :, pl.ds(column, half)] + term).astype(BF16))
 
 
@@ -240,6 +250,11 @@
         theirs_kernel,
         [wide_shape, shape(near_shape, BF16)],
         [VMEM, VMEM, VMEM],
+        scratch=[
+            pltpu.VMEM((wide_levels, owners) + tile, BF16),
+            pltpu.SemaphoreType.DMA((wide_levels,)),
+        ],
+        whole=[ANY, VMEM],
         flops=flops,
         moved=2 * moved,
     )(basis_core, by_core, mine)

time: 75 us -> 75 us (level)
  no operation moved by 1% of the time
where the time goes in v8:
time: 75 us; the launch traced here: 74.2 us
  starting transfers between devices  56 us (75%)
  Pallas kernels  6.15 us (8%)
  waiting for transfers between devices  6.03 us (8%)
  local copies, waits for them, and re-layouts  5.49 us (7%)
    ppermute x8, starting transfers between devices, swap(): lax.ppermute(block, axis, [(i, i ^ bit) for i in range(lax.axis_size(axis...  36.1 us
    all_to_all x3, starting transfers between devices, exchange(): moved = lax.all_to_all(flat, axes, split_axis=0, concat_axis=0, tiled=True)  19.9 us
    all_to_all x3, waiting for transfers between devices, exchange(): moved = lax.all_to_all(flat, axes, split_axis=0, concat_axis=0, tiled=True)  5.54 us
    unnamed x16, local copies, waits for them, and re-layouts  5.33 us
  transfers between devices with their start and end apart: 11, of which 3 were waited for; matrix products, arithmetic and copies ran while one was open for 0% of the time, Pallas kernels for 5%

profile of v8, /device:TPU:1, one launch (start us, length us, event | category | flops | bytes accessed | tf_op | source)
XLA Modules:
  0.0 74.2 jit_solution(10557536355032202212)
XLA Ops:
  0.0 8.8 %collective-permute-start = (bf16[8,2,256,128]{3,2,1,0:T(8,128)(2,1)}, bf16[8,2,256,128]{3,2,1,0:T(8,128)(2,1)S(1)}, u32[]{:S(2)}, u32[]{:S(2)}) collective-permute-start(bf16[8,2,256,128]{3,2,1,0:T(8,128)(2,1)} %basis.3), channel_id=1, source_target_pairs={{0,1},{1,0},{2,3},{3,2},{4,5},{5,4},{6,7},{7,6},{8,9},{9,8},{10,11... | collective-permute-start | bytes 3145736 | tf_op jit(solution)/shard_map/ppermute | solution.py:209
  8.8 1.9 %collective-permute-start.1 = (bf16[2,256,512]{2,1,0:T(8,128)(2,1)}, bf16[2,256,512]{2,1,0:T(8,128)(2,1)S(1)}, u32[]{:S(2)}, u32[]{:S(2)}) collective-permute-start(bf16[2,256,512]{2,1,0:T(8,128)(2,1)} %own.1), channel_id=1, source_target_pairs={{0,1},{1,0},{2,3},{3,2},{4,5},{5,4},{6,7},{7,6},{8,9},{9,8},{10,11... | collective-permute-start | bytes 1572872 | tf_op jit(solution)/shard_map/ppermute | solution.py:209
  10.7 0.0 copy-start.1
  10.7 1.2 %copy-done.1 = bf16[8,2,256,128]{3,2,1,0:T(8,128)(2,1)S(1)} copy-done((bf16[8,2,256,128]{3,2,1,0:T(8,128)(2,1)S(1)}, bf16[8,2,256,128]{3,2,1,0:T(8,128)(2,1)}, u32[]{:S(2)}) %copy-start.1) | copy-done | bytes 1048600
  11.9 0.0 copy-start.2
  11.9 1.0 %copy-done.2 = bf16[2,256,512]{2,1,0:T(8,128)(2,1)S(1)} copy-done((bf16[2,256,512]{2,1,0:T(8,128)(2,1)S(1)}, bf16[2,256,512]{2,1,0:T(8,128)(2,1)}, u32[]{:S(2)}) %copy-start.2) | copy-done | bytes 524312
  13.0 0.5 shard_map.55.mine
  13.5 0.0 copy-start.3
  13.5 0.0 collective-permute-done.1.sides.by_core
  13.5 0.0 collective-permute-done.basis
  13.5 1.1 %shard_map.56 = (bf16[16,5,2,8,128]{4,3,2,1,0:T(8,128)(2,1)}, bf16[4,128,256]{2,1,0:T(8,128)(2,1)S(1)}) custom-call(bf16[8,2,256,128]{3,2,1,0:T(8,128)(2,1)S(1)} %collective-permute-done.basis, bf16[2,256,512]{2,1,0:T(8,128)(2,1)S(1)} %collective-permute-done.1.sides.by_core, f32[9,128,256]{2,1,0:T(8,128)S(1)} %shard_map.55.mine), custom_call_target="tpu_custom_call" | custom-call | flops 268435456 | bytes 5505024 | tf_op jit(solution)/shard_map/pallas_call | solution.py:249
  14.6 5.7 %all-to-all-start = ((bf16[16,80,128]{2,1,0:T(8,128)(2,1)}), bf16[16,80,128]{2,1,0:T(8,128)(2,1)S(1)}, u32[]{:S(2)}, u32[]{:S(2)}) async-start(bf16[16,80,128]{2,1,0:T(8,128)(2,1)} %bitcast.9), calls=%async_computation | async-start | bytes 655360 | tf_op jit(solution)/shard_map/all_to_all | solution.py:228
  20.3 3.3 %collective-permute-start.2 = (bf16[4,128,256]{2,1,0:T(8,128)(2,1)S(1)}, bf16[4,128,256]{2,1,0:T(8,128)(2,1)S(1)}, u32[]{:S(2)}, u32[]{:S(2)}) collective-permute-start(bf16[4,128,256]{2,1,0:T(8,128)(2,1)S(1)} %get-tuple-element.8), channel_id=1, source_target_pairs={{0,2},{2,0},{1,3},{3,1},{4,6},{6,4},{5,7},{7,5},{8,10},{10,8},{9,1... | collective-permute-start | bytes 786440 | tf_op jit(solution)/shard_map/ppermute | solution.py:209
  23.6 0.0 copy-done.3
  23.6 2.0 %collective-permute-start.5 = (bf16[2,256,512]{2,1,0:T(8,128)(2,1)S(1)}, bf16[2,256,512]{2,1,0:T(8,128)(2,1)S(1)}, u32[]{:S(2)}, u32[]{:S(2)}) collective-permute-start(bf16[2,256,512]{2,1,0:T(8,128)(2,1)S(1)} %copy-done.3), channel_id=1, source_target_pairs={{0,2},{2,0},{1,3},{3,1},{4,6},{6,4},{5,7},{7,5},{8,10},{10,8},{9,1... | collective-permute-start | bytes 1572872 | tf_op jit(solution)/shard_map/ppermute | solution.py:209
  25.7 4.9 %all-to-all-done = bf16[16,80,128]{2,1,0:T(8,128)(2,1)S(1)} async-done(((bf16[16,80,128]{2,1,0:T(8,128)(2,1)}), bf16[16,80,128]{2,1,0:T(8,128)(2,1)S(1)}, u32[]{:S(2)}, u32[]{:S(2)}) %all-to-all-start) | async-done | bytes 327712 | tf_op jit(solution)/shard_map/all_to_all | solution.py:228
  30.6 0.7 shard_map.57
  31.3 9.1 %all-to-all-start.1 = ((f32[16,16,128]{2,1,0:T(8,128)}), f32[16,16,128]{2,1,0:T(8,128)S(1)}, u32[]{:S(2)}, u32[]{:S(2)}) async-start(f32[16,16,128]{2,1,0:T(8,128)} %bitcast.11), calls=%async_computation.1 | async-start | bytes 262144 | tf_op jit(solution)/shard_map/all_to_all | solution.py:228
  40.4 0.0 collective-permute-done.2
  40.4 0.1 add_convert_fusion.near
  40.5 3.9 %collective-permute-start.3 = (bf16[2,128,256]{2,1,0:T(8,128)(2,1)S(1)}, bf16[2,128,256]{2,1,0:T(8,128)(2,1)S(1)}, u32[]{:S(2)}, u32[]{:S(2)}) collective-permute-start(bf16[2,128,256]{2,1,0:T(8,128)(2,1)S(1)} %slice.12), channel_id=1, source_target_pairs={{0,4},{4,0},{8,12},{12,8},{16,20},{20,16},{24,28},{28,24},{1,5},{5... | collective-permute-start | bytes 393224 | tf_op jit(solution)/shard_map/ppermute | solution.py:209
  44.4 0.1 stack.39
  44.5 0.0 collective-permute-done.5.by_chip
  44.5 4.2 %collective-permute-start.6 = (bf16[2,256,512]{2,1,0:T(8,128)(2,1)S(1)}, bf16[2,256,512]{2,1,0:T(8,128)(2,1)S(1)}, u32[]{:S(2)}, u32[]{:S(2)}) collective-permute-start(bf16[2,256,512]{2,1,0:T(8,128)(2,1)S(1)} %collective-permute-done.5.by_chip), channel_id=1, source_target_pairs={{0,1},{1,0},{2,3},{3,2},{4,5},{5,4},{6,7},{7,6},{8,9},{9,8},{10,11... | collective-permute-start | bytes 1572872 | tf_op jit(solution)/shard_map/ppermute | solution.py:209
  48.7 0.0 collective-permute-done.3.near_7
  48.7 0.6 all-to-all-done.1
  49.3 0.0 copy-start.7
  49.3 0.8 %shard_map.58 = bf16[16,5,2,8,128]{4,3,2,1,0:T(8,128)(2,1)} custom-call(f32[16,2,8,128]{3,2,1,0:T(8,128)S(1)} %bitcast.20, bf16[16,5,2,8,128]{4,3,2,1,0:T(8,128)(2,1)S(1)} %bitcast.19, bf16[2,128,256]{2,1,0:T(8,128)(2,1)S(1)} %collective-permute-done.3.near_7), custom_call_target="tpu_custom_call" | custom-call | flops 2000000000 | bytes 655360 | tf_op jit(solution)/shard_map/pallas_call | solution.py:275
  50.1 5.1 %all-to-all-start.2 = ((bf16[16,80,128]{2,1,0:T(8,128)(2,1)}), bf16[16,80,128]{2,1,0:T(8,128)(2,1)S(1)}, u32[]{:S(2)}, u32[]{:S(2)}) async-start(bf16[16,80,128]{2,1,0:T(8,128)(2,1)} %bitcast.13), calls=%async_computation.2 | async-start | bytes 655360 | tf_op jit(solution)/shard_map/all_to_all | solution.py:228
  55.2 0.0 copy-done.7
  55.2 0.2 select_reduce_fusion
  55.4 4.2 %collective-permute-start.4 = (bf16[128,256]{1,0:T(8,128)(2,1)S(1)}, bf16[128,256]{1,0:T(8,128)(2,1)S(1)}, u32[]{:S(2)}, u32[]{:S(2)}) collective-permute-start(bf16[128,256]{1,0:T(8,128)(2,1)S(1)} %fusion), channel_id=1, source_target_pairs={{0,8},{4,12},{8,0},{12,4},{16,24},{20,28},{24,16},{28,20},{1,9},{5... | collective-permute-start | bytes 196616 | tf_op jit(solution)/shard_map/ppermute | solution.py:209
  59.6 0.0 collective-permute-done.6.by_both
  59.6 0.0 copy-start.5
  59.6 0.8 %copy-done.5 = bf16[2,256,512]{2,1,0:T(8,128)(2,1)} copy-done((bf16[2,256,512]{2,1,0:T(8,128)(2,1)}, bf16[2,256,512]{2,1,0:T(8,128)(2,1)S(1)}, u32[]{:S(2)}) %copy-start.5) | copy-done | bytes 524312
  60.4 0.0 copy-start.4
  60.4 1.2 %copy-done.4 = bf16[2,256,1024]{2,1,0:T(8,128)(2,1)S(1)} copy-done((bf16[2,256,1024]{2,1,0:T(8,128)(2,1)S(1)}, bf16[2,256,1024]{2,1,0:T(8,128)(2,1)}, u32[]{:S(2)}) %copy-start.4) | copy-done | bytes 1048600
  61.6 1.0 %copy-done.6 = bf16[2,256,512]{2,1,0:T(8,128)(2,1)S(1)} copy-done((bf16[2,256,512]{2,1,0:T(8,128)(2,1)S(1)}, bf16[2,256,512]{2,1,0:T(8,128)(2,1)}, u32[]{:S(2)}) %copy-start.6) | copy-done | bytes 524312
  62.6 0.7 shard_map.59.late.dense
  63.4 0.0 collective-permute-done.4.near_6
  63.4 0.0 all-to-all-done.2
  63.4 0.1 broadcast_in_dim.18.limits
  63.5 0.1 shard_map.60.coef
  63.6 7.9 %collective-permute-start.7 = (bf16[1152,256]{1,0:T(8,128)(2,1)S(1)}, bf16[1152,256]{1,0:T(8,128)(2,1)S(1)}, u32[]{:S(2)}, u32[]{:S(2)}) collective-permute-start(bf16[1152,256]{1,0:T(8,128)(2,1)S(1)} %shard_map.60.coef), channel_id=1, source_target_pairs={{0,1},{1,0},{2,3},{3,2},{4,5},{5,4},{6,7},{7,6},{8,9},{9,8},{10,11... | collective-permute-start | bytes 1769480 | tf_op jit(solution)/shard_map/ppermute | solution.py:209
  71.5 0.0 copy-done
  71.5 1.1 %shard_map.61.begun = bf16[2,256,512]{2,1,0:T(8,128)(2,1)} custom-call(bf16[1152,256]{1,0:T(8,128)(2,1)S(1)} %shard_map.60.coef, bf16[8,2,256,128]{3,2,1,0:T(8,128)(2,1)S(1)} %copy-done, f32[2,256,512]{2,1,0:T(8,128)S(1)} %shard_map.59.late.dense), custom_call_target="tpu_custom_call" | custom-call | flops 268435456 | bytes 2686976 | tf_op jit(solution)/shard_map/pallas_call | solution.py:299
  72.6 0.5 collective-permute-done.7.coef
  73.1 1.1 %shard_map.62 = bf16[2,256,512]{2,1,0:T(8,128)(2,1)} custom-call(bf16[1152,256]{1,0:T(8,128)(2,1)S(1)} %collective-permute-done.7.coef, bf16[8,2,256,128]{3,2,1,0:T(8,128)(2,1)S(1)} %copy-done, f32[2,256,512]{2,1,0:T(8,128)S(1)} %shard_map.59.late.dense, bf16[2,256,512]{2,1,0:T(8,128)(2,1)} %shard_map.61.begun), custom_call_target="tpu_custom_call", output_to_operand_aliasing={{}: (3, {})} | custom-call | flops 268435456 | bytes 2686976 | tf_op jit(solution)/shard_map/pallas_call | solution.py:308
  (4 shorter events, 0.0 us)
Async XLA Ops:
  0.0 13.5 %collective-permute-start = (bf16[8,2,256,128]{3,2,1,0:T(8,128)(2,1)}, bf16[8,2,256,128]{3,2,1,0:T(8,128)(2,1)S(1)}, u32[]{:S(2)}, u32[]{:S(2)}) collective-permute-start(bf16[8,2,256,128]{3,2,1,0:T(8,128)(2,1)} %basis.3), channel_id=1, source_target_pairs={{0,1},{1,0},{2,3},{3,2},{4,5},{5,4},{6,7},{7,6},{8,9},{9,8},{10,11... | collective-permute-start | bytes 3145736 | tf_op jit(solution)/shard_map/ppermute | solution.py:209
  8.8 4.7 %collective-permute-start.1 = (bf16[2,256,512]{2,1,0:T(8,128)(2,1)}, bf16[2,256,512]{2,1,0:T(8,128)(2,1)S(1)}, u32[]{:S(2)}, u32[]{:S(2)}) collective-permute-start(bf16[2,256,512]{2,1,0:T(8,128)(2,1)} %own.1), channel_id=1, source_target_pairs={{0,1},{1,0},{2,3},{3,2},{4,5},{5,4},{6,7},{7,6},{8,9},{9,8},{10,11... | collective-permute-start | bytes 1572872 | tf_op jit(solution)/shard_map/ppermute | solution.py:209
  10.7 1.2 %copy-start.1 = (bf16[8,2,256,128]{3,2,1,0:T(8,128)(2,1)S(1)}, bf16[8,2,256,128]{3,2,1,0:T(8,128)(2,1)}, u32[]{:S(2)}) copy-start(bf16[8,2,256,128]{3,2,1,0:T(8,128)(2,1)} %basis.3) | copy-start | bytes 3145732
  11.9 1.0 %copy-start.2 = (bf16[2,256,512]{2,1,0:T(8,128)(2,1)S(1)}, bf16[2,256,512]{2,1,0:T(8,128)(2,1)}, u32[]{:S(2)}) copy-start(bf16[2,256,512]{2,1,0:T(8,128)(2,1)} %own.1) | copy-start | bytes 1572868
  13.5 10.1 %copy-start.3 = (bf16[2,256,512]{2,1,0:T(8,128)(2,1)S(1)}, bf16[2,256,512]{2,1,0:T(8,128)(2,1)}, u32[]{:S(2)}) copy-start(bf16[2,256,512]{2,1,0:T(8,128)(2,1)} %own.1) | copy-start | bytes 1572868
  14.6 15.9 %all-to-all-start = ((bf16[16,80,128]{2,1,0:T(8,128)(2,1)}), bf16[16,80,128]{2,1,0:T(8,128)(2,1)S(1)}, u32[]{:S(2)}, u32[]{:S(2)}) async-start(bf16[16,80,128]{2,1,0:T(8,128)(2,1)} %bitcast.9), calls=%async_computation | async-start | bytes 655360 | tf_op jit(solution)/shard_map/all_to_all | solution.py:228
  20.3 20.0 %collective-permute-start.2 = (bf16[4,128,256]{2,1,0:T(8,128)(2,1)S(1)}, bf16[4,128,256]{2,1,0:T(8,128)(2,1)S(1)}, u32[]{:S(2)}, u32[]{:S(2)}) collective-permute-start(bf16[4,128,256]{2,1,0:T(8,128)(2,1)S(1)} %get-tuple-element.8), channel_id=1, source_target_pairs={{0,2},{2,0},{1,3},{3,1},{4,6},{6,4},{5,7},{7,5},{8,10},{10,8},{9,1... | collective-permute-start | bytes 786440 | tf_op jit(solution)/shard_map/ppermute | solution.py:209
  23.6 20.8 %collective-permute-start.5 = (bf16[2,256,512]{2,1,0:T(8,128)(2,1)S(1)}, bf16[2,256,512]{2,1,0:T(8,128)(2,1)S(1)}, u32[]{:S(2)}, u32[]{:S(2)}) collective-permute-start(bf16[2,256,512]{2,1,0:T(8,128)(2,1)S(1)} %copy-done.3), channel_id=1, source_target_pairs={{0,2},{2,0},{1,3},{3,1},{4,6},{6,4},{5,7},{7,5},{8,10},{10,8},{9,1... | collective-permute-start | bytes 1572872 | tf_op jit(solution)/shard_map/ppermute | solution.py:209
  31.3 18.0 %all-to-all-start.1 = ((f32[16,16,128]{2,1,0:T(8,128)}), f32[16,16,128]{2,1,0:T(8,128)S(1)}, u32[]{:S(2)}, u32[]{:S(2)}) async-start(f32[16,16,128]{2,1,0:T(8,128)} %bitcast.11), calls=%async_computation.1 | async-start | bytes 262144 | tf_op jit(solution)/shard_map/all_to_all | solution.py:228
  40.5 8.2 %collective-permute-start.3 = (bf16[2,128,256]{2,1,0:T(8,128)(2,1)S(1)}, bf16[2,128,256]{2,1,0:T(8,128)(2,1)S(1)}, u32[]{:S(2)}, u32[]{:S(2)}) collective-permute-start(bf16[2,128,256]{2,1,0:T(8,128)(2,1)S(1)} %slice.12), channel_id=1, source_target_pairs={{0,4},{4,0},{8,12},{12,8},{16,20},{20,16},{24,28},{28,24},{1,5},{5... | collective-permute-start | bytes 393224 | tf_op jit(solution)/shard_map/ppermute | solution.py:209
  44.5 15.1 %collective-permute-start.6 = (bf16[2,256,512]{2,1,0:T(8,128)(2,1)S(1)}, bf16[2,256,512]{2,1,0:T(8,128)(2,1)S(1)}, u32[]{:S(2)}, u32[]{:S(2)}) collective-permute-start(bf16[2,256,512]{2,1,0:T(8,128)(2,1)S(1)} %collective-permute-done.5.by_chip), channel_id=1, source_target_pairs={{0,1},{1,0},{2,3},{3,2},{4,5},{5,4},{6,7},{7,6},{8,9},{9,8},{10,11... | collective-permute-start | bytes 1572872 | tf_op jit(solution)/shard_map/ppermute | solution.py:209
  49.3 5.9 %copy-start.7 = (s32[510]{0:T(512)S(1)}, s32[510]{0:T(512)}, u32[]{:S(2)}) copy-start(s32[510]{0:T(512)} %param.9) | copy-start | bytes 6124
  50.1 13.3 %all-to-all-start.2 = ((bf16[16,80,128]{2,1,0:T(8,128)(2,1)}), bf16[16,80,128]{2,1,0:T(8,128)(2,1)S(1)}, u32[]{:S(2)}, u32[]{:S(2)}) async-start(bf16[16,80,128]{2,1,0:T(8,128)(2,1)} %bitcast.13), calls=%async_computation.2 | async-start | bytes 655360 | tf_op jit(solution)/shard_map/all_to_all | solution.py:228
  55.4 8.0 %collective-permute-start.4 = (bf16[128,256]{1,0:T(8,128)(2,1)S(1)}, bf16[128,256]{1,0:T(8,128)(2,1)S(1)}, u32[]{:S(2)}, u32[]{:S(2)}) collective-permute-start(bf16[128,256]{1,0:T(8,128)(2,1)S(1)} %fusion), channel_id=1, source_target_pairs={{0,8},{4,12},{8,0},{12,4},{16,24},{20,28},{24,16},{28,20},{1,9},{5... | collective-permute-start | bytes 196616 | tf_op jit(solution)/shard_map/ppermute | solution.py:209
  59.6 0.8 %copy-start.5 = (bf16[2,256,512]{2,1,0:T(8,128)(2,1)}, bf16[2,256,512]{2,1,0:T(8,128)(2,1)S(1)}, u32[]{:S(2)}) copy-start(bf16[2,256,512]{2,1,0:T(8,128)(2,1)S(1)} %collective-permute-done.6.by_both) | copy-start | bytes 1572868
  60.4 1.2 %copy-start.4 = (bf16[2,256,1024]{2,1,0:T(8,128)(2,1)S(1)}, bf16[2,256,1024]{2,1,0:T(8,128)(2,1)}, u32[]{:S(2)}) copy-start(bf16[2,256,1024]{2,1,0:T(8,128)(2,1)} %blocks.1) | copy-start | bytes 3145732
  61.6 1.0 %copy-start.6 = (bf16[2,256,512]{2,1,0:T(8,128)(2,1)S(1)}, bf16[2,256,512]{2,1,0:T(8,128)(2,1)}, u32[]{:S(2)}) copy-start(bf16[2,256,512]{2,1,0:T(8,128)(2,1)} %copy-done.5) | copy-start | bytes 1572868
  63.5 8.1 %copy-start = (bf16[8,2,256,128]{3,2,1,0:T(8,128)(2,1)S(1)}, bf16[8,2,256,128]{3,2,1,0:T(8,128)(2,1)}, u32[]{:S(2)}) copy-start(bf16[8,2,256,128]{3,2,1,0:T(8,128)(2,1)} %basis.5) | copy-start | bytes 3145732
  63.6 9.5 %collective-permute-start.7 = (bf16[1152,256]{1,0:T(8,128)(2,1)S(1)}, bf16[1152,256]{1,0:T(8,128)(2,1)S(1)}, u32[]{:S(2)}, u32[]{:S(2)}) collective-permute-start(bf16[1152,256]{1,0:T(8,128)(2,1)S(1)} %shard_map.60.coef), channel_id=1, source_target_pairs={{0,1},{1,0},{2,3},{3,2},{4,5},{5,4},{6,7},{7,6},{8,9},{9,8},{10,11... | collective-permute-start | bytes 1769480 | tf_op jit(solution)/shard_map/ppermute | solution.py:209

commit v9 on v7

--- a/solution.py
+++ b/solution.py
@@ -77,6 +77,10 @@
 
 def far_major(high, count):
     return (high & 1) * (count // 2) + (high >> 1)
+
+
+def near_kernel(mine, theirs, late, out):
+    out[...] = (mine[...].astype(F32) + theirs[...].astype(F32)).astype(BF16)
 
 
 def ring_kernel(parts, out):
@@ -244,7 +248,9 @@
         moved=2 * moved,
     )(basis_core, by_core, mine)
     wide = exchange(wide, ("chip", "z"))
-    near = (near.astype(F32) + swap(near, "chip").astype(F32)).astype(BF16)
+    near = call(
+        near_kernel, shape(near_shape, BF16), [VMEM, VMEM, ANY], moved=6 * slots * rank * half
+    )(near, swap(near, "chip"), wide)
     near_7 = swap(near[:2], "z", 1)
     near_6 = swap((near[0].astype(F32) + near_7[0].astype(F32)).astype(BF16), "z", 2)
     to_high = call(

time: 75 us -> 77.6 us (1.035)
  waiting for transfers between devices: 5.97 us -> 10.5 us
  local copies, waits for them, and re-layouts: 5.49 us -> 3.66 us
  starting transfers between devices: 56 us -> 54.8 us
  Pallas kernels: 6.3 us -> 7.41 us
    ppermute x8, waiting for transfers between devices: 0.45 us -> 5.61 us  [swap(): lax.ppermute(block, axis, [(i, i ^ bit) for i in range(lax.axis_size(axis...]
    ppermute x8, starting transfers between devices: 36.1 us -> 33.8 us  [swap(): lax.ppermute(block, axis, [(i, i ^ bit) for i in range(lax.axis_size(axis...]
    unnamed x16 -> x12, local copies, waits for them, and re-layouts: 5.33 us -> 3.5 us
    all_to_all x3, starting transfers between devices: 19.8 us -> 21 us  [exchange(): moved = lax.all_to_all(flat, axes, split_axis=0, concat_axis=0, tiled=True)]
    pallas_call x1, Pallas kernels: 0.7 us -> 1.75 us  [local(): call(dense_kernel, shape((leaves, rows, width), F32), [VMEM] * 5, flops=L...]
  transfers between devices with their start and end apart: 11 -> 11, of which waited for: 3 -> 4; matrix products, arithmetic and copies ran while one was open for 0% -> 0% of each run, Pallas kernels for 5% -> 6%
where the time goes in v9:
time: 77.6 us; the launch traced here: 76.8 us
  starting transfers between devices  54.8 us (71%)
  waiting for transfers between devices  10.5 us (14%)
  Pallas kernels  7.41 us (10%)
  local copies, waits for them, and re-layouts  3.66 us (5%)
    ppermute x8, starting transfers between devices, swap(): lax.ppermute(block, axis, [(i, i ^ bit) for i in range(lax.axis_size(axis...  33.8 us
    all_to_all x3, starting transfers between devices, exchange(): moved = lax.all_to_all(flat, axes, split_axis=0, concat_axis=0, tiled=True)  21 us
    ppermute x8, waiting for transfers between devices, swap(): lax.ppermute(block, axis, [(i, i ^ bit) for i in range(lax.axis_size(axis...  5.61 us
    all_to_all x3, waiting for transfers between devices, exchange(): moved = lax.all_to_all(flat, axes, split_axis=0, concat_axis=0, tiled=True)  4.91 us
    unnamed x12, local copies, waits for them, and re-layouts  3.5 us
    pallas_call x1, Pallas kernels, local(): call(dense_kernel, shape((leaves, rows, width), F32), [VMEM] * 5, flops=L...  1.75 us
  transfers between devices with their start and end apart: 11, of which 4 were waited for; matrix products, arithmetic and copies ran while one was open for 0% of the time, Pallas kernels for 6%

profile of v9, /device:TPU:1, one launch (start us, length us, event | category | flops | bytes accessed | tf_op | source)
XLA Modules:
  0.0 76.8 jit_solution(3964267785111548779)
XLA Ops:
  0.0 8.8 %collective-permute-start = (bf16[8,2,256,128]{3,2,1,0:T(8,128)(2,1)}, bf16[8,2,256,128]{3,2,1,0:T(8,128)(2,1)S(1)}, u32[]{:S(2)}, u32[]{:S(2)}) collective-permute-start(bf16[8,2,256,128]{3,2,1,0:T(8,128)(2,1)} %basis.3), channel_id=1, source_target_pairs={{0,1},{1,0},{2,3},{3,2},{4,5},{5,4},{6,7},{7,6},{8,9},{9,8},{10,11... | collective-permute-start | bytes 3145736 | tf_op jit(solution)/shard_map/ppermute | solution.py:203
  8.8 1.9 %collective-permute-start.1 = (bf16[2,256,512]{2,1,0:T(8,128)(2,1)}, bf16[2,256,512]{2,1,0:T(8,128)(2,1)S(1)}, u32[]{:S(2)}, u32[]{:S(2)}) collective-permute-start(bf16[2,256,512]{2,1,0:T(8,128)(2,1)} %own.1), channel_id=1, source_target_pairs={{0,1},{1,0},{2,3},{3,2},{4,5},{5,4},{6,7},{7,6},{8,9},{9,8},{10,11... | collective-permute-start | bytes 1572872 | tf_op jit(solution)/shard_map/ppermute | solution.py:203
  10.7 0.0 copy-start.1
  10.7 1.2 %copy-done.1 = bf16[8,2,256,128]{3,2,1,0:T(8,128)(2,1)S(1)} copy-done((bf16[8,2,256,128]{3,2,1,0:T(8,128)(2,1)S(1)}, bf16[8,2,256,128]{3,2,1,0:T(8,128)(2,1)}, u32[]{:S(2)}) %copy-start.1) | copy-done | bytes 1048600
  11.9 0.0 copy-start.2
  11.9 1.0 %copy-done.2 = bf16[2,256,512]{2,1,0:T(8,128)(2,1)S(1)} copy-done((bf16[2,256,512]{2,1,0:T(8,128)(2,1)S(1)}, bf16[2,256,512]{2,1,0:T(8,128)(2,1)}, u32[]{:S(2)}) %copy-start.2) | copy-done | bytes 524312
  13.0 0.5 shard_map.55.mine
  13.5 0.0 copy-start.3
  13.5 0.0 collective-permute-done.1.sides.by_core
  13.5 0.0 collective-permute-done.basis
  13.5 1.2 %shard_map.56 = (bf16[16,5,2,8,128]{4,3,2,1,0:T(8,128)(2,1)}, bf16[4,128,256]{2,1,0:T(8,128)(2,1)S(1)}) custom-call(bf16[8,2,256,128]{3,2,1,0:T(8,128)(2,1)S(1)} %collective-permute-done.basis, bf16[2,256,512]{2,1,0:T(8,128)(2,1)S(1)} %collective-permute-done.1.sides.by_core, f32[9,128,256]{2,1,0:T(8,128)S(1)} %shard_map.55.mine), custom_call_target="tpu_custom_call" | custom-call | flops 268435456 | bytes 5505024 | tf_op jit(solution)/shard_map/pallas_call | solution.py:243
  14.7 5.7 %all-to-all-start = ((bf16[16,80,128]{2,1,0:T(8,128)(2,1)}), bf16[16,80,128]{2,1,0:T(8,128)(2,1)S(1)}, u32[]{:S(2)}, u32[]{:S(2)}) async-start(bf16[16,80,128]{2,1,0:T(8,128)(2,1)} %bitcast.9), calls=%async_computation | async-start | bytes 655360 | tf_op jit(solution)/shard_map/all_to_all | solution.py:222
  20.4 0.0 copy-done.3
  20.4 3.3 %collective-permute-start.5 = (bf16[2,256,512]{2,1,0:T(8,128)(2,1)S(1)}, bf16[2,256,512]{2,1,0:T(8,128)(2,1)S(1)}, u32[]{:S(2)}, u32[]{:S(2)}) collective-permute-start(bf16[2,256,512]{2,1,0:T(8,128)(2,1)S(1)} %copy-done.3), channel_id=1, source_target_pairs={{0,2},{2,0},{1,3},{3,1},{4,6},{6,4},{5,7},{7,5},{8,10},{10,8},{9,1... | collective-permute-start | bytes 1572872 | tf_op jit(solution)/shard_map/ppermute | solution.py:203
  23.7 2.0 %collective-permute-start.2 = (bf16[4,128,256]{2,1,0:T(8,128)(2,1)S(1)}, bf16[4,128,256]{2,1,0:T(8,128)(2,1)S(1)}, u32[]{:S(2)}, u32[]{:S(2)}) collective-permute-start(bf16[4,128,256]{2,1,0:T(8,128)(2,1)S(1)} %get-tuple-element.8.mine), channel_id=1, source_target_pairs={{0,2},{2,0},{1,3},{3,1},{4,6},{6,4},{5,7},{7,5},{8,10},{10,8},{9,1... | collective-permute-start | bytes 786440 | tf_op jit(solution)/shard_map/ppermute | solution.py:203
  25.7 4.9 %all-to-all-done = bf16[16,80,128]{2,1,0:T(8,128)(2,1)S(1)} async-done(((bf16[16,80,128]{2,1,0:T(8,128)(2,1)}), bf16[16,80,128]{2,1,0:T(8,128)(2,1)S(1)}, u32[]{:S(2)}, u32[]{:S(2)}) %all-to-all-start) | async-done | bytes 327712 | tf_op jit(solution)/shard_map/all_to_all | solution.py:222
  30.6 0.7 shard_map.57
  31.3 9.1 %all-to-all-start.1 = ((f32[16,16,128]{2,1,0:T(8,128)}), f32[16,16,128]{2,1,0:T(8,128)S(1)}, u32[]{:S(2)}, u32[]{:S(2)}) async-start(f32[16,16,128]{2,1,0:T(8,128)} %bitcast.11), calls=%async_computation.1 | async-start | bytes 262144 | tf_op jit(solution)/shard_map/all_to_all | solution.py:222
  40.4 4.0 %collective-permute-done.2.theirs = bf16[4,128,256]{2,1,0:T(8,128)(2,1)S(1)} collective-permute-done((bf16[4,128,256]{2,1,0:T(8,128)(2,1)S(1)}, bf16[4,128,256]{2,1,0:T(8,128)(2,1)S(1)}, u32[]{:S(2)}, u32[]{:S(2)}) %collective-permute-start.2) | collective-permute-done | bytes 262176 | tf_op jit(solution)/shard_map/ppermute | solution.py:203
  44.4 0.1 shard_map.58.near
  44.5 2.0 %collective-permute-start.3 = (bf16[2,128,256]{2,1,0:T(8,128)(2,1)S(1)}, bf16[2,128,256]{2,1,0:T(8,128)(2,1)S(1)}, u32[]{:S(2)}, u32[]{:S(2)}) collective-permute-start(bf16[2,128,256]{2,1,0:T(8,128)(2,1)S(1)} %slice.12), channel_id=1, source_target_pairs={{0,4},{4,0},{8,12},{12,8},{16,20},{20,16},{24,28},{28,24},{1,5},{5... | collective-permute-start | bytes 393224 | tf_op jit(solution)/shard_map/ppermute | solution.py:203
  46.5 0.1 stack.39
  46.6 0.0 collective-permute-done.5.by_chip
  46.6 4.0 %collective-permute-start.6 = (bf16[2,256,512]{2,1,0:T(8,128)(2,1)S(1)}, bf16[2,256,512]{2,1,0:T(8,128)(2,1)}, u32[]{:S(2)}, u32[]{:S(2)}) collective-permute-start(bf16[2,256,512]{2,1,0:T(8,128)(2,1)S(1)} %collective-permute-done.5.by_chip), channel_id=1, source_target_pairs={{0,1},{1,0},{2,3},{3,2},{4,5},{5,4},{6,7},{7,6},{8,9},{9,8},{10,11... | collective-permute-start | bytes 1572872 | tf_op jit(solution)/shard_map/ppermute | solution.py:203
  50.6 0.0 collective-permute-done.3.near_7
  50.6 0.0 all-to-all-done.1
  50.6 0.0 copy-start.5
  50.7 0.8 %shard_map.59 = bf16[16,5,2,8,128]{4,3,2,1,0:T(8,128)(2,1)} custom-call(f32[16,2,8,128]{3,2,1,0:T(8,128)S(1)} %bitcast.21, bf16[16,5,2,8,128]{4,3,2,1,0:T(8,128)(2,1)S(1)} %bitcast.20, bf16[2,128,256]{2,1,0:T(8,128)(2,1)S(1)} %collective-permute-done.3.near_7), custom_call_target="tpu_custom_call" | custom-call | flops 2000000000 | bytes 655360 | tf_op jit(solution)/shard_map/pallas_call | solution.py:266
  51.4 6.2 %all-to-all-start.2 = ((bf16[16,80,128]{2,1,0:T(8,128)(2,1)}), bf16[16,80,128]{2,1,0:T(8,128)(2,1)S(1)}, u32[]{:S(2)}, u32[]{:S(2)}) async-start(bf16[16,80,128]{2,1,0:T(8,128)(2,1)} %bitcast.13), calls=%async_computation.2 | async-start | bytes 655360 | tf_op jit(solution)/shard_map/all_to_all | solution.py:222
  57.7 0.0 copy-done.5
  57.7 0.2 select_reduce_fusion
  57.9 4.2 %collective-permute-start.4 = (bf16[128,256]{1,0:T(8,128)(2,1)S(1)}, bf16[128,256]{1,0:T(8,128)(2,1)S(1)}, u32[]{:S(2)}, u32[]{:S(2)}) collective-permute-start(bf16[128,256]{1,0:T(8,128)(2,1)S(1)} %fusion), channel_id=1, source_target_pairs={{0,8},{4,12},{8,0},{12,4},{16,24},{20,28},{24,16},{28,20},{1,9},{5... | collective-permute-start | bytes 196616 | tf_op jit(solution)/shard_map/ppermute | solution.py:203
  62.1 0.0 collective-permute-done.6.by_both
  62.1 0.0 copy-start.4
  62.1 1.2 %copy-done.4 = bf16[2,256,1024]{2,1,0:T(8,128)(2,1)S(1)} copy-done((bf16[2,256,1024]{2,1,0:T(8,128)(2,1)S(1)}, bf16[2,256,1024]{2,1,0:T(8,128)(2,1)}, u32[]{:S(2)}) %copy-start.4) | copy-done | bytes 1048600
  63.3 1.8 %shard_map.60.late.dense = f32[2,256,512]{2,1,0:T(8,128)S(1)} custom-call(bf16[2,256,1024]{2,1,0:T(8,128)(2,1)S(1)} %copy-done.4, bf16[2,256,512]{2,1,0:T(8,128)(2,1)S(1)} %copy-done.3, bf16[2,256,512]{2,1,0:T(8,128)(2,1)S(1)} %collective-permute-done.1.sides.by_core, bf16[2,256,512]{2,1,0:T(8,128)(2,1)S(1)} %collective-permute-done.5.by_chip, ...), custom_call_target="tpu_custom_call" | custom-call | flops 3000000000 | bytes 4194304 | tf_op jit(solution)/shard_map/pallas_call | solution.py:274
  65.1 1.2 %collective-permute-done.4.near_6 = bf16[128,256]{1,0:T(8,128)(2,1)S(1)} collective-permute-done((bf16[128,256]{1,0:T(8,128)(2,1)S(1)}, bf16[128,256]{1,0:T(8,128)(2,1)S(1)}, u32[]{:S(2)}, u32[]{:S(2)}) %collective-permute-start.4) | collective-permute-done | bytes 65568 | tf_op jit(solution)/shard_map/ppermute | solution.py:203
  66.2 0.0 all-to-all-done.2
  66.2 0.1 broadcast_in_dim.18.limits
  66.3 0.0 copy-start
  66.3 0.1 shard_map.61.coef
  66.5 7.6 %collective-permute-start.7 = (bf16[1152,256]{1,0:T(8,128)(2,1)S(1)}, bf16[1152,256]{1,0:T(8,128)(2,1)S(1)}, u32[]{:S(2)}, u32[]{:S(2)}) collective-permute-start(bf16[1152,256]{1,0:T(8,128)(2,1)S(1)} %shard_map.61.coef), channel_id=1, source_target_pairs={{0,1},{1,0},{2,3},{3,2},{4,5},{5,4},{6,7},{7,6},{8,9},{9,8},{10,11... | collective-permute-start | bytes 1769480 | tf_op jit(solution)/shard_map/ppermute | solution.py:203
  74.1 0.0 copy-done
  74.1 1.2 %shard_map.62.begun = bf16[2,256,512]{2,1,0:T(8,128)(2,1)} custom-call(bf16[1152,256]{1,0:T(8,128)(2,1)S(1)} %shard_map.61.coef, bf16[8,2,256,128]{3,2,1,0:T(8,128)(2,1)S(1)} %copy-done, f32[2,256,512]{2,1,0:T(8,128)S(1)} %shard_map.60.late.dense), custom_call_target="tpu_custom_call" | custom-call | flops 268435456 | bytes 2686976 | tf_op jit(solution)/shard_map/pallas_call | solution.py:290
  75.2 0.4 collective-permute-done.7.coef
  75.7 1.2 %shard_map.63 = bf16[2,256,512]{2,1,0:T(8,128)(2,1)} custom-call(bf16[1152,256]{1,0:T(8,128)(2,1)S(1)} %collective-permute-done.7.coef, bf16[8,2,256,128]{3,2,1,0:T(8,128)(2,1)S(1)} %copy-done, f32[2,256,512]{2,1,0:T(8,128)S(1)} %shard_map.60.late.dense, bf16[2,256,512]{2,1,0:T(8,128)(2,1)} %shard_map.62.begun), custom_call_target="tpu_custom_call", output_to_operand_aliasing={{}: (3, {})} | custom-call | flops 268435456 | bytes 2686976 | tf_op jit(solution)/shard_map/pallas_call | solution.py:299
  (2 shorter events, 0.0 us)
Async XLA Ops:
  0.0 13.5 %collective-permute-start = (bf16[8,2,256,128]{3,2,1,0:T(8,128)(2,1)}, bf16[8,2,256,128]{3,2,1,0:T(8,128)(2,1)S(1)}, u32[]{:S(2)}, u32[]{:S(2)}) collective-permute-start(bf16[8,2,256,128]{3,2,1,0:T(8,128)(2,1)} %basis.3), channel_id=1, source_target_pairs={{0,1},{1,0},{2,3},{3,2},{4,5},{5,4},{6,7},{7,6},{8,9},{9,8},{10,11... | collective-permute-start | bytes 3145736 | tf_op jit(solution)/shard_map/ppermute | solution.py:203
  8.8 4.7 %collective-permute-start.1 = (bf16[2,256,512]{2,1,0:T(8,128)(2,1)}, bf16[2,256,512]{2,1,0:T(8,128)(2,1)S(1)}, u32[]{:S(2)}, u32[]{:S(2)}) collective-permute-start(bf16[2,256,512]{2,1,0:T(8,128)(2,1)} %own.1), channel_id=1, source_target_pairs={{0,1},{1,0},{2,3},{3,2},{4,5},{5,4},{6,7},{7,6},{8,9},{9,8},{10,11... | collective-permute-start | bytes 1572872 | tf_op jit(solution)/shard_map/ppermute | solution.py:203
  10.7 1.2 %copy-start.1 = (bf16[8,2,256,128]{3,2,1,0:T(8,128)(2,1)S(1)}, bf16[8,2,256,128]{3,2,1,0:T(8,128)(2,1)}, u32[]{:S(2)}) copy-start(bf16[8,2,256,128]{3,2,1,0:T(8,128)(2,1)} %basis.3) | copy-start | bytes 3145732
  11.9 1.0 %copy-start.2 = (bf16[2,256,512]{2,1,0:T(8,128)(2,1)S(1)}, bf16[2,256,512]{2,1,0:T(8,128)(2,1)}, u32[]{:S(2)}) copy-start(bf16[2,256,512]{2,1,0:T(8,128)(2,1)} %own.1) | copy-start | bytes 1572868
  13.5 6.9 %copy-start.3 = (bf16[2,256,512]{2,1,0:T(8,128)(2,1)S(1)}, bf16[2,256,512]{2,1,0:T(8,128)(2,1)}, u32[]{:S(2)}) copy-start(bf16[2,256,512]{2,1,0:T(8,128)(2,1)} %own.1) | copy-start | bytes 1572868
  14.7 15.9 %all-to-all-start = ((bf16[16,80,128]{2,1,0:T(8,128)(2,1)}), bf16[16,80,128]{2,1,0:T(8,128)(2,1)S(1)}, u32[]{:S(2)}, u32[]{:S(2)}) async-start(bf16[16,80,128]{2,1,0:T(8,128)(2,1)} %bitcast.9), calls=%async_computation | async-start | bytes 655360 | tf_op jit(solution)/shard_map/all_to_all | solution.py:222
  20.4 26.2 %collective-permute-start.5 = (bf16[2,256,512]{2,1,0:T(8,128)(2,1)S(1)}, bf16[2,256,512]{2,1,0:T(8,128)(2,1)S(1)}, u32[]{:S(2)}, u32[]{:S(2)}) collective-permute-start(bf16[2,256,512]{2,1,0:T(8,128)(2,1)S(1)} %copy-done.3), channel_id=1, source_target_pairs={{0,2},{2,0},{1,3},{3,1},{4,6},{6,4},{5,7},{7,5},{8,10},{10,8},{9,1... | collective-permute-start | bytes 1572872 | tf_op jit(solution)/shard_map/ppermute | solution.py:203
  23.7 20.7 %collective-permute-start.2 = (bf16[4,128,256]{2,1,0:T(8,128)(2,1)S(1)}, bf16[4,128,256]{2,1,0:T(8,128)(2,1)S(1)}, u32[]{:S(2)}, u32[]{:S(2)}) collective-permute-start(bf16[4,128,256]{2,1,0:T(8,128)(2,1)S(1)} %get-tuple-element.8.mine), channel_id=1, source_target_pairs={{0,2},{2,0},{1,3},{3,1},{4,6},{6,4},{5,7},{7,5},{8,10},{10,8},{9,1... | collective-permute-start | bytes 786440 | tf_op jit(solution)/shard_map/ppermute | solution.py:203
  31.3 19.3 %all-to-all-start.1 = ((f32[16,16,128]{2,1,0:T(8,128)}), f32[16,16,128]{2,1,0:T(8,128)S(1)}, u32[]{:S(2)}, u32[]{:S(2)}) async-start(f32[16,16,128]{2,1,0:T(8,128)} %bitcast.11), calls=%async_computation.1 | async-start | bytes 262144 | tf_op jit(solution)/shard_map/all_to_all | solution.py:222
  44.5 6.2 %collective-permute-start.3 = (bf16[2,128,256]{2,1,0:T(8,128)(2,1)S(1)}, bf16[2,128,256]{2,1,0:T(8,128)(2,1)S(1)}, u32[]{:S(2)}, u32[]{:S(2)}) collective-permute-start(bf16[2,128,256]{2,1,0:T(8,128)(2,1)S(1)} %slice.12), channel_id=1, source_target_pairs={{0,4},{4,0},{8,12},{12,8},{16,20},{20,16},{24,28},{28,24},{1,5},{5... | collective-permute-start | bytes 393224 | tf_op jit(solution)/shard_map/ppermute | solution.py:203
  46.6 15.5 %collective-permute-start.6 = (bf16[2,256,512]{2,1,0:T(8,128)(2,1)S(1)}, bf16[2,256,512]{2,1,0:T(8,128)(2,1)}, u32[]{:S(2)}, u32[]{:S(2)}) collective-permute-start(bf16[2,256,512]{2,1,0:T(8,128)(2,1)S(1)} %collective-permute-done.5.by_chip), channel_id=1, source_target_pairs={{0,1},{1,0},{2,3},{3,2},{4,5},{5,4},{6,7},{7,6},{8,9},{9,8},{10,11... | collective-permute-start | bytes 1572872 | tf_op jit(solution)/shard_map/ppermute | solution.py:203
  50.6 7.0 %copy-start.5 = (s32[510]{0:T(512)S(1)}, s32[510]{0:T(512)}, u32[]{:S(2)}) copy-start(s32[510]{0:T(512)} %param.9) | copy-start | bytes 6124
  51.4 14.8 %all-to-all-start.2 = ((bf16[16,80,128]{2,1,0:T(8,128)(2,1)}), bf16[16,80,128]{2,1,0:T(8,128)(2,1)S(1)}, u32[]{:S(2)}, u32[]{:S(2)}) async-start(bf16[16,80,128]{2,1,0:T(8,128)(2,1)} %bitcast.13), calls=%async_computation.2 | async-start | bytes 655360 | tf_op jit(solution)/shard_map/all_to_all | solution.py:222
  57.9 8.4 %collective-permute-start.4 = (bf16[128,256]{1,0:T(8,128)(2,1)S(1)}, bf16[128,256]{1,0:T(8,128)(2,1)S(1)}, u32[]{:S(2)}, u32[]{:S(2)}) collective-permute-start(bf16[128,256]{1,0:T(8,128)(2,1)S(1)} %fusion), channel_id=1, source_target_pairs={{0,8},{4,12},{8,0},{12,4},{16,24},{20,28},{24,16},{28,20},{1,9},{5... | collective-permute-start | bytes 196616 | tf_op jit(solution)/shard_map/ppermute | solution.py:203
  62.1 1.2 %copy-start.4 = (bf16[2,256,1024]{2,1,0:T(8,128)(2,1)S(1)}, bf16[2,256,1024]{2,1,0:T(8,128)(2,1)}, u32[]{:S(2)}) copy-start(bf16[2,256,1024]{2,1,0:T(8,128)(2,1)} %blocks.1) | copy-start | bytes 3145732
  66.3 7.8 %copy-start = (bf16[8,2,256,128]{3,2,1,0:T(8,128)(2,1)S(1)}, bf16[8,2,256,128]{3,2,1,0:T(8,128)(2,1)}, u32[]{:S(2)}) copy-start(bf16[8,2,256,128]{3,2,1,0:T(8,128)(2,1)} %basis.5) | copy-start | bytes 3145732
  66.5 9.2 %collective-permute-start.7 = (bf16[1152,256]{1,0:T(8,128)(2,1)S(1)}, bf16[1152,256]{1,0:T(8,128)(2,1)S(1)}, u32[]{:S(2)}, u32[]{:S(2)}) collective-permute-start(bf16[1152,256]{1,0:T(8,128)(2,1)S(1)} %shard_map.61.coef), channel_id=1, source_target_pairs={{0,1},{1,0},{2,3},{3,2},{4,5},{5,4},{6,7},{7,6},{8,9},{9,8},{10,11... | collective-permute-start | bytes 1769480 | tf_op jit(solution)/shard_map/ppermute | solution.py:203
